TPU v7x, 32 devices: a whole 2x2x4 slice. The times are simulated.
32 devices in a mesh: segment: 2 (over x), dp: 4 (over z), rep: 4 (over y, core).
Axes of the slice: x: 2, y: 2, z: 4, core: 2. Of those that a mesh axis runs over, the one named last changes fastest.
Arguments:
- block_input: bfloat16 [16384, 512], P(('dp', 'rep')), may hold values from -6 to 6
- cotangent: bfloat16 [16384, 512], P(('dp', 'rep')), may hold values from -6 to 6
- window_group: int32 [16, 2], P(('dp', 'rep')), may hold values from 0 to 1, as said below
- w_qkv: bfloat16 [2, 512, 1536], P('segment'), may hold values from -0.25 to 0.25
- w_out: bfloat16 [2, 512, 512], P('segment'), may hold values from -1 to 1
- w_up: bfloat16 [2, 512, 2048], P('segment'), may hold values from -0.25 to 0.25
- w_down: bfloat16 [2, 2048, 512], P('segment'), may hold values from -0.125 to 0.125
- up_bias: bfloat16 [2, 2048], P('segment'), may hold values from -3 to 3
- norm_gains: bfloat16 [2, 2, 512], P('segment'), may hold values from 0.25 to 1.75
- biases: bfloat16 [2, 4, 512], P('segment'), may hold values from -2 to 2
Outputs:
- ends: float32 [2, 16384, 512], P('segment', ('dp', 'rep'))
- grad_qkv: float32 [2, 512, 1536], P('segment', 'dp')
- grad_out: float32 [2, 512, 512], P('segment', 'dp')
- grad_up: float32 [2, 512, 2048], P('segment', 'dp')
- grad_down: float32 [2, 2048, 512], P('segment', 'dp')
- grad_up_bias: float32 [2, 2048], P('segment', 'dp')
- grad_norm_gains: float32 [2, 2, 512], P('segment', None, 'dp')
- grad_biases: float32 [2, 4, 512], P('segment', None, 'dp')
Inputs may be any that keep to these rules, and one draw needn't show every extreme that they name: `window_group`: in every row, half of the 2 entries are 1 and half are 0.
All inputs are finite; a program needn't handle non-finite values.
Results may differ from a plain program's by a relative error of at most 0.019.
Values may be sent and summed in bfloat16 or wider, within the bound.
A program may use at most 128 MiB of HBM per device.

v0:
```python
import math

import jax
import jax.numpy as jnp
from jax import lax
from jax.sharding import PartitionSpec as P

HEADS = 8


small_eps = 1e-05


def from_behind(value, axis, steps):
    count = lax.axis_size(axis)
    first, last = (max(0, -steps), min(count, count - steps))
    return lax.ppermute(value, axis, [(source, source + steps) for source in range(first, last)])


def window_mask(row_count, window_flag):
    position = lax.broadcasted_iota(jnp.int32, (row_count, row_count), 0)
    earlier = lax.broadcasted_iota(jnp.int32, (row_count, row_count), 1)
    window_width = jnp.where(window_flag == 1, row_count, row_count // 2).astype(jnp.int32)
    return (earlier <= position) & (position // window_width == earlier // window_width)


def norm_forward(values, norm_gain, norm_shift):
    centred = values - jnp.mean(values, axis=-1, keepdims=True)
    variance = jnp.mean(centred * centred, axis=-1, keepdims=True)
    inverse = lax.rsqrt(variance + small_eps)
    normed = centred * inverse
    return (normed * norm_gain + norm_shift, normed, inverse)


def norm_backward(grad_result, normed, inverse, norm_gain):
    scaled = grad_result * norm_gain
    centred = scaled - jnp.mean(scaled, axis=-1, keepdims=True)
    return (centred - normed * jnp.mean(scaled * normed, axis=-1, keepdims=True)) * inverse


def times_transpose(left, right):
    return lax.dot_general(
        left, right, (((1,), (1,)), ((), ())), preferred_element_type=jnp.float32
    )


def outer_sum(left, right):
    return lax.dot_general(
        left, right, (((0,), (0,)), ((), ())), preferred_element_type=jnp.float32
    )


def gelu_value(pre_act):
    return pre_act * (lax.erf(pre_act / math.sqrt(2.0)) + 1.0) / 2.0


def gelu_slope(pre_act):
    return (lax.erf(pre_act / math.sqrt(2.0)) + 1.0) / 2.0 + pre_act * jnp.exp(
        -0.5 * pre_act * pre_act
    ) / math.sqrt(2.0 * math.pi)


def attend_scores(sections, allowed):
    score_scale = 1.0 / math.sqrt(sections.shape[-1])
    scores = jnp.einsum(
        "qhe,khe->hqk", sections[:, 0], sections[:, 1], preferred_element_type=jnp.float32
    )
    return (jnp.where(allowed, scores * score_scale, -1e30), score_scale)


def attend_forward(qkv_low, allowed):
    row_count = qkv_low.shape[0]
    sections = qkv_low.reshape(row_count, 3, HEADS, -1)
    masked, score_scale = attend_scores(sections, allowed)
    row_max = jnp.max(masked, axis=-1, keepdims=True)
    raised = jnp.exp(masked - row_max)
    row_total = jnp.sum(raised, axis=-1, keepdims=True)
    shares = (raised / row_total).astype(jnp.bfloat16)
    mixture = jnp.einsum("hqk,khe->qhe", shares, sections[:, 2], preferred_element_type=jnp.float32)
    return (mixture.reshape(row_count, -1).astype(jnp.bfloat16), row_max + jnp.log(row_total))


def attend_backward(qkv_low, allowed, log_total, grad_mixture):
    row_count = qkv_low.shape[0]
    sections = qkv_low.reshape(row_count, 3, HEADS, -1)
    grad_heads = grad_mixture.reshape(row_count, HEADS, -1)
    masked, score_scale = attend_scores(sections, allowed)
    shares = jnp.exp(masked - log_total)
    grad_shares = jnp.einsum(
        "qhe,khe->hqk", grad_heads, sections[:, 2], preferred_element_type=jnp.float32
    )
    row_inner = jnp.sum(shares * grad_shares, axis=-1, keepdims=True)
    grad_scores = (shares * (grad_shares - row_inner)).astype(jnp.bfloat16)
    grad_query = (
        jnp.einsum("hqk,khe->qhe", grad_scores, sections[:, 1], preferred_element_type=jnp.float32)
        * score_scale
    )
    grad_key = (
        jnp.einsum("hqk,qhe->khe", grad_scores, sections[:, 0], preferred_element_type=jnp.float32)
        * score_scale
    )
    grad_value = jnp.einsum(
        "hqk,qhe->khe", shares.astype(jnp.bfloat16), grad_heads, preferred_element_type=jnp.float32
    )
    stacked = jnp.stack([grad_query, grad_key, grad_value], axis=1)
    return stacked.reshape(row_count, -1).astype(jnp.bfloat16)


def layer_forward(inputs, allowed, weights):
    w_qkv, w_out, w_up, w_down, bias_up, norm_gain, bias_rows = weights
    qkv_low = jnp.dot(inputs, w_qkv, preferred_element_type=jnp.float32).astype(jnp.bfloat16)
    mixture_low, log_total = attend_forward(qkv_low, allowed)
    branch = jnp.dot(mixture_low, w_out, preferred_element_type=jnp.float32) + bias_rows[0]
    hidden, normed_one, inverse_one = norm_forward(
        inputs.astype(jnp.float32) + branch, norm_gain[0], bias_rows[1]
    )
    hidden_low = hidden.astype(jnp.bfloat16)
    pre_act = jnp.dot(hidden_low, w_up, preferred_element_type=jnp.float32) + bias_up
    active = gelu_value(pre_act).astype(jnp.bfloat16)
    branch_two = jnp.dot(active, w_down, preferred_element_type=jnp.float32) + bias_rows[2]
    output, normed_two, inverse_two = norm_forward(hidden + branch_two, norm_gain[1], bias_rows[3])
    kept = (
        inputs,
        qkv_low,
        log_total,
        mixture_low,
        normed_one,
        inverse_one,
        hidden_low,
        pre_act,
        active,
        normed_two,
        inverse_two,
    )
    return (output, kept)


def layer_backward(grad_output, allowed, kept, weights, valid):
    w_qkv, w_out, w_up, w_down, bias_up, norm_gain, bias_rows = weights
    (
        inputs,
        qkv_low,
        log_total,
        mixture_low,
        normed_one,
        inverse_one,
        hidden_low,
        pre_act,
        active,
        normed_two,
        inverse_two,
    ) = kept
    grad_sum_two = norm_backward(grad_output, normed_two, inverse_two, norm_gain[1])
    down_grad = grad_sum_two.astype(jnp.bfloat16)
    grad_pre = times_transpose(down_grad, w_down) * gelu_slope(pre_act)
    up_grad = grad_pre.astype(jnp.bfloat16)
    grad_hidden = grad_sum_two + times_transpose(up_grad, w_up)
    grad_sum_one = norm_backward(grad_hidden, normed_one, inverse_one, norm_gain[0])
    branch_grad = grad_sum_one.astype(jnp.bfloat16)
    grad_mixture = times_transpose(branch_grad, w_out).astype(jnp.bfloat16)
    grad_qkv = attend_backward(qkv_low, allowed, log_total, grad_mixture)
    grad_inputs = grad_sum_one + times_transpose(grad_qkv, w_qkv)
    mask_low = valid.astype(jnp.bfloat16)
    gain_terms = (
        jnp.stack(
            [jnp.sum(grad_hidden * normed_one, axis=0), jnp.sum(grad_output * normed_two, axis=0)]
        )[None]
        * valid
    )
    bias_terms = (
        jnp.stack(
            [
                jnp.sum(grad_sum_one, axis=0),
                jnp.sum(grad_hidden, axis=0),
                jnp.sum(grad_sum_two, axis=0),
                jnp.sum(grad_output, axis=0),
            ]
        )[None]
        * valid
    )
    up_terms = jnp.sum(grad_pre, axis=0)[None] * valid
    pieces = (
        inputs,
        grad_qkv * mask_low,
        mixture_low,
        branch_grad * mask_low,
        hidden_low,
        up_grad * mask_low,
        active,
        down_grad * mask_low,
        up_terms,
        gain_terms,
        bias_terms,
    )
    return (grad_inputs, pieces)


def weight_sums(pieces):
    (
        inputs,
        grad_qkv,
        mixture_low,
        branch_grad,
        hidden_low,
        up_grad,
        active,
        down_grad,
        up_terms,
        gain_terms,
        bias_terms,
    ) = pieces
    return (
        outer_sum(inputs, grad_qkv),
        outer_sum(mixture_low, branch_grad),
        outer_sum(hidden_low, up_grad),
        outer_sum(active, down_grad),
        jnp.sum(up_terms, axis=0),
        jnp.sum(gain_terms, axis=0),
        jnp.sum(bias_terms, axis=0),
    )


def on_device(
    block_input, cotangent, window_group, w_qkv, w_out, w_up, w_down, up_bias, norm_gains, biases
):
    weights = (
        w_qkv[0],
        w_out[0],
        w_up[0],
        w_down[0],
        up_bias[0].astype(jnp.float32),
        norm_gains[0].astype(jnp.float32),
        biases[0].astype(jnp.float32),
    )
    micro = window_group.shape[1]
    row_count = block_input.shape[0] // micro
    model_width = block_input.shape[1]
    segment_first = lax.axis_index("segment") == 0
    blank = jnp.zeros((row_count, model_width), jnp.bfloat16)
    incoming = blank
    kept_slots = []
    forward_rows = []
    for tick_index in range(micro + 1):
        if tick_index < micro:
            own_rows = block_input[tick_index * row_count : (tick_index + 1) * row_count]
        else:
            own_rows = blank
        inputs = jnp.where(segment_first, own_rows, incoming)
        window_flag = jnp.where(
            segment_first,
            window_group[0, min(tick_index, micro - 1)],
            window_group[0, max(tick_index - 1, 0)],
        )
        allowed = window_mask(row_count, window_flag)
        output, kept = layer_forward(inputs, allowed, weights)
        kept_slots.append((kept, allowed))
        forward_rows.append(output)
        if tick_index < micro:
            incoming = from_behind(output.astype(jnp.bfloat16), "segment", 1)
    returning = blank
    input_rows = [None] * (micro + 1)
    running = None
    for tick_index in range(micro + 1):
        slot_index = micro - tick_index
        if tick_index < micro:
            own_grad = cotangent[
                (micro - 1 - tick_index) * row_count : (micro - tick_index) * row_count
            ]
        else:
            own_grad = blank
        grad_output = jnp.where(segment_first, returning, own_grad).astype(jnp.float32)
        valid = jnp.where(segment_first, float(tick_index >= 1), float(tick_index < micro)).astype(
            jnp.float32
        )
        kept, allowed = kept_slots[slot_index]
        grad_inputs, pieces = layer_backward(grad_output, allowed, kept, weights, valid)
        input_rows[slot_index] = grad_inputs
        tick_sums = weight_sums(pieces)
        running = (
            tick_sums
            if running is None
            else tuple((left + right for left, right in zip(running, tick_sums)))
        )
        if tick_index < micro:
            returning = from_behind(grad_inputs.astype(jnp.bfloat16), "segment", -1)
    final_rows = jnp.concatenate(forward_rows[1:], axis=0)
    first_rows = jnp.concatenate(input_rows[:micro], axis=0)
    ends = jnp.where(segment_first, first_rows, final_rows)[None]
    sum_qkv, sum_out, sum_up, sum_down, sum_up_bias, sum_gains, sum_biases = tuple(
        (term[None] for term in running)
    )
    shares = (
        lax.psum_scatter(
            sum_qkv.astype(jnp.bfloat16), "dp", scatter_dimension=1, tiled=True
        ).astype(jnp.float32),
        lax.psum_scatter(
            sum_out.astype(jnp.bfloat16), "dp", scatter_dimension=1, tiled=True
        ).astype(jnp.float32),
        lax.psum_scatter(sum_up.astype(jnp.bfloat16), "dp", scatter_dimension=1, tiled=True).astype(
            jnp.float32
        ),
        lax.psum_scatter(
            sum_down.astype(jnp.bfloat16), "dp", scatter_dimension=1, tiled=True
        ).astype(jnp.float32),
        lax.psum_scatter(
            sum_up_bias.astype(jnp.bfloat16), "dp", scatter_dimension=1, tiled=True
        ).astype(jnp.float32),
        lax.psum_scatter(
            sum_gains.astype(jnp.bfloat16), "dp", scatter_dimension=2, tiled=True
        ).astype(jnp.float32),
        lax.psum_scatter(
            sum_biases.astype(jnp.bfloat16), "dp", scatter_dimension=2, tiled=True
        ).astype(jnp.float32),
    )
    part_qkv, part_out, part_up, part_down, part_up_bias, part_gains, part_biases = shares
    shares = (
        lax.psum(part_qkv.astype(jnp.bfloat16), "rep").astype(jnp.float32),
        lax.psum(part_out.astype(jnp.bfloat16), "rep").astype(jnp.float32),
        lax.psum(part_up.astype(jnp.bfloat16), "rep").astype(jnp.float32),
        lax.psum(part_down.astype(jnp.bfloat16), "rep").astype(jnp.float32),
        lax.psum(part_up_bias.astype(jnp.bfloat16), "rep").astype(jnp.float32),
        lax.psum(part_gains.astype(jnp.bfloat16), "rep").astype(jnp.float32),
        lax.psum(part_biases.astype(jnp.bfloat16), "rep").astype(jnp.float32),
    )
    return (ends, shares[0], shares[1], shares[2], shares[3], shares[4], shares[5], shares[6])


def solution(mesh):
    return jax.shard_map(
        on_device,
        mesh=mesh,
        in_specs=(
            P(("dp", "rep"), None),
            P(("dp", "rep"), None),
            P(("dp", "rep"), None),
            P("segment", None, None),
            P("segment", None, None),
            P("segment", None, None),
            P("segment", None, None),
            P("segment", None),
            P("segment", None, None),
            P("segment", None, None),
        ),
        out_specs=(
            P("segment", ("dp", "rep"), None),
            P("segment", "dp", None),
            P("segment", "dp", None),
            P("segment", "dp", None),
            P("segment", "dp", None),
            P("segment", "dp"),
            P("segment", None, "dp"),
            P("segment", None, "dp"),
        ),
        check_vma=False,
    )
```

profile of v0, /device:TPU:0, one launch (start us, length us, event | category | flops | bytes accessed | tf_op | source)
XLA Modules:
  0.0 469.4 jit_solution(5664639372987324017)
XLA Ops:
  9.4 2.1 fusion.248
  11.7 3.8 convolution_convert_fusion.2
  15.5 2.6 copy.87
  18.5 2.7 fusion.252
  22.4 2.0 copy-done.1
  24.4 2.7 fusion.140
  28.0 3.8 multiply_convert_fusion.5
  34.4 5.8 %collective-permute-start = (bf16[512,512]{0,1:T(8,128)(2,1)}, bf16[512,512]{0,1:T(8,128)(2,1)}, u32[]{:S(2)}, u32[]{:S(2)}) collective-permute-start(bf16[512,512]{0,1:T(8,128)(2,1)} %add_convert_fusion.2), channel_id=1, source_target_pairs={{0,16},{1,17},{2,18},{3,19},{4,20},{5,21},{6,22},{7,23},{8,24},{9,... | collective-permute-start | bytes 1572872 | tf_op jit(solution)/shard_map/ppermute | solution.py:17
  40.2 2.0 copy.145
  44.1 6.6 %collective-permute-done = bf16[512,512]{0,1:T(8,128)(2,1)} collective-permute-done((bf16[512,512]{0,1:T(8,128)(2,1)}, bf16[512,512]{0,1:T(8,128)(2,1)}, u32[]{:S(2)}, u32[]{:S(2)}) %collective-permute-start) | collective-permute-done | bytes 524320 | tf_op jit(solution)/shard_map/ppermute | solution.py:17
  52.6 3.6 convolution_convert_fusion.1
  56.2 2.6 copy.90
  58.8 2.7 fusion.255
  62.7 2.0 copy-done.2
  64.7 2.7 fusion.139
  68.2 3.8 multiply_convert_fusion.4
  75.8 5.4 %collective-permute-start.1 = (bf16[512,512]{0,1:T(8,128)(2,1)}, bf16[512,512]{0,1:T(8,128)(2,1)}, u32[]{:S(2)}, u32[]{:S(2)}) collective-permute-start(bf16[512,512]{0,1:T(8,128)(2,1)} %get-tuple-element.83), channel_id=1, source_target_pairs={{0,16},{1,17},{2,18},{3,19},{4,20},{5,21},{6,22},{7,23},{8,24},{9,... | collective-permute-start | bytes 1572872 | tf_op jit(solution)/shard_map/ppermute | solution.py:17
  83.0 2.0 copy.144
  85.6 5.3 %collective-permute-done.1 = bf16[512,512]{0,1:T(8,128)(2,1)} collective-permute-done((bf16[512,512]{0,1:T(8,128)(2,1)}, bf16[512,512]{0,1:T(8,128)(2,1)}, u32[]{:S(2)}, u32[]{:S(2)}) %collective-permute-start.1) | collective-permute-done | bytes 524320 | tf_op jit(solution)/shard_map/ppermute | solution.py:17
  90.8 3.6 convolution_convert_fusion
  94.4 2.6 copy.94
  97.0 2.7 fusion.258
  103.4 1.9 multiply_convert_fusion.3
  107.4 3.4 fusion.264
  110.8 1.9 multiply_reduce_fusion.5
  113.6 1.9 multiply_reduce_fusion.2
  115.5 2.6 multiply_convert_fusion.2
  126.7 2.1 copy.147
  128.8 3.0 fusion.186
  131.8 9.2 %collective-permute-done.2 = bf16[512,512]{0,1:T(8,128)(2,1)} collective-permute-done((bf16[512,512]{0,1:T(8,128)(2,1)}, bf16[512,512]{0,1:T(8,128)(2,1)}, u32[]{:S(2)}, u32[]{:S(2)}) %collective-permute-start.2) | collective-permute-done | bytes 524320 | tf_op jit(solution)/shard_map/ppermute | solution.py:17
  142.8 5.0 %fusion.263 = (f32[2048]{0:T(1024)S(1)}, bf16[512,2048]{1,0:T(8,128)(2,1)S(1)}) fusion(f32[512,2048]{1,0:T(8,128)} %get-tuple-element.110, f32[2048]{0:T(1024)S(1)} %bitcast.420, bf16[1,2048,512]{2,1,0:T(8,128)(2,1)S(1)} %copy-done.64, f32[512]{0:T(512)S(1)} %broadcast_multiply_fusion.8, f32[512]{0:T(512)S(1)} %add_rsqrt_fusion.2, ...), kind=kOutput, calls=%fused_computation.370 | convolution fusion | flops 1088681984 | bytes 9988096 | tf_op jit(solution)/shard_map/dot_general | solution.py:42
  147.9 1.9 multiply_reduce_fusion.4
  152.8 1.9 multiply_reduce_fusion.1
  154.7 2.6 multiply_convert_fusion.1
  161.1 2.0 fusion.261
  166.1 2.8 fusion.265
  168.9 7.5 %collective-permute-done.3 = bf16[512,512]{0,1:T(8,128)(2,1)S(1)} collective-permute-done((bf16[512,512]{0,1:T(8,128)(2,1)S(1)}, bf16[512,512]{0,1:T(8,128)(2,1)S(1)}, u32[]{:S(2)}, u32[]{:S(2)}) %collective-permute-start.3) | collective-permute-done | bytes 524320 | tf_op jit(solution)/shard_map/ppermute | solution.py:17
  177.3 3.2 fusion.262
  180.6 2.5 multiply_reduce_fusion.3
  185.8 1.9 multiply_reduce_fusion
  187.7 2.6 multiply_convert_fusion
  191.8 2.2 fusion.89
  194.0 2.2 fusion.86
  197.6 2.9 broadcast_multiply_fusion
  200.5 2.1 fusion.191
  202.6 2.2 fusion.37
  205.2 3.6 fusion.183
  210.5 3.1 fusion.36
  213.7 3.4 fusion.60
  219.1 2.7 fusion.35
  221.9 3.6 fusion.242
  228.8 26.8 %reduce-scatter.14.cloned.1.call-done = bf16[1,128,1536]{2,1,0:T(8,128)(2,1)} async-done(((bf16[1,512,1536]{2,1,0:T(8,128)(2,1)}), bf16[1,128,1536]{2,1,0:T(8,128)(2,1)}) %reduce-scatter.14.cloned.1.call-update) | async-done | bytes 393232 | tf_op jit(solution)/shard_map/reduce_scatter | solution.py:293
  255.6 45.2 %reduce-scatter.20.cloned.1.call-done = bf16[1,512,512]{2,1,0:T(8,128)(2,1)} async-done(((bf16[1,2048,512]{2,1,0:T(8,128)(2,1)}), bf16[1,512,512]{2,1,0:T(8,128)(2,1)}) %reduce-scatter.20.cloned.1.call-update) | async-done | bytes 524304 | tf_op jit(solution)/shard_map/reduce_scatter | solution.py:302
  300.7 46.0 %reduce-scatter.18.cloned.1.call-done = bf16[1,128,2048]{2,1,0:T(8,128)(2,1)} async-done(((bf16[1,512,2048]{2,1,0:T(8,128)(2,1)}), bf16[1,128,2048]{2,1,0:T(8,128)(2,1)}) %reduce-scatter.18.cloned.1.call-update) | async-done | bytes 524304 | tf_op jit(solution)/shard_map/reduce_scatter | solution.py:299
  346.8 3.0 fusion.99
  351.6 2.9 copy.113
  354.5 13.5 %reduce-scatter.24.cloned.1.call-done = bf16[128,2]{1,0:T(8,128)(2,1)} async-done(((bf16[512,2]{1,0:T(8,128)(2,1)}), bf16[128,2]{1,0:T(8,128)(2,1)}) %reduce-scatter.24.cloned.1.call-update) | async-done | bytes 528
  368.9 19.2 %reduce-scatter.26.cloned.1.call-done = bf16[128,4]{1,0:T(8,128)(2,1)} async-done(((bf16[512,4]{1,0:T(8,128)(2,1)}), bf16[128,4]{1,0:T(8,128)(2,1)}) %reduce-scatter.26.cloned.1.call-update) | async-done | bytes 1040
  389.0 21.9 %reduce-scatter.22.cloned.1.call-done = bf16[512,1]{1,0:T(8,128)(2,1)} async-done(((bf16[2048,1]{1,0:T(8,128)(2,1)}), bf16[512,1]{1,0:T(8,128)(2,1)}) %reduce-scatter.22.cloned.1.call-update) | async-done | bytes 1040
  411.9 5.7 %all-reduce = (bf16[1,512]{1,0:T(2,128)(2,1)S(1)}, bf16[1,2,128]{2,1,0:T(2,128)(2,1)S(1)}, bf16[1,4,128]{2,1,0:T(4,128)(2,1)S(1)}) all-reduce(bf16[1,512]{1,0:T(2,128)(2,1)S(1)} %copy.137, bf16[1,2,128]{2,1,0:T(2,128)(2,1)S(1)} %copy.139, bf16[1,4,128]{2,1,0:T(4,128)(2,1)S(1)} %copy.141), channel_id=1, replica_groups=mesh['segment'=2,'dp'=4,'rep'=4] {'rep'}, use_global_device_ids=true, to_apply=%region_45.46 | all-reduce | flops 1280 | bytes 5120 | tf_op jit(solution)/shard_map/psum | solution.py:321
  419.3 35.9 %all-reduce.4.cloned.1.call-done = (bf16[1,128,1536]{2,1,0:T(8,128)(2,1)}, bf16[1,128,512]{2,1,0:T(8,128)(2,1)}, bf16[1,128,2048]{2,1,0:T(8,128)(2,1)}, bf16[1,512,512]{2,1,0:T(8,128)(2,1)}) async-done(((bf16[1,128,1536]{2,1,0:T(8,128)(2,1)}, bf16[1,128,512]{2,1,0:T(8,128)(2,1)}, bf16[1,128,2048]{2,1,0:T(8,128)(2,1)}, bf16[1,512,512]{2,1,0:T(8,128)(2,1)}), (bf16[1,128,1536]{2,1,0:T(8,128)(2,1)}, ...) | async-done | bytes 1572880 | tf_op jit(solution)/shard_map/psum | solution.py:317
  455.2 2.2 convert_element_type.371
  457.3 2.1 convert_element_type.374
  459.5 2.0 convert_element_type.365
  (269 shorter events, 63.9 us)
Async XLA Ops:
  7.2 20.8 %copy-start = (bf16[1,512,2048]{2,1,0:T(8,128)(2,1)S(1)}, bf16[1,512,2048]{2,1,0:T(8,128)(2,1)}, u32[]{:S(2)}) copy-start(bf16[1,512,2048]{2,1,0:T(8,128)(2,1)} %param.15) | copy-start | bytes 6291460
  7.2 221.6 %reduce-scatter.16.cloned.1.call-start = ((), (), s32[]{:S(2)}) async-start(), calls=%async_computation.8 | async-start | bytes 655360 | tf_op jit(solution)/shard_map/reduce_scatter | solution.py:296
  11.7 15.5 %copy-start.50 = (bf16[512,512]{0,1:T(8,128)(2,1)}, bf16[512,512]{0,1:T(8,128)(2,1)S(1)}, u32[]{:S(2)}) copy-start(bf16[512,512]{0,1:T(8,128)(2,1)S(1)} %copy.146) | copy-start | bytes 1572868
  21.2 3.2 copy-start.1
  24.4 2.7 copy-start.57
  24.4 2.7 copy-start.21
  24.4 3.5 copy-start.59
  24.4 3.5 copy-start.58
  27.7 4.1 copy-start.14
  28.0 3.8 copy-start.61
  34.4 16.3 %collective-permute-start = (bf16[512,512]{0,1:T(8,128)(2,1)}, bf16[512,512]{0,1:T(8,128)(2,1)}, u32[]{:S(2)}, u32[]{:S(2)}) collective-permute-start(bf16[512,512]{0,1:T(8,128)(2,1)} %add_convert_fusion.2), channel_id=1, source_target_pairs={{0,16},{1,17},{2,18},{3,19},{4,20},{5,21},{6,22},{7,23},{8,24},{9,... | collective-permute-start | bytes 1572872 | tf_op jit(solution)/shard_map/ppermute | solution.py:17
  61.5 3.2 copy-start.2
  64.7 2.7 copy-start.22
  64.7 2.7 copy-start.29
  68.0 4.1 copy-start.7
  68.2 3.8 copy-start.62
  73.5 7.7 %copy-start.52 = (bf16[1024,512]{1,0:T(8,128)(2,1)S(1)}, bf16[1024,512]{1,0:T(8,128)(2,1)}, u32[]{:S(2)}) copy-start(bf16[1024,512]{1,0:T(8,128)(2,1)} %param.11) | copy-start | bytes 3145732
  75.8 15.0 %collective-permute-start.1 = (bf16[512,512]{0,1:T(8,128)(2,1)}, bf16[512,512]{0,1:T(8,128)(2,1)}, u32[]{:S(2)}, u32[]{:S(2)}) collective-permute-start(bf16[512,512]{0,1:T(8,128)(2,1)} %get-tuple-element.83), channel_id=1, source_target_pairs={{0,16},{1,17},{2,18},{3,19},{4,20},{5,21},{6,22},{7,23},{8,24},{9,... | collective-permute-start | bytes 1572872 | tf_op jit(solution)/shard_map/ppermute | solution.py:17
  102.7 2.7 copy-start.55
  103.2 9.5 %copy-start.38 = (f32[512,512]{0,1:T(8,128)}, f32[512,512]{0,1:T(8,128)S(1)}, u32[]{:S(2)}) copy-start(f32[512,512]{0,1:T(8,128)S(1)} %get-tuple-element.116) | copy-start | bytes 3145732
  106.9 3.9 copy-start.6
  113.2 9.9 %copy-start.19 = (f32[512,512]{0,1:T(8,128)}, f32[512,512]{0,1:T(8,128)S(1)}, u32[]{:S(2)}) copy-start(f32[512,512]{0,1:T(8,128)S(1)} %get-tuple-element.76) | copy-start | bytes 3145732
  125.4 15.6 %collective-permute-start.2 = (bf16[512,512]{0,1:T(8,128)(2,1)}, bf16[512,512]{0,1:T(8,128)(2,1)}, u32[]{:S(2)}, u32[]{:S(2)}) collective-permute-start(bf16[512,512]{0,1:T(8,128)(2,1)} %fusion.135), channel_id=1, source_target_pairs={{16,0},{17,1},{18,2},{19,3},{20,4},{21,5},{22,6},{23,7},{24,8},{25... | collective-permute-start | bytes 1572872 | tf_op jit(solution)/shard_map/ppermute | solution.py:17
  128.8 14.0 %copy-start.4 = (f32[512,512]{0,1:T(8,128)S(1)}, f32[512,512]{0,1:T(8,128)}, u32[]{:S(2)}) copy-start(f32[512,512]{0,1:T(8,128)} %copy-done.3) | copy-start | bytes 3145732
  128.8 14.0 %copy-start.64 = (bf16[1,2048,512]{2,1,0:T(8,128)(2,1)S(1)}, bf16[1,2048,512]{2,1,0:T(8,128)(2,1)}, u32[]{:S(2)}) copy-start(bf16[1,2048,512]{2,1,0:T(8,128)(2,1)} %param.16) | copy-start | bytes 6291460
  142.7 5.1 %copy-start.31 = (bf16[512,512]{0,1:T(8,128)(2,1)}, bf16[512,512]{0,1:T(8,128)(2,1)S(1)}, u32[]{:S(2)}) copy-start(bf16[512,512]{0,1:T(8,128)(2,1)S(1)} %get-tuple-element.81) | copy-start | bytes 1572868
  142.8 5.0 %copy-start.8 = (f32[512,512]{0,1:T(8,128)S(1)}, f32[512,512]{0,1:T(8,128)}, u32[]{:S(2)}) copy-start(f32[512,512]{0,1:T(8,128)} %copy-done.7) | copy-start | bytes 3145732
  147.8 3.1 slice-start.2
  147.8 4.3 slice-start.3
  149.7 3.1 copy-start.12
  161.1 3.4 copy-start.36
  161.1 3.4 copy-start.45
  161.1 5.0 %copy-start.30 = (bf16[512,512]{0,1:T(8,128)(2,1)S(1)}, bf16[512,512]{0,1:T(8,128)(2,1)}, u32[]{:S(2)}) copy-start(bf16[512,512]{0,1:T(8,128)(2,1)} %copy-done.28) | copy-start | bytes 1572868
  163.1 13.2 %copy-start.32 = (bf16[512,512]{0,1:T(8,128)(2,1)S(1)}, bf16[512,512]{0,1:T(8,128)(2,1)}, u32[]{:S(2)}) copy-start(bf16[512,512]{0,1:T(8,128)(2,1)} %copy-done.31) | copy-start | bytes 1572868
  163.1 13.2 %collective-permute-start.3 = (bf16[512,512]{0,1:T(8,128)(2,1)S(1)}, bf16[512,512]{0,1:T(8,128)(2,1)S(1)}, u32[]{:S(2)}, u32[]{:S(2)}) collective-permute-start(bf16[512,512]{0,1:T(8,128)(2,1)S(1)} %get-tuple-element.127), channel_id=1, source_target_pairs={{16,0},{17,1},{18,2},{19,3},{20,4},{21,5},{22,6},{23,7},{24,8},{25... | collective-permute-start | bytes 1572872 | tf_op jit(solution)/shard_map/ppermute | solution.py:17
  166.1 11.2 %copy-start.65 = (bf16[1,2048,512]{2,1,0:T(8,128)(2,1)S(1)}, bf16[1,2048,512]{2,1,0:T(8,128)(2,1)}, u32[]{:S(2)}) copy-start(bf16[1,2048,512]{2,1,0:T(8,128)(2,1)} %param.16) | copy-start | bytes 6291460
  166.1 11.2 %copy-start.69 = (f32[512,2048]{1,0:T(8,128)S(1)}, f32[512,2048]{1,0:T(8,128)}, u32[]{:S(2)}) copy-start(f32[512,2048]{1,0:T(8,128)} %get-tuple-element.102) | copy-start | bytes 12582916
  176.3 4.2 copy-start.26
  177.3 3.3 copy-start.15
  180.5 2.5 copy-start.48
  180.5 3.4 slice-start
  180.6 4.6 slice-start.1
  183.0 2.7 copy-start.11
  183.5 12.8 %copy-start.17 = (f32[512,512]{0,1:T(8,128)}, f32[512,512]{0,1:T(8,128)S(1)}, u32[]{:S(2)}) copy-start(f32[512,512]{0,1:T(8,128)S(1)} %get-tuple-element.72) | copy-start | bytes 3145732
  197.6 58.0 %reduce-scatter.14.cloned.1.call-start = ((), (), s32[]{:S(2)}) async-start(), calls=%async_computation.7 | async-start | bytes 1966080 | tf_op jit(solution)/shard_map/reduce_scatter | solution.py:293
  197.6 5.0 %copy-start.10 = (f32[512,1536]{1,0:T(8,128)S(1)}, f32[512,1536]{1,0:T(8,128)}, u32[]{:S(2)}) copy-start(f32[512,1536]{1,0:T(8,128)} %fusion.265) | copy-start | bytes 9437188
  197.6 5.0 %copy-start.25 = (bf16[512,3,8,64]{0,3,2,1:T(8,128)(2,1)S(1)}, bf16[512,3,8,64]{0,3,2,1:T(8,128)(2,1)}, u32[]{:S(2)}) copy-start(bf16[512,3,8,64]{0,3,2,1:T(8,128)(2,1)} %get-tuple-element.77) | copy-start | bytes 4718596
  204.8 95.9 %reduce-scatter.20.cloned.1.call-start = ((), (), s32[]{:S(2)}) async-start(), calls=%async_computation.10 | async-start | bytes 2621440 | tf_op jit(solution)/shard_map/reduce_scatter | solution.py:302
  205.1 3.6 copy-start.5
  205.1 3.6 copy-start.33
  205.2 3.6 copy-start.40
  213.6 133.1 %reduce-scatter.18.cloned.1.call-start = ((), (), s32[]{:S(2)}) async-start(), calls=%async_computation.9 | async-start | bytes 2621440 | tf_op jit(solution)/shard_map/reduce_scatter | solution.py:299
  213.7 3.4 copy-start.9
  213.7 3.4 copy-start.47
  221.8 4.7 copy-start.60
  221.8 146.2 %reduce-scatter.24.cloned.1.call-start = ((), (), s32[]{:S(2)}) async-start(), calls=%async_computation.12 | async-start | bytes 163840
  225.5 121.3 %copy-start.18 = (f32[512,512]{0,1:T(8,128)S(1)}, f32[512,512]{0,1:T(8,128)}, u32[]{:S(2)}) copy-start(f32[512,512]{0,1:T(8,128)} %copy-done.17) | copy-start | bytes 3145732
  226.5 161.7 %reduce-scatter.26.cloned.1.call-start = ((), (), s32[]{:S(2)}) async-start(), calls=%async_computation.13 | async-start | bytes 163840
  227.5 183.4 %reduce-scatter.22.cloned.1.call-start = ((), (), s32[]{:S(2)}) async-start(), calls=%async_computation.11 | async-start | bytes 655360
  228.7 226.5 %all-reduce.4.cloned.1.call-start = ((), (), s32[]{:S(2)}) async-start(), calls=%async_computation.14 | async-start | bytes 3145728 | tf_op jit(solution)/shard_map/psum | solution.py:317
  346.8 3.1 copy-start.34
  346.8 3.1 copy-start.35
  346.8 3.1 copy-start.51
  455.2 6.3 %copy-start.56 = (bf16[1,128,512]{2,1,0:T(8,128)(2,1)S(1)}, bf16[1,128,512]{2,1,0:T(8,128)(2,1)}, u32[]{:S(2)}) copy-start(bf16[1,128,512]{2,1,0:T(8,128)(2,1)} %get-tuple-element.68) | copy-start | bytes 393220
  (22 other events, 35.2 us)
Sparse Core Ops, SparseCore 0:
  197.7 21.9 reduce-scatter.15
  222.0 33.5 reduce-scatter.13
  257.9 42.8 reduce-scatter.19
  303.6 43.1 reduce-scatter.17
  349.4 18.5 reduce-scatter.23
  370.8 17.3 reduce-scatter.25
  391.0 19.8 reduce-scatter.21
  413.5 41.6 all-reduce.3
where the time goes:
time: 478 us; the launch traced here: 469 us
  waiting for transfers between devices  237 us (50%)
  matrix products  115 us (24%)
  other arithmetic  40.3 us (8%)
  local copies, waits for them, and re-layouts  38.7 us (8%)
  between operations  18.5 us (4%)
  starting transfers between devices  14.4 us (3%)
  blocking collectives  5.65 us (1%)
    unnamed x11, waiting for transfers between devices  54.7 us
    reduce_scatter x1, waiting for transfers between devices, on_device(): lax.psum_scatter(sum_up.astype(jnp.bfloat16), 'dp', scatter_dimension=1,...  46 us
    reduce_scatter x1, waiting for transfers between devices, on_device(): lax.psum_scatter(sum_down.astype(jnp.bfloat16), 'dp', scatter_dimension=1...  45.2 us
    psum x1, waiting for transfers between devices, on_device(): lax.psum(part_qkv.astype(jnp.bfloat16), 'rep').astype(jnp.float32)  35.9 us
    ppermute x4, waiting for transfers between devices, from_behind(): lax.ppermute(value, axis, [(source, source + steps) for source in range(f...  28.6 us
    dot_general x12, matrix products, outer_sum(): lax.dot_general(left, right, (((0,), (0,)), ((), ())), preferred_element_...  28.5 us
    reduce_scatter x1, waiting for transfers between devices, on_device(): lax.psum_scatter(sum_qkv.astype(jnp.bfloat16), 'dp', scatter_dimension=1,...  26.8 us
    unnamed x163, local copies, waits for them, and re-layouts  26.3 us
  transfers between devices with their start and end apart: 12, of which 11 were waited for; matrix products, arithmetic and copies ran while one was open for 12% of the time, Pallas kernels for 0%

commit v1 on v0

v1 whole, which is shorter than its diff:
```python
import functools
import math

import jax
import jax.numpy as jnp
from jax import lax
from jax.experimental import pallas as pl
from jax.experimental.pallas import tpu as pltpu
from jax.sharding import PartitionSpec as P

MESH = pl.DeviceIdType.MESH
F32 = jnp.float32
BF16 = jnp.bfloat16
HEADS = 8
LANES = 128
PIECES = 4
EPS = 1e-05
GAIN_ONE, GAIN_TWO, BIAS_OUT, BIAS_ONE, BIAS_DOWN, BIAS_TWO, BIAS_UP = range(7)
STATS = 10


def dot_plain(left, right):
    return lax.dot_general(left, right, (((1,), (0,)), ((), ())), preferred_element_type=F32)


def dot_turned(left, right):
    return lax.dot_general(left, right, (((1,), (1,)), ((), ())), preferred_element_type=F32)


def row_mean(values):
    return jnp.sum(values, axis=0, keepdims=True) * (1.0 / values.shape[0])


def fold(values):
    total = values[:, :LANES]
    for start in range(LANES, values.shape[1], LANES):
        total = total + values[:, start : start + LANES]
    return total


def pair_blocks(values):
    half = values.shape[0] // 2
    blank = jnp.zeros((half, values.shape[1]), values.dtype)
    first = jnp.concatenate([values[:half], blank], axis=0)
    second = jnp.concatenate([blank, values[half:]], axis=0)
    return jnp.concatenate([first, second], axis=1)


def layer_kernel(
    dp_count,
    flag_ref,
    x_hbm,
    ct_hbm,
    w_qkv_hbm,
    w_out_hbm,
    w_up_hbm,
    w_down_hbm,
    up_bias_ref,
    gains_ref,
    biases_ref,
    ends_hbm,
    fin_hbm,
    small_hbm,
    w_qkv,
    w_out,
    w_up,
    w_down,
    turned,
    down_turned,
    rows_in,
    x_t,
    qkv,
    keys_rm,
    values_rm,
    share,
    share_off,
    mixture,
    norm_one,
    norm_two,
    inverses,
    hidden_low,
    slope,
    active,
    down_grad,
    branch_grad,
    grad_mix,
    outgoing,
    incoming_grad,
    columns,
    sums,
    key_sums,
    wide_a,
    wide_b,
    ends_v,
    core_in,
    side_in,
    dp_in,
    fin,
    small,
    small_dp,
    small_rep,
    small_out,
    load_sem,
    seg_send,
    seg_recv,
    ends_sem,
    core_send,
    core_recv,
    side_send,
    side_recv,
    dp_send,
    dp_recv,
    join_send,
    join_recv,
    last_send,
    last_recv,
    sdp_send,
    sdp_recv,
    srep_send,
    srep_recv,
    fin_sem,
):
    width = w_out.shape[0]
    piece = x_t.shape[1] // PIECES
    pairs = qkv.shape[1]
    share_rows = width // dp_count
    segment = lax.axis_index("segment")
    dp = lax.axis_index("dp")
    rep = lax.axis_index("rep")
    core = lax.rem(rep, 2)
    side = lax.div(rep, 2)
    other_core = side * 2 + (1 - core)
    other_side = (1 - side) * 2 + core

    loads = [
        (w_qkv_hbm.at[0], w_qkv),
        (w_out_hbm.at[0], w_out),
        (w_up_hbm.at[0], w_up),
    ]
    for block in range(4):
        loads.append((w_down_hbm.at[0, pl.ds(block * width, width), :], w_down.at[block]))
    load_copies = [
        pltpu.make_async_copy(source, target, load_sem.at[index + 1])
        for index, (source, target) in enumerate(loads)
    ]
    first_rows = pltpu.make_async_copy(x_hbm, rows_in, load_sem.at[0])
    last_rows = pltpu.make_async_copy(ct_hbm, rows_in, load_sem.at[0])

    @pl.when(segment == 0)
    def _():
        first_rows.start()

    @pl.when(segment == 1)
    def _():
        last_rows.start()

    for copy in load_copies:
        copy.start()

    barrier = pltpu.get_barrier_semaphore()
    pl.semaphore_signal(
        barrier, inc=1, device_id={"segment": 1 - segment}, device_id_type=MESH
    )
    for step in range(1, 4):
        pl.semaphore_signal(
            barrier, inc=1, device_id={"rep": lax.rem(rep + step, 4)}, device_id_type=MESH
        )
    for step in range(1, dp_count):
        pl.semaphore_signal(
            barrier, inc=1, device_id={"dp": lax.rem(dp + step, dp_count)}, device_id_type=MESH
        )

    params = [gains_ref[0].astype(F32), biases_ref[0].astype(F32)]
    for block in range(4):
        params.append(up_bias_ref[:, block * width : (block + 1) * width].astype(F32))
    params.append(jnp.zeros((16 - STATS, width), F32))
    upright = jnp.concatenate(params, axis=0).T
    for index in range(STATS):
        columns[index] = jnp.broadcast_to(upright[:, index : index + 1], (width, LANES)).astype(BF16)
    for index in range(STATS):
        sums[index] = jnp.zeros((width, LANES), F32)
    key_sums[0] = jnp.zeros(key_sums.shape[1:], F32)

    def column(index):
        part = columns[index].astype(F32)
        return jnp.concatenate([part] * (piece // LANES), axis=1)

    def gather_sum(index, values):
        sums[index] = sums[index] + fold(values)

    for copy in load_copies:
        copy.wait()
    first_rows.wait()

    for block in range(3):
        turned[block] = w_qkv[:, block * width : (block + 1) * width].T
    turned[3] = w_out[...].T
    for block in range(4):
        turned[4 + block] = w_up[:, block * width : (block + 1) * width].T
    for block in range(4):
        down_turned[:, block * width : (block + 1) * width] = w_down[block].T

    pl.semaphore_wait(barrier, 4 + dp_count - 1)

    flag = flag_ref[0, 0].astype(F32)

    def lanes_of(index):
        return pl.ds(pl.multiple_of(index * piece, piece), piece)

    def forward_copy(index):
        return pltpu.make_async_remote_copy(
            src_ref=outgoing.at[index],
            dst_ref=x_t.at[:, lanes_of(index)],
            send_sem=seg_send.at[index],
            recv_sem=seg_recv.at[index],
            device_id={"segment": 1 - segment},
            device_id_type=MESH,
        )

    def backward_copy(index):
        return pltpu.make_async_remote_copy(
            src_ref=outgoing.at[index],
            dst_ref=incoming_grad.at[index],
            send_sem=seg_send.at[index],
            recv_sem=seg_recv.at[index],
            device_id={"segment": 1 - segment},
            device_id_type=MESH,
        )

    def ends_copy(index):
        return pltpu.make_async_copy(ends_v.at[index], ends_hbm.at[index], ends_sem.at[index])

    def own_rows(index):
        half = lax.rem(index, 2)
        whole = jnp.where(index < 2, 1.0, 0.0).astype(F32)
        weight = whole * flag + (1.0 - whole) * (1.0 - flag)
        picked = rows_in[half].astype(F32) * weight + rows_in[2 + half].astype(F32) * (1.0 - weight)
        return picked.T

    def attend(index, has_off):
        lanes = lanes_of(index)

        def one_pair(pair, carry):
            queries = pair_blocks(qkv[0, pair, :, lanes])
            scores = dot_plain(keys_rm[index, pair], queries)
            key_at = lax.broadcasted_iota(jnp.int32, (piece, piece), 0)
            query_at = lax.broadcasted_iota(jnp.int32, (piece, piece), 1)
            allowed = key_at <= query_at
            if has_off:
                scores_off = dot_plain(keys_rm[0, pair], queries)
            half = queries.shape[0] // 2
            for head in range(2):
                span = slice(head * piece, (head + 1) * piece)
                rows = slice(head * half, (head + 1) * half)
                own = jnp.where(allowed, scores[:, span], -1e30)
                top = jnp.max(own, axis=0, keepdims=True)
                if has_off:
                    off = scores_off[:, span]
                    top = jnp.maximum(top, jnp.max(off, axis=0, keepdims=True))
                raised = jnp.exp(own - top)
                total = jnp.sum(raised, axis=0, keepdims=True)
                if has_off:
                    raised_off = jnp.exp(off - top)
                    total = total + jnp.sum(raised_off, axis=0, keepdims=True)
                scale = 1.0 / total
                low = (raised * scale).astype(BF16)
                share[index, pair, head] = low
                mixed = dot_plain(qkv[2, pair, rows, lanes], low)
                if has_off:
                    low_off = (raised_off * scale).astype(BF16)
                    share_off[pair, head] = low_off
                    mixed = mixed + dot_plain(qkv[2, pair, rows, :piece], low_off)
                mixture[pair, rows, lanes] = mixed.astype(BF16)
            return carry

        lax.fori_loop(0, pairs, one_pair, 0)

    def norm(values, index, which, normed_ref):
        lanes = lanes_of(index)
        centred = values - row_mean(values)
        inverse = lax.rsqrt(row_mean(centred * centred) + EPS)
        normed = centred * inverse
        normed_ref[:, lanes] = normed
        inverses[index, which] = inverse
        return normed

    def forward(index):
        lanes = lanes_of(index)

        @pl.when(segment == 0)
        def _():
            x_t[:, lanes] = own_rows(index).astype(BF16)

        @pl.when(segment == 1)
        def _():
            forward_copy(index).wait_recv()

        inputs = x_t[:, lanes]
        queries = dot_plain(turned[0], inputs) * (1.0 / math.sqrt(width // HEADS))
        qkv[0, :, :, lanes] = queries.astype(BF16).reshape(pairs, LANES, piece)
        keys = dot_plain(turned[1], inputs)
        qkv[1, :, :, lanes] = keys.astype(BF16).reshape(pairs, LANES, piece)
        values = dot_plain(turned[2], inputs)
        qkv[2, :, :, lanes] = values.astype(BF16).reshape(pairs, LANES, piece)
        for pair in range(pairs):
            rows = slice(pair * LANES, (pair + 1) * LANES)
            keys_rm[index, pair] = keys[rows].T.astype(BF16)
            values_rm[index, pair] = values[rows].T.astype(BF16)

        @pl.when(index == 1)
        def _():
            attend(index, True)

        @pl.when(index != 1)
        def _():
            attend(index, False)

        branch = dot_plain(turned[3], mixture[:, :, lanes].reshape(width, piece))
        sum_one = x_t[:, lanes].astype(F32) + (branch + column(BIAS_OUT))
        normed = norm(sum_one, index, 0, norm_one)
        hidden = normed * column(GAIN_ONE) + column(BIAS_ONE)
        wide_a[...] = hidden
        hidden_low[:, lanes] = hidden.astype(BF16)

        def up_block(block, carry):
            pre = dot_plain(turned[4 + block], hidden_low[:, lanes]) + column(BIAS_UP + block)
            level = (lax.erf(pre * (1.0 / math.sqrt(2.0))) + 1.0) * 0.5
            active[block, :, lanes] = (pre * level).astype(BF16)
            bell = jnp.exp(-0.5 * pre * pre) * (1.0 / math.sqrt(2.0 * math.pi))
            slope[block, :, lanes] = (level + pre * bell).astype(BF16)
            return carry

        lax.fori_loop(0, 4, up_block, 0)
        branch_two = dot_plain(down_turned[...], active[:, :, lanes].reshape(4 * width, piece))
        sum_two = wide_a[...] + (branch_two + column(BIAS_DOWN))
        normed_two = norm(sum_two, index, 1, norm_two)
        output = normed_two * column(GAIN_TWO) + column(BIAS_TWO)

        @pl.when(segment == 0)
        def _():
            outgoing[index] = output.astype(BF16)
            forward_copy(index).start()

        @pl.when(segment == 1)
        def _():
            ends_v[index] = output.T
            ends_copy(index).start()

    def norm_back(grad, index, which, normed_ref, gain):
        lanes = lanes_of(index)
        normed = normed_ref[:, lanes]
        scaled = grad * column(gain)
        inner = row_mean(scaled * normed)
        return (scaled - row_mean(scaled) - normed * inner) * inverses[index, which]

    def attend_back(index, has_off):
        lanes = lanes_of(index)
        slot = jnp.where(index == 0, 1, 0)
        score_scale = 1.0 / math.sqrt(width // HEADS)

        def one_pair(pair, carry):
            grads = grad_mix[pair]
            blocks = pair_blocks(grads)
            back = dot_plain(values_rm[index, pair], blocks)
            if has_off:
                back_off = dot_plain(values_rm[0, pair], blocks)
            half = grads.shape[0] // 2
            for head in range(2):
                span = slice(head * piece, (head + 1) * piece)
                rows = slice(head * half, (head + 1) * half)
                low = share[index, pair, head]
                wide = low.astype(F32)
                product = wide * back[:, span]
                inner = jnp.sum(product, axis=0, keepdims=True)
                if has_off:
                    low_off = share_off[pair, head]
                    wide_off = low_off.astype(F32)
                    product_off = wide_off * back_off[:, span]
                    inner = inner + jnp.sum(product_off, axis=0, keepdims=True)
                grad_scores = (product - wide * inner).astype(BF16)
                queries = qkv[0, pair, rows, lanes]
                grad_query = dot_plain(qkv[1, pair, rows, lanes], grad_scores)
                grad_key = dot_turned(queries, grad_scores) + key_sums[slot, 0, pair, rows]
                grad_value = dot_turned(grads[rows], low) + key_sums[slot, 1, pair, rows]
                if has_off:
                    grad_off = (product_off - wide_off * inner).astype(BF16)
                    grad_query = grad_query + dot_plain(qkv[1, pair, rows, :piece], grad_off)
                    key_sums[1, 0, pair, rows] = dot_turned(queries, grad_off)
                    key_sums[1, 1, pair, rows] = dot_turned(grads[rows], low_off)
                qkv[0, pair, rows, lanes] = (grad_query * score_scale).astype(BF16)
                qkv[1, pair, rows, lanes] = grad_key.astype(BF16)
                qkv[2, pair, rows, lanes] = grad_value.astype(BF16)
            return carry

        lax.fori_loop(0, pairs, one_pair, 0)

    def backward(index):
        lanes = lanes_of(index)

        @pl.when(segment == 1)
        def _():
            incoming_grad[index] = own_rows(index).astype(BF16)

        @pl.when(segment == 0)
        def _():
            backward_copy(index).wait_recv()

        grad = incoming_grad[index].astype(F32)
        gather_sum(GAIN_TWO, grad * norm_two[:, lanes])
        gather_sum(BIAS_TWO, grad)
        grad_two = norm_back(grad, index, 1, norm_two, GAIN_TWO)
        gather_sum(BIAS_DOWN, grad_two)
        wide_a[...] = grad_two
        down_grad[:, lanes] = grad_two.astype(BF16)

        def down_block(block, carry):
            back = dot_plain(w_down[block], down_grad[:, lanes])
            grad_pre = back * slope[block, :, lanes].astype(F32)
            gather_sum(BIAS_UP + block, grad_pre)
            slope[block, :, lanes] = grad_pre.astype(BF16)
            return carry

        lax.fori_loop(0, 4, down_block, 0)
        grad_hidden = wide_a[...] + dot_plain(
            w_up[...], slope[:, :, lanes].reshape(4 * width, piece)
        )
        gather_sum(GAIN_ONE, grad_hidden * norm_one[:, lanes])
        gather_sum(BIAS_ONE, grad_hidden)
        grad_one = norm_back(grad_hidden, index, 0, norm_one, GAIN_ONE)
        gather_sum(BIAS_OUT, grad_one)
        wide_b[...] = grad_one
        branch_grad[:, lanes] = grad_one.astype(BF16)
        grad_mix[...] = (
            dot_plain(w_out[...], branch_grad[:, lanes]).astype(BF16).reshape(pairs, LANES, piece)
        )

        @pl.when(index == 1)
        def _():
            attend_back(index, True)

        @pl.when(index != 1)
        def _():
            attend_back(index, False)

        grad_input = wide_b[...] + dot_plain(
            w_qkv[...], qkv[:, :, :, lanes].reshape(3 * width, piece)
        )

        @pl.when(segment == 1)
        def _():
            outgoing[index] = grad_input.astype(BF16)
            backward_copy(index).start()

        @pl.when(segment == 0)
        def _():
            ends_v[index] = grad_input.T
            ends_copy(index).start()

    def one_step(step, carry):
        first_index = jnp.where(step < 4, step, jnp.where(step < 6, 5 - step, step - 4))
        last_index = jnp.where(step < 2, step, jnp.where(step < 4, 3 - step, lax.div(step, 2)))
        first_is = jnp.where(step < 4, 1, 0)
        last_is = jnp.where(step < 2, 1, jnp.where(step < 4, 0, 1 - lax.rem(step, 2)))
        index = jnp.where(segment == 0, first_index, last_index)
        is_forward = jnp.where(segment == 0, first_is, last_is)

        @pl.when(is_forward == 1)
        def _():
            forward(index)

        @pl.when(is_forward == 0)
        def _():
            backward(index)

        return carry

    lax.fori_loop(0, 2 * PIECES, one_step, 0)

    def held(group):
        return (w_down, 0) if group == 0 else (turned, 4 if group == 1 else 0)

    def core_copy(group):
        buffer, base = held(group)
        return pltpu.make_async_remote_copy(
            src_ref=buffer.at[pl.ds(base + 2 * (1 - core), 2)],
            dst_ref=core_in.at[group],
            send_sem=core_send.at[group],
            recv_sem=core_recv.at[group],
            device_id={"rep": other_core},
            device_id_type=MESH,
        )

    def side_copy(group):
        buffer, base = held(group)
        return pltpu.make_async_remote_copy(
            src_ref=buffer.at[base + 2 * core + (1 - side)],
            dst_ref=side_in.at[group],
            send_sem=side_send.at[group],
            recv_sem=side_recv.at[group],
            device_id={"rep": other_side},
            device_id_type=MESH,
        )

    def dp_copy(group, step):
        buffer, base = held(group)
        target = lax.rem(dp + step, dp_count)
        rows = pl.ds(pl.multiple_of(target * share_rows, share_rows), share_rows)
        return pltpu.make_async_remote_copy(
            src_ref=buffer.at[base + 2 * core + side, rows],
            dst_ref=dp_in.at[group, step - 1],
            send_sem=dp_send.at[group, step - 1],
            recv_sem=dp_recv.at[group, step - 1],
            device_id={"dp": target},
            device_id_type=MESH,
        )

    def join_copy(group):
        return pltpu.make_async_remote_copy(
            src_ref=fin.at[group, 2 * core + side],
            dst_ref=fin.at[group, 2 * core + side],
            send_sem=join_send.at[group],
            recv_sem=join_recv.at[group],
            device_id={"rep": other_side},
            device_id_type=MESH,
        )

    def last_copy(group):
        return pltpu.make_async_remote_copy(
            src_ref=fin.at[group, pl.ds(2 * core, 2)],
            dst_ref=fin.at[group, pl.ds(2 * core, 2)],
            send_sem=last_send.at[group],
            recv_sem=last_recv.at[group],
            device_id={"rep": other_core},
            device_id_type=MESH,
        )

    def down_sums():
        part = 4 * share_rows
        count = width // part

        def one(block, carry):
            result = dot_turned(active[block], down_grad[...]).astype(BF16)
            for each in range(count):
                for position in range(4):
                    start = each * part + position * share_rows
                    target = pl.multiple_of((block * count + each) * share_rows, share_rows)
                    w_down[position, pl.ds(target, share_rows), :] = result[
                        start : start + share_rows
                    ]
            return carry

        lax.fori_loop(0, 4, one, 0)

    def up_sums():
        def one(block, carry):
            turned[4 + block] = dot_turned(hidden_low[...], slope[block]).astype(BF16)
            return carry

        lax.fori_loop(0, 4, one, 0)

    def qkv_sums():
        def one(block, carry):
            turned[block] = dot_turned(
                x_t[...], qkv[block].reshape(width, PIECES * piece)
            ).astype(BF16)
            return carry

        lax.fori_loop(0, 3, one, 0)
        turned[3] = dot_turned(
            mixture[...].reshape(width, PIECES * piece), branch_grad[...]
        ).astype(BF16)

    def after_core(group):
        buffer, base = held(group)
        copy = core_copy(group)
        copy.wait_send()
        copy.wait_recv()
        first = base + 2 * core + (1 - side)
        buffer[first] = (
            buffer[first].astype(F32) + core_in[group, 1 - side].astype(F32)
        ).astype(BF16)
        side_copy(group).start()

    def after_side(group):
        buffer, base = held(group)
        copy = side_copy(group)
        copy.wait_send()
        copy.wait_recv()
        second = base + 2 * core + side
        buffer[second] = (
            buffer[second].astype(F32)
            + core_in[group, side].astype(F32)
            + side_in[group].astype(F32)
        ).astype(BF16)
        for step in range(1, dp_count):
            dp_copy(group, step).start()

    def after_dp(group):
        buffer, base = held(group)
        rows = pl.ds(pl.multiple_of(dp * share_rows, share_rows), share_rows)
        total = buffer[base + 2 * core + side, rows, :].astype(F32)
        for step in range(1, dp_count):
            copy = dp_copy(group, step)
            copy.wait_send()
            copy.wait_recv()
            total = total + dp_in[group, step - 1].astype(F32)
        fin[group, 2 * core + side] = total.astype(BF16)
        join_copy(group).start()

    def after_join(group):
        copy = join_copy(group)
        copy.wait_send()
        copy.wait_recv()
        last_copy(group).start()

    def fin_copy(group):
        return pltpu.make_async_copy(fin.at[group], fin_hbm.at[group], fin_sem.at[group])

    def after_last(group):
        copy = last_copy(group)
        copy.wait_send()
        copy.wait_recv()
        fin_copy(group).start()

    def small_dp_copy(step):
        target = lax.rem(dp + step, dp_count)
        return pltpu.make_async_remote_copy(
            src_ref=small.at[target],
            dst_ref=small_dp.at[step - 1],
            send_sem=sdp_send.at[step - 1],
            recv_sem=sdp_recv.at[step - 1],
            device_id={"dp": target},
            device_id_type=MESH,
        )

    def small_rep_copy(step):
        return pltpu.make_async_remote_copy(
            src_ref=small_rep.at[rep],
            dst_ref=small_rep.at[rep],
            send_sem=srep_send.at[step - 1],
            recv_sem=srep_recv.at[step - 1],
            device_id={"rep": lax.rem(rep + step, 4)},
            device_id_type=MESH,
        )

    down_sums()
    core_copy(0).start()
    up_sums()
    core_copy(1).start()
    after_core(0)
    qkv_sums()
    core_copy(2).start()
    after_core(1)

    rows_of = [jnp.sum(sums[index].T, axis=0, keepdims=True) for index in range(STATS)]
    small[...] = jnp.zeros(small.shape, F32)
    for share_index in range(dp_count):
        for index in range(BIAS_UP):
            start = share_index * share_rows
            small[share_index, index : index + 1, :share_rows] = rows_of[index][
                :, start : start + share_rows
            ]
        for part in range(4):
            start = (share_index * 4 + part) * share_rows
            block, start = start // width, start % width
            small[share_index, BIAS_UP + part : BIAS_UP + part + 1, :share_rows] = rows_of[
                BIAS_UP + block
            ][:, start : start + share_rows]
    for step in range(1, dp_count):
        small_dp_copy(step).start()

    after_core(2)
    after_side(0)
    small_total = small[dp]
    for step in range(1, dp_count):
        copy = small_dp_copy(step)
        copy.wait_send()
        copy.wait_recv()
        small_total = small_total + small_dp[step - 1]
    small_rep[rep] = small_total
    for step in range(1, 4):
        small_rep_copy(step).start()
    after_side(1)
    after_dp(0)
    after_side(2)
    after_join(0)
    after_dp(1)
    after_last(0)
    after_join(1)
    for step in range(1, 4):
        copy = small_rep_copy(step)
        copy.wait_send()
        copy.wait_recv()
    small_out[...] = (small_rep[0] + small_rep[1]) + (small_rep[2] + small_rep[3])
    small_copy = pltpu.make_async_copy(small_out, small_hbm, load_sem.at[0])
    small_copy.start()
    after_last(1)
    after_dp(2)
    after_join(2)
    after_last(2)

    for index in range(PIECES):

        @pl.when(segment == 0)
        def _():
            forward_copy(index).wait_send()

        @pl.when(segment == 1)
        def _():
            backward_copy(index).wait_send()

        ends_copy(index).wait()
    for group in range(3):
        fin_copy(group).wait()
    small_copy.wait()


def finish_kernel(
    flag_ref,
    ends_in,
    fin,
    small,
    ends,
    grad_qkv,
    grad_out,
    grad_up,
    grad_down,
    grad_up_bias,
    grad_gains,
    grad_biases,
    sem,
):
    half = ends_in.shape[0] // 2
    share_rows, width = fin.shape[2:]
    start = pl.multiple_of(half * (1 - flag_ref[0, 0]), half)
    copies = [
        pltpu.make_async_copy(
            ends_in.at[pl.ds(0, half)], ends.at[0, pl.ds(start, half)], sem.at[0]
        ),
        pltpu.make_async_copy(
            ends_in.at[pl.ds(half, half)], ends.at[0, pl.ds(half - start, half)], sem.at[1]
        ),
    ]
    for copy in copies:
        copy.start()
    for position in range(4):
        columns = slice(position * width, (position + 1) * width)
        rows = slice(position * share_rows, (position + 1) * share_rows)
        grad_down[0, rows, :] = fin[0, position].astype(F32)
        grad_up[0, :, columns] = fin[1, position].astype(F32)
        if position < 3:
            grad_qkv[0, :, columns] = fin[2, position].astype(F32)
        else:
            grad_out[0] = fin[2, position].astype(F32)
        grad_up_bias[:, rows] = small[BIAS_UP + position : BIAS_UP + position + 1, :share_rows]
    grad_gains[0] = small[:2, :share_rows]
    grad_biases[0] = small[2:BIAS_UP, :share_rows]
    for copy in copies:
        copy.wait()


def on_device(
    dp_count,
    block_input,
    cotangent,
    window_group,
    w_qkv,
    w_out,
    w_up,
    w_down,
    up_bias,
    norm_gains,
    biases,
):
    rows, width = block_input.shape
    piece = rows // PIECES
    pairs = width // LANES
    share_rows = width // dp_count
    small_width = max(share_rows, LANES)
    any_spec = pl.BlockSpec(memory_space=pl.ANY)
    vmem_spec = pl.BlockSpec(memory_space=pltpu.VMEM)
    smem_spec = pl.BlockSpec(memory_space=pltpu.SMEM)
    dma = pltpu.SemaphoreType.DMA
    vmem = pltpu.VMEM
    ends_in, fin, small = pl.pallas_call(
        functools.partial(layer_kernel, dp_count),
        out_shape=(
            jax.ShapeDtypeStruct((PIECES, piece, width), F32),
            jax.ShapeDtypeStruct((3, 4, share_rows, width), BF16),
            jax.ShapeDtypeStruct((16, small_width), F32),
        ),
        in_specs=[smem_spec] + [any_spec] * 6 + [vmem_spec] * 3,
        out_specs=(any_spec,) * 3,
        scratch_shapes=[
            vmem((width, 3 * width), BF16),
            vmem((width, width), BF16),
            vmem((width, 4 * width), BF16),
            vmem((4, width, width), BF16),
            vmem((8, width, width), BF16),
            vmem((width, 4 * width), BF16),
            vmem((PIECES, piece, width), BF16),
            vmem((width, rows), BF16),
            vmem((3, pairs, LANES, rows), BF16),
            vmem((PIECES, pairs, piece, LANES), BF16),
            vmem((PIECES, pairs, piece, LANES), BF16),
            vmem((PIECES, pairs, 2, piece, piece), BF16),
            vmem((pairs, 2, piece, piece), BF16),
            vmem((pairs, LANES, rows), BF16),
            vmem((width, rows), F32),
            vmem((width, rows), F32),
            vmem((PIECES, 2, 1, piece), F32),
            vmem((width, rows), BF16),
            vmem((4, width, rows), BF16),
            vmem((4, width, rows), BF16),
            vmem((width, rows), BF16),
            vmem((width, rows), BF16),
            vmem((pairs, LANES, piece), BF16),
            vmem((PIECES, width, piece), BF16),
            vmem((PIECES, width, piece), BF16),
            vmem((STATS, width, LANES), BF16),
            vmem((STATS, width, LANES), F32),
            vmem((2, 2, pairs, LANES, piece), F32),
            vmem((width, piece), F32),
            vmem((width, piece), F32),
            vmem((PIECES, piece, width), F32),
            vmem((3, 2, width, width), BF16),
            vmem((3, width, width), BF16),
            vmem((3, dp_count - 1, share_rows, width), BF16),
            vmem((3, 4, share_rows, width), BF16),
            vmem((dp_count, 16, small_width), F32),
            vmem((dp_count - 1, 16, small_width), F32),
            vmem((4, 16, small_width), F32),
            vmem((16, small_width), F32),
            dma((8,)),
            dma((PIECES,)),
            dma((PIECES,)),
            dma((PIECES,)),
            dma((3,)),
            dma((3,)),
            dma((3,)),
            dma((3,)),
            dma((3, dp_count - 1)),
            dma((3, dp_count - 1)),
            dma((3,)),
            dma((3,)),
            dma((3,)),
            dma((3,)),
            dma((dp_count - 1,)),
            dma((dp_count - 1,)),
            dma((3,)),
            dma((3,)),
            dma((3,)),
        ],
        compiler_params=pltpu.CompilerParams(
            collective_id=0, has_side_effects=True, vmem_limit_bytes=63 * 1024 * 1024
        ),
    )(
        window_group,
        block_input.reshape(PIECES, piece, width),
        cotangent.reshape(PIECES, piece, width),
        w_qkv,
        w_out,
        w_up,
        w_down,
        up_bias,
        norm_gains,
        biases,
    )
    return pl.pallas_call(
        finish_kernel,
        out_shape=(
            jax.ShapeDtypeStruct((1, rows, width), F32),
            jax.ShapeDtypeStruct((1, share_rows, 3 * width), F32),
            jax.ShapeDtypeStruct((1, share_rows, width), F32),
            jax.ShapeDtypeStruct((1, share_rows, 4 * width), F32),
            jax.ShapeDtypeStruct((1, 4 * share_rows, width), F32),
            jax.ShapeDtypeStruct((1, 4 * share_rows), F32),
            jax.ShapeDtypeStruct((1, 2, share_rows), F32),
            jax.ShapeDtypeStruct((1, 4, share_rows), F32),
        ),
        in_specs=[smem_spec, any_spec, vmem_spec, vmem_spec],
        out_specs=(any_spec,) + (vmem_spec,) * 7,
        scratch_shapes=[dma((2,))],
        compiler_params=pltpu.CompilerParams(vmem_limit_bytes=32 * 1024 * 1024),
    )(window_group, ends_in.reshape(rows, width), fin, small)


def solution(mesh):
    return jax.shard_map(
        functools.partial(on_device, mesh.shape["dp"]),
        mesh=mesh,
        in_specs=(
            P(("dp", "rep"), None),
            P(("dp", "rep"), None),
            P(("dp", "rep"), None),
            P("segment", None, None),
            P("segment", None, None),
            P("segment", None, None),
            P("segment", None, None),
            P("segment", None),
            P("segment", None, None),
            P("segment", None, None),
        ),
        out_specs=(
            P("segment", ("dp", "rep"), None),
            P("segment", "dp", None),
            P("segment", "dp", None),
            P("segment", "dp", None),
            P("segment", "dp", None),
            P("segment", "dp"),
            P("segment", None, "dp"),
            P("segment", None, "dp"),
        ),
        check_vma=False,
    )
```

time: 478 us -> 155 us (0.32); the launches traced: 469 us -> 155 us
  waiting for transfers between devices: 237 us -> 0 us
  Pallas kernels: 0 us -> 150 us
  matrix products: 115 us -> 0 us
  other arithmetic: 40.3 us -> 0 us
  local copies, waits for them, and re-layouts: 38.7 us -> 3.69 us
  between operations: 18.5 us -> 0.67 us
  starting transfers between devices: 14.4 us -> 0 us
  blocking collectives: 5.65 us -> 0 us
    pallas_call x0 -> x2, Pallas kernels: none -> 150 us  [the longest x1 147 us: on_device(): pl.pallas_call(functools.partial(layer_kernel, dp_count), out_shape=(jax....]
    reduce_scatter x4 -> x0, waiting for transfers between devices: 118 us -> none  [the longest x1 46 us: on_device(): lax.psum_scatter(sum_up.astype(jnp.bfloat16), 'dp', scatter_dimension=1,...]
    dot_general x54 -> x0, matrix products: 115 us -> none  [the longest x12 28.5 us: outer_sum(): lax.dot_general(left, right, (((0,), (0,)), ((), ())), preferred_element_...]
    unnamed x11 -> x0, waiting for transfers between devices: 54.7 us -> none
    psum x1 -> x0, waiting for transfers between devices: 35.9 us -> none  [on_device(): lax.psum(part_qkv.astype(jnp.bfloat16), 'rep').astype(jnp.float32)]
    ppermute x4 -> x0, waiting for transfers between devices: 28.6 us -> none  [from_behind(): lax.ppermute(value, axis, [(source, source + steps) for source in range(f...]
    unnamed x163 -> x8, local copies, waits for them, and re-layouts: 26.3 us -> 3.69 us
    convert_element_type x15 -> x0, other arithmetic: 17.7 us -> none  [the longest x3 7.7 us: attend_backward(): grad_scores = (shares * (grad_shares - row_inner)).astype(jnp.bfloat16)]
  transfers between devices with their start and end apart: 12 -> 0, of which waited for: 11 -> 0; matrix products, arithmetic and copies ran while one was open for 12% -> 0% of each run, Pallas kernels for 0% -> 0%
where the time goes in v1:
time: 155 us
  Pallas kernels  150 us (97%)
  local copies, waits for them, and re-layouts  3.69 us (2%)
    pallas_call x1, Pallas kernels, on_device(): pl.pallas_call(functools.partial(layer_kernel, dp_count), out_shape=(jax....  147 us
    unnamed x8, local copies, waits for them, and re-layouts  3.69 us
    pallas_call x1, Pallas kernels, on_device(): pl.pallas_call(finish_kernel, out_shape=(jax.ShapeDtypeStruct((1, rows, w...  3.54 us

profile of v1, /device:TPU:0, one launch (start us, length us, event | category | flops | bytes accessed | tf_op | source)
XLA Modules:
  0.0 154.6 jit_solution(7472916759806271993)
XLA Ops:
  0.6 0.0 copy-start.3
  0.6 146.7 %shard_map.161 = (f32[4,256,512]{2,1,0:T(8,128)}, bf16[3,4,128,512]{3,2,1,0:T(8,128)(2,1)}, f32[16,128]{1,0:T(8,128)}) custom-call(s32[1,2]{1,0:T(1,128)} %flag_ref.3, bf16[4,256,512]{2,1,0:T(8,128)(2,1)} %bitcast.4, bf16[4,256,512]{2,1,0:T(8,128)(2,1)} %bitcast.5, bf16[1,512,1536]{2,1,0:T(8,128)(2,1)} %w_qkv_hbm.1, bf16[1,512,512]{2,1,0:T(8,128)(2,1)} %w_out_hbm.1, ...), custom_call_target="tpu_custom_call" | custom-call | tf_op jit(solution)/shard_map/pallas_call | solution.py:785
  147.4 0.0 copy-done.3
  147.4 0.0 copy-start
  147.4 1.6 %copy-done = f32[4,256,512]{2,1,0:T(8,128)S(1)} copy-done((f32[4,256,512]{2,1,0:T(8,128)S(1)}, f32[4,256,512]{2,1,0:T(8,128)}, u32[]{:S(2)}) %copy-start) | copy-done | bytes 2097176
  149.0 0.0 copy-start.1
  149.0 1.4 copy-done.1
  150.4 0.0 copy-start.2
  150.4 0.7 copy-done.2
  151.1 3.5 %shard_map.162 = (f32[1,1024,512]{2,1,0:T(8,128)}, f32[1,128,1536]{2,1,0:T(8,128)}, f32[1,128,512]{2,1,0:T(8,128)}, f32[1,128,2048]{2,1,0:T(8,128)}, f32[1,512,5...) custom-call(s32[1,2]{1,0:T(1,128)S(1)} %copy-done.3, f32[1024,512]{1,0:T(8,128)S(1)} %bitcast.3, ...), custom_call_target="tpu_custom_call" | custom-call | tf_op jit(solution)/shard_map/pallas_call | solution.py:869
Async XLA Ops:
  0.6 146.7 %copy-start.3 = (s32[1,2]{1,0:T(1,128)S(1)}, s32[1,2]{1,0:T(1,128)}, u32[]{:S(2)}) copy-start(s32[1,2]{1,0:T(1,128)} %flag_ref.3) | copy-start | bytes 28
  147.4 1.6 %copy-start = (f32[4,256,512]{2,1,0:T(8,128)S(1)}, f32[4,256,512]{2,1,0:T(8,128)}, u32[]{:S(2)}) copy-start(f32[4,256,512]{2,1,0:T(8,128)} %get-tuple-element.11) | copy-start | bytes 6291460
  149.0 1.4 copy-start.1
  150.4 0.7 copy-start.2

commit v2 on v1

--- a/solution.py
+++ b/solution.py
@@ -17,6 +17,7 @@
 EPS = 1e-05
 GAIN_ONE, GAIN_TWO, BIAS_OUT, BIAS_ONE, BIAS_DOWN, BIAS_TWO, BIAS_UP = range(7)
 STATS = 10
+CHUNK = 64
 
 
 def dot_plain(left, right):
@@ -25,10 +26,6 @@
 
 def dot_turned(left, right):
     return lax.dot_general(left, right, (((1,), (1,)), ((), ())), preferred_element_type=F32)
-
-
-def row_mean(values):
-    return jnp.sum(values, axis=0, keepdims=True) * (1.0 / values.shape[0])
 
 
 def fold(values):
@@ -89,6 +86,7 @@
     columns,
     sums,
     key_sums,
+    score_grad,
     wide_a,
     wide_b,
     ends_v,
@@ -181,12 +179,7 @@
         sums[index] = jnp.zeros((width, LANES), F32)
     key_sums[0] = jnp.zeros(key_sums.shape[1:], F32)
 
-    def column(index):
-        part = columns[index].astype(F32)
-        return jnp.concatenate([part] * (piece // LANES), axis=1)
-
-    def gather_sum(index, values):
-        sums[index] = sums[index] + fold(values)
+    chunks = [slice(start, start + CHUNK) for start in range(0, width, CHUNK)]
 
     for copy in load_copies:
         copy.wait()
@@ -228,7 +221,14 @@
         )
 
     def ends_copy(index):
-        return pltpu.make_async_copy(ends_v.at[index], ends_hbm.at[index], ends_sem.at[index])
+        return pltpu.make_async_copy(
+            ends_v.at[lax.rem(index, 2)], ends_hbm.at[index], ends_sem.at[index]
+        )
+
+    def free_ends(index):
+        @pl.when(index >= 2)
+        def _():
+            ends_copy(index - 2).wait()
 
     def own_rows(index):
         half = lax.rem(index, 2)
@@ -239,50 +239,69 @@
 
     def attend(index, has_off):
         lanes = lanes_of(index)
-
-        def one_pair(pair, carry):
+        half = LANES // 2
+        key_at = lax.broadcasted_iota(jnp.int32, (LANES, LANES), 0)
+        query_at = lax.broadcasted_iota(jnp.int32, (LANES, LANES), 1)
+        allowed = key_at <= query_at
+        blank = jnp.zeros((LANES, LANES), BF16)
+        for pair in range(pairs):
             queries = pair_blocks(qkv[0, pair, :, lanes])
             scores = dot_plain(keys_rm[index, pair], queries)
-            key_at = lax.broadcasted_iota(jnp.int32, (piece, piece), 0)
-            query_at = lax.broadcasted_iota(jnp.int32, (piece, piece), 1)
-            allowed = key_at <= query_at
             if has_off:
                 scores_off = dot_plain(keys_rm[0, pair], queries)
-            half = queries.shape[0] // 2
             for head in range(2):
-                span = slice(head * piece, (head + 1) * piece)
                 rows = slice(head * half, (head + 1) * half)
-                own = jnp.where(allowed, scores[:, span], -1e30)
-                top = jnp.max(own, axis=0, keepdims=True)
+                for part in range(2):
+                    start = head * piece + part * LANES
+                    span = slice(start, start + LANES)
+                    place = slice(part * LANES, (part + 1) * LANES)
+                    tiles = [jnp.where(allowed, scores[place, span], -1e30)]
+                    if part:
+                        tiles.append(scores[:LANES, span])
+                    if has_off:
+                        tiles.append(scores_off[:LANES, span])
+                        tiles.append(scores_off[LANES:, span])
+                    top = functools.reduce(jnp.maximum, tiles)
+                    top = jnp.max(top, axis=0, keepdims=True)
+                    raised = [jnp.exp(tile - top) for tile in tiles]
+                    total = functools.reduce(jnp.add, raised)
+                    scale = 1.0 / jnp.sum(total, axis=0, keepdims=True)
+                    low = [(tile * scale).astype(BF16) for tile in raised]
+                    share[index, pair, head, place, place] = low[0]
+                    if part:
+                        share[index, pair, head, :LANES, place] = low[1]
+                    else:
+                        share[index, pair, head, LANES:, place] = blank
+                    if has_off:
+                        share_off[pair, head, :LANES, place] = low[-2]
+                        share_off[pair, head, LANES:, place] = low[-1]
+                mixed = dot_plain(qkv[2, pair, rows, lanes], share[index, pair, head])
                 if has_off:
-                    off = scores_off[:, span]
-                    top = jnp.maximum(top, jnp.max(off, axis=0, keepdims=True))
-                raised = jnp.exp(own - top)
-                total = jnp.sum(raised, axis=0, keepdims=True)
-                if has_off:
-                    raised_off = jnp.exp(off - top)
-                    total = total + jnp.sum(raised_off, axis=0, keepdims=True)
-                scale = 1.0 / total
-                low = (raised * scale).astype(BF16)
-                share[index, pair, head] = low
-                mixed = dot_plain(qkv[2, pair, rows, lanes], low)
-                if has_off:
-                    low_off = (raised_off * scale).astype(BF16)
-                    share_off[pair, head] = low_off
-                    mixed = mixed + dot_plain(qkv[2, pair, rows, :piece], low_off)
+                    mixed = mixed + dot_plain(qkv[2, pair, rows, :piece], share_off[pair, head])
                 mixture[pair, rows, lanes] = mixed.astype(BF16)
-            return carry
-
-        lax.fori_loop(0, pairs, one_pair, 0)
-
-    def norm(values, index, which, normed_ref):
-        lanes = lanes_of(index)
-        centred = values - row_mean(values)
-        inverse = lax.rsqrt(row_mean(centred * centred) + EPS)
-        normed = centred * inverse
-        normed_ref[:, lanes] = normed
+
+    def part_sum(values):
+        return jnp.sum(values.reshape(values.shape[0] // 8, 8, values.shape[1]), axis=0)
+
+    def full_mean(parts):
+        return jnp.sum(parts, axis=0, keepdims=True) * (1.0 / width)
+
+    def column(index, rows):
+        part = columns[index, rows, :].astype(F32)
+        return jnp.concatenate([part] * (piece // LANES), axis=1)
+
+    def gather_sum(index, rows, values):
+        sums[index, rows, :] = sums[index, rows, :] + fold(values)
+
+    def norm_chunks(index, which, total):
+        mean = full_mean(total)
+        spread = jnp.zeros((8, piece), F32)
+        for rows in chunks:
+            centred = wide_a[rows, :] - mean
+            spread = spread + part_sum(centred * centred)
+        inverse = lax.rsqrt(full_mean(spread) + EPS)
         inverses[index, which] = inverse
-        return normed
+        return mean, inverse
 
     def forward(index):
         lanes = lanes_of(index)
@@ -296,16 +315,17 @@
             forward_copy(index).wait_recv()
 
         inputs = x_t[:, lanes]
-        queries = dot_plain(turned[0], inputs) * (1.0 / math.sqrt(width // HEADS))
-        qkv[0, :, :, lanes] = queries.astype(BF16).reshape(pairs, LANES, piece)
-        keys = dot_plain(turned[1], inputs)
-        qkv[1, :, :, lanes] = keys.astype(BF16).reshape(pairs, LANES, piece)
-        values = dot_plain(turned[2], inputs)
-        qkv[2, :, :, lanes] = values.astype(BF16).reshape(pairs, LANES, piece)
-        for pair in range(pairs):
-            rows = slice(pair * LANES, (pair + 1) * LANES)
-            keys_rm[index, pair] = keys[rows].T.astype(BF16)
-            values_rm[index, pair] = values[rows].T.astype(BF16)
+        score_scale = 1.0 / math.sqrt(width // HEADS)
+        for block in range(3):
+            result = dot_plain(turned[block], inputs)
+            for pair in range(pairs):
+                low = result[pair * LANES : (pair + 1) * LANES]
+                low = (low * score_scale if block == 0 else low).astype(BF16)
+                qkv[block, pair, :, lanes] = low
+                if block == 1:
+                    keys_rm[index, pair] = low.T
+                if block == 2:
+                    values_rm[index, pair] = low.T
 
         @pl.when(index == 1)
         def _():
@@ -316,83 +336,114 @@
             attend(index, False)
 
         branch = dot_plain(turned[3], mixture[:, :, lanes].reshape(width, piece))
-        sum_one = x_t[:, lanes].astype(F32) + (branch + column(BIAS_OUT))
-        normed = norm(sum_one, index, 0, norm_one)
-        hidden = normed * column(GAIN_ONE) + column(BIAS_ONE)
-        wide_a[...] = hidden
-        hidden_low[:, lanes] = hidden.astype(BF16)
-
-        def up_block(block, carry):
-            pre = dot_plain(turned[4 + block], hidden_low[:, lanes]) + column(BIAS_UP + block)
-            level = (lax.erf(pre * (1.0 / math.sqrt(2.0))) + 1.0) * 0.5
-            active[block, :, lanes] = (pre * level).astype(BF16)
-            bell = jnp.exp(-0.5 * pre * pre) * (1.0 / math.sqrt(2.0 * math.pi))
-            slope[block, :, lanes] = (level + pre * bell).astype(BF16)
-            return carry
-
-        lax.fori_loop(0, 4, up_block, 0)
+        total = jnp.zeros((8, piece), F32)
+        for rows in chunks:
+            sum_one = x_t[rows, lanes].astype(F32) + (branch[rows] + column(BIAS_OUT, rows))
+            wide_a[rows, :] = sum_one
+            total = total + part_sum(sum_one)
+        mean, inverse = norm_chunks(index, 0, total)
+        for rows in chunks:
+            normed = (wide_a[rows, :] - mean) * inverse
+            norm_one[rows, lanes] = normed
+            hidden = normed * column(GAIN_ONE, rows) + column(BIAS_ONE, rows)
+            hidden_low[rows, lanes] = hidden.astype(BF16)
+
+        def activate(block, pre_block):
+            for rows in chunks:
+                pre = pre_block[rows] + column(BIAS_UP + block, rows)
+                level = (lax.erf(pre * (1.0 / math.sqrt(2.0))) + 1.0) * 0.5
+                active[block, rows, lanes] = (pre * level).astype(BF16)
+                bell = jnp.exp(-0.5 * pre * pre) * (1.0 / math.sqrt(2.0 * math.pi))
+                slope[block, rows, lanes] = (level + pre * bell).astype(BF16)
+
+        for block in range(4):
+            activate(block, dot_plain(turned[4 + block], hidden_low[:, lanes]))
         branch_two = dot_plain(down_turned[...], active[:, :, lanes].reshape(4 * width, piece))
-        sum_two = wide_a[...] + (branch_two + column(BIAS_DOWN))
-        normed_two = norm(sum_two, index, 1, norm_two)
-        output = normed_two * column(GAIN_TWO) + column(BIAS_TWO)
+        total = jnp.zeros((8, piece), F32)
+        for rows in chunks:
+            hidden = norm_one[rows, lanes] * column(GAIN_ONE, rows) + column(BIAS_ONE, rows)
+            sum_two = hidden + (branch_two[rows] + column(BIAS_DOWN, rows))
+            wide_a[rows, :] = sum_two
+            total = total + part_sum(sum_two)
+        mean, inverse = norm_chunks(index, 1, total)
+
+        def outputs(rows):
+            normed = (wide_a[rows, :] - mean) * inverse
+            norm_two[rows, lanes] = normed
+            return normed * column(GAIN_TWO, rows) + column(BIAS_TWO, rows)
 
         @pl.when(segment == 0)
         def _():
-            outgoing[index] = output.astype(BF16)
+            for rows in chunks:
+                outgoing[index, rows, :] = outputs(rows).astype(BF16)
             forward_copy(index).start()
 
         @pl.when(segment == 1)
         def _():
-            ends_v[index] = output.T
+            free_ends(index)
+            for start in range(0, width, LANES):
+                rows = slice(start, start + LANES)
+                ends_v[lax.rem(index, 2), :, rows] = outputs(rows).T
             ends_copy(index).start()
-
-    def norm_back(grad, index, which, normed_ref, gain):
-        lanes = lanes_of(index)
-        normed = normed_ref[:, lanes]
-        scaled = grad * column(gain)
-        inner = row_mean(scaled * normed)
-        return (scaled - row_mean(scaled) - normed * inner) * inverses[index, which]
 
     def attend_back(index, has_off):
         lanes = lanes_of(index)
         slot = jnp.where(index == 0, 1, 0)
+        half = LANES // 2
         score_scale = 1.0 / math.sqrt(width // HEADS)
-
-        def one_pair(pair, carry):
+        blank = jnp.zeros((LANES, LANES), BF16)
+        for pair in range(pairs):
             grads = grad_mix[pair]
             blocks = pair_blocks(grads)
             back = dot_plain(values_rm[index, pair], blocks)
             if has_off:
                 back_off = dot_plain(values_rm[0, pair], blocks)
-            half = grads.shape[0] // 2
             for head in range(2):
-                span = slice(head * piece, (head + 1) * piece)
                 rows = slice(head * half, (head + 1) * half)
-                low = share[index, pair, head]
-                wide = low.astype(F32)
-                product = wide * back[:, span]
-                inner = jnp.sum(product, axis=0, keepdims=True)
-                if has_off:
-                    low_off = share_off[pair, head]
-                    wide_off = low_off.astype(F32)
-                    product_off = wide_off * back_off[:, span]
-                    inner = inner + jnp.sum(product_off, axis=0, keepdims=True)
-                grad_scores = (product - wide * inner).astype(BF16)
+                for part in range(2):
+                    start = head * piece + part * LANES
+                    span = slice(start, start + LANES)
+                    place = slice(part * LANES, (part + 1) * LANES)
+                    shares = [share[index, pair, head, place, place].astype(F32)]
+                    backs = [back[place, span]]
+                    if part:
+                        shares.append(share[index, pair, head, :LANES, place].astype(F32))
+                        backs.append(back[:LANES, span])
+                    if has_off:
+                        for low_half in range(2):
+                            keys = slice(low_half * LANES, (low_half + 1) * LANES)
+                            shares.append(share_off[pair, head, keys, place].astype(F32))
+                            backs.append(back_off[keys, span])
+                    products = [left * right for left, right in zip(shares, backs)]
+                    inner = jnp.sum(functools.reduce(jnp.add, products), axis=0, keepdims=True)
+                    low = [
+                        (product - left * inner).astype(BF16)
+                        for product, left in zip(products, shares)
+                    ]
+                    score_grad[head, place, place] = low[0]
+                    if part:
+                        score_grad[head, :LANES, place] = low[1]
+                    else:
+                        score_grad[head, LANES:, place] = blank
+                    if has_off:
+                        score_grad[2 + head, :LANES, place] = low[-2]
+                        score_grad[2 + head, LANES:, place] = low[-1]
                 queries = qkv[0, pair, rows, lanes]
+                grad_scores = score_grad[head]
                 grad_query = dot_plain(qkv[1, pair, rows, lanes], grad_scores)
                 grad_key = dot_turned(queries, grad_scores) + key_sums[slot, 0, pair, rows]
-                grad_value = dot_turned(grads[rows], low) + key_sums[slot, 1, pair, rows]
+                grad_value = (
+                    dot_turned(grads[rows], share[index, pair, head])
+                    + key_sums[slot, 1, pair, rows]
+                )
                 if has_off:
-                    grad_off = (product_off - wide_off * inner).astype(BF16)
+                    grad_off = score_grad[2 + head]
                     grad_query = grad_query + dot_plain(qkv[1, pair, rows, :piece], grad_off)
                     key_sums[1, 0, pair, rows] = dot_turned(queries, grad_off)
-                    key_sums[1, 1, pair, rows] = dot_turned(grads[rows], low_off)
+                    key_sums[1, 1, pair, rows] = dot_turned(grads[rows], share_off[pair, head])
                 qkv[0, pair, rows, lanes] = (grad_query * score_scale).astype(BF16)
                 qkv[1, pair, rows, lanes] = grad_key.astype(BF16)
                 qkv[2, pair, rows, lanes] = grad_value.astype(BF16)
-            return carry
-
-        lax.fori_loop(0, pairs, one_pair, 0)
 
     def backward(index):
         lanes = lanes_of(index)
@@ -405,31 +456,54 @@
         def _():
             backward_copy(index).wait_recv()
 
-        grad = incoming_grad[index].astype(F32)
-        gather_sum(GAIN_TWO, grad * norm_two[:, lanes])
-        gather_sum(BIAS_TWO, grad)
-        grad_two = norm_back(grad, index, 1, norm_two, GAIN_TWO)
-        gather_sum(BIAS_DOWN, grad_two)
-        wide_a[...] = grad_two
-        down_grad[:, lanes] = grad_two.astype(BF16)
-
-        def down_block(block, carry):
+        plain = jnp.zeros((8, piece), F32)
+        inner = jnp.zeros((8, piece), F32)
+        for rows in chunks:
+            grad = incoming_grad[index, rows, :].astype(F32)
+            product = grad * norm_two[rows, lanes]
+            gather_sum(GAIN_TWO, rows, product)
+            gather_sum(BIAS_TWO, rows, grad)
+            gain = column(GAIN_TWO, rows)
+            plain = plain + part_sum(grad * gain)
+            inner = inner + part_sum(product * gain)
+        plain = full_mean(plain)
+        inner = full_mean(inner)
+        inverse = inverses[index, 1]
+        for rows in chunks:
+            scaled = incoming_grad[index, rows, :].astype(F32) * column(GAIN_TWO, rows)
+            grad_two = (scaled - plain - norm_two[rows, lanes] * inner) * inverse
+            gather_sum(BIAS_DOWN, rows, grad_two)
+            wide_a[rows, :] = grad_two
+            down_grad[rows, lanes] = grad_two.astype(BF16)
+
+        for block in range(4):
             back = dot_plain(w_down[block], down_grad[:, lanes])
-            grad_pre = back * slope[block, :, lanes].astype(F32)
-            gather_sum(BIAS_UP + block, grad_pre)
-            slope[block, :, lanes] = grad_pre.astype(BF16)
-            return carry
-
-        lax.fori_loop(0, 4, down_block, 0)
-        grad_hidden = wide_a[...] + dot_plain(
-            w_up[...], slope[:, :, lanes].reshape(4 * width, piece)
-        )
-        gather_sum(GAIN_ONE, grad_hidden * norm_one[:, lanes])
-        gather_sum(BIAS_ONE, grad_hidden)
-        grad_one = norm_back(grad_hidden, index, 0, norm_one, GAIN_ONE)
-        gather_sum(BIAS_OUT, grad_one)
-        wide_b[...] = grad_one
-        branch_grad[:, lanes] = grad_one.astype(BF16)
+            for rows in chunks:
+                grad_pre = back[rows] * slope[block, rows, lanes].astype(F32)
+                gather_sum(BIAS_UP + block, rows, grad_pre)
+                slope[block, rows, lanes] = grad_pre.astype(BF16)
+
+        through = dot_plain(w_up[...], slope[:, :, lanes].reshape(4 * width, piece))
+        plain = jnp.zeros((8, piece), F32)
+        inner = jnp.zeros((8, piece), F32)
+        for rows in chunks:
+            grad_hidden = wide_a[rows, :] + through[rows]
+            wide_a[rows, :] = grad_hidden
+            product = grad_hidden * norm_one[rows, lanes]
+            gather_sum(GAIN_ONE, rows, product)
+            gather_sum(BIAS_ONE, rows, grad_hidden)
+            gain = column(GAIN_ONE, rows)
+            plain = plain + part_sum(grad_hidden * gain)
+            inner = inner + part_sum(product * gain)
+        plain = full_mean(plain)
+        inner = full_mean(inner)
+        inverse = inverses[index, 0]
+        for rows in chunks:
+            scaled = wide_a[rows, :] * column(GAIN_ONE, rows)
+            grad_one = (scaled - plain - norm_one[rows, lanes] * inner) * inverse
+            gather_sum(BIAS_OUT, rows, grad_one)
+            wide_b[rows, :] = grad_one
+            branch_grad[rows, lanes] = grad_one.astype(BF16)
         grad_mix[...] = (
             dot_plain(w_out[...], branch_grad[:, lanes]).astype(BF16).reshape(pairs, LANES, piece)
         )
@@ -442,18 +516,20 @@
         def _():
             attend_back(index, False)
 
-        grad_input = wide_b[...] + dot_plain(
-            w_qkv[...], qkv[:, :, :, lanes].reshape(3 * width, piece)
-        )
+        through = dot_plain(w_qkv[...], qkv[:, :, :, lanes].reshape(3 * width, piece))
 
         @pl.when(segment == 1)
         def _():
-            outgoing[index] = grad_input.astype(BF16)
+            for rows in chunks:
+                outgoing[index, rows, :] = (wide_b[rows, :] + through[rows]).astype(BF16)
             backward_copy(index).start()
 
         @pl.when(segment == 0)
         def _():
-            ends_v[index] = grad_input.T
+            free_ends(index)
+            for start in range(0, width, LANES):
+                rows = slice(start, start + LANES)
+                ends_v[lax.rem(index, 2), :, rows] = (wide_b[rows, :] + through[rows]).T
             ends_copy(index).start()
 
     def one_step(step, carry):
@@ -709,6 +785,7 @@
         def _():
             backward_copy(index).wait_send()
 
+    for index in range(2, PIECES):
         ends_copy(index).wait()
     for group in range(3):
         fin_copy(group).wait()
@@ -728,34 +805,59 @@
     grad_up_bias,
     grad_gains,
     grad_biases,
-    sem,
+    fin_v,
+    wide_qkv,
+    wide_out,
+    wide_up,
+    wide_down,
+    ends_sem,
+    in_sem,
+    out_sem,
 ):
     half = ends_in.shape[0] // 2
     share_rows, width = fin.shape[2:]
     start = pl.multiple_of(half * (1 - flag_ref[0, 0]), half)
-    copies = [
+    ends_copies = [
         pltpu.make_async_copy(
-            ends_in.at[pl.ds(0, half)], ends.at[0, pl.ds(start, half)], sem.at[0]
+            ends_in.at[pl.ds(0, half)], ends.at[0, pl.ds(start, half)], ends_sem.at[0]
         ),
         pltpu.make_async_copy(
-            ends_in.at[pl.ds(half, half)], ends.at[0, pl.ds(half - start, half)], sem.at[1]
+            ends_in.at[pl.ds(half, half)], ends.at[0, pl.ds(half - start, half)], ends_sem.at[1]
         ),
     ]
-    for copy in copies:
+    loads = [
+        pltpu.make_async_copy(fin.at[group], fin_v.at[group], in_sem.at[group])
+        for group in range(3)
+    ]
+    stores = [
+        pltpu.make_async_copy(wide, target.at[0], out_sem.at[index])
+        for index, (wide, target) in enumerate(
+            ((wide_down, grad_down), (wide_up, grad_up), (wide_qkv, grad_qkv), (wide_out, grad_out))
+        )
+    ]
+    for copy in loads + ends_copies:
         copy.start()
+    loads[0].wait()
     for position in range(4):
-        columns = slice(position * width, (position + 1) * width)
         rows = slice(position * share_rows, (position + 1) * share_rows)
-        grad_down[0, rows, :] = fin[0, position].astype(F32)
-        grad_up[0, :, columns] = fin[1, position].astype(F32)
-        if position < 3:
-            grad_qkv[0, :, columns] = fin[2, position].astype(F32)
-        else:
-            grad_out[0] = fin[2, position].astype(F32)
+        wide_down[rows, :] = fin_v[0, position].astype(F32)
+    stores[0].start()
+    loads[1].wait()
+    for position in range(4):
+        wide_up[:, position * width : (position + 1) * width] = fin_v[1, position].astype(F32)
+    stores[1].start()
+    loads[2].wait()
+    for position in range(3):
+        wide_qkv[:, position * width : (position + 1) * width] = fin_v[2, position].astype(F32)
+    stores[2].start()
+    wide_out[...] = fin_v[2, 3].astype(F32)
+    stores[3].start()
+    for position in range(4):
+        rows = slice(position * share_rows, (position + 1) * share_rows)
         grad_up_bias[:, rows] = small[BIAS_UP + position : BIAS_UP + position + 1, :share_rows]
     grad_gains[0] = small[:2, :share_rows]
     grad_biases[0] = small[2:BIAS_UP, :share_rows]
-    for copy in copies:
+    for copy in stores + ends_copies:
         copy.wait()
 
 
@@ -820,9 +922,10 @@
             vmem((STATS, width, LANES), BF16),
             vmem((STATS, width, LANES), F32),
             vmem((2, 2, pairs, LANES, piece), F32),
+            vmem((4, piece, piece), BF16),
             vmem((width, piece), F32),
             vmem((width, piece), F32),
-            vmem((PIECES, piece, width), F32),
+            vmem((2, piece, width), F32),
             vmem((3, 2, width, width), BF16),
             vmem((3, width, width), BF16),
             vmem((3, dp_count - 1, share_rows, width), BF16),
@@ -878,10 +981,19 @@
             jax.ShapeDtypeStruct((1, 2, share_rows), F32),
             jax.ShapeDtypeStruct((1, 4, share_rows), F32),
         ),
-        in_specs=[smem_spec, any_spec, vmem_spec, vmem_spec],
-        out_specs=(any_spec,) + (vmem_spec,) * 7,
-        scratch_shapes=[dma((2,))],
-        compiler_params=pltpu.CompilerParams(vmem_limit_bytes=32 * 1024 * 1024),
+        in_specs=[smem_spec, any_spec, any_spec, vmem_spec],
+        out_specs=(any_spec,) * 5 + (vmem_spec,) * 3,
+        scratch_shapes=[
+            vmem((3, 4, share_rows, width), BF16),
+            vmem((share_rows, 3 * width), F32),
+            vmem((share_rows, width), F32),
+            vmem((share_rows, 4 * width), F32),
+            vmem((4 * share_rows, width), F32),
+            dma((2,)),
+            dma((3,)),
+            dma((4,)),
+        ],
+        compiler_params=pltpu.CompilerParams(vmem_limit_bytes=63 * 1024 * 1024),
     )(window_group, ends_in.reshape(rows, width), fin, small)
 
 

time: 155 us -> 203 us (1.31)
  Pallas kernels: 150 us -> 202 us
  local copies, waits for them, and re-layouts: 3.69 us -> 0 us
    pallas_call x1, Pallas kernels: 3.54 us -> 66 us  [on_device(): pl.pallas_call(finish_kernel, out_shape=(jax.ShapeDtypeStruct((1, rows, w...]
    pallas_call x1, Pallas kernels: 147 us -> 136 us  [on_device(): pl.pallas_call(functools.partial(layer_kernel, dp_count), out_shape=(jax....]
    unnamed x8 -> x0, local copies, waits for them, and re-layouts: 3.69 us -> none
where the time goes in v2:
time: 203 us
  Pallas kernels  202 us (100%)
    pallas_call x1, Pallas kernels, on_device(): pl.pallas_call(functools.partial(layer_kernel, dp_count), out_shape=(jax....  136 us
    pallas_call x1, Pallas kernels, on_device(): pl.pallas_call(finish_kernel, out_shape=(jax.ShapeDtypeStruct((1, rows, w...  66 us

profile of v2, /device:TPU:0, one launch (start us, length us, event | category | flops | bytes accessed | tf_op | source)
XLA Modules:
  0.0 202.9 jit_solution(6340263092554263076)
XLA Ops:
  0.6 136.1 %shard_map.161 = (f32[4,256,512]{2,1,0:T(8,128)}, bf16[3,4,128,512]{3,2,1,0:T(8,128)(2,1)}, f32[16,128]{1,0:T(8,128)}) custom-call(s32[1,2]{1,0:T(1,128)} %flag_ref.3, bf16[4,256,512]{2,1,0:T(8,128)(2,1)} %bitcast.4, bf16[4,256,512]{2,1,0:T(8,128)(2,1)} %bitcast.5, bf16[1,512,1536]{2,1,0:T(8,128)(2,1)} %w_qkv_hbm.1, bf16[1,512,512]{2,1,0:T(8,128)(2,1)} %w_out_hbm.1, ...), custom_call_target="tpu_custom_call" | custom-call | tf_op jit(solution)/shard_map/pallas_call | solution.py:887
  136.7 66.0 %shard_map.162 = (f32[1,1024,512]{2,1,0:T(8,128)}, f32[1,128,1536]{2,1,0:T(8,128)}, f32[1,128,512]{2,1,0:T(8,128)}, f32[1,128,2048]{2,1,0:T(8,128)}, f32[1,512,5...) custom-call(s32[1,2]{1,0:T(1,128)} %flag_ref.3, f32[1024,512]{1,0:T(8,128)} %bitcast.3, ...), custom_call_target="tpu_custom_call" | custom-call | tf_op jit(solution)/shard_map/pallas_call | solution.py:972

commit v3 on v2

--- a/solution.py
+++ b/solution.py
@@ -33,6 +33,17 @@
     for start in range(LANES, values.shape[1], LANES):
         total = total + values[:, start : start + LANES]
     return total
+
+
+def normal_level(values, bell):
+    depth = 1.0 + jnp.abs(values) * (0.3275911 / math.sqrt(2.0))
+    near = pl.reciprocal(depth, approx=True)
+    near = near * (2.0 - depth * near)
+    series = near * (0.5 * 1.061405429) + (0.5 * -1.453152027)
+    for factor in (1.421413741, -0.284496736, 0.254829592):
+        series = series * near + 0.5 * factor
+    upper = series * near * bell
+    return jnp.where(values < 0.0, upper, 1.0 - upper)
 
 
 def pair_blocks(values):
@@ -351,10 +362,12 @@
         def activate(block, pre_block):
             for rows in chunks:
                 pre = pre_block[rows] + column(BIAS_UP + block, rows)
+                bell = jnp.exp2(pre * pre * (-0.5 * math.log2(math.e)))
                 level = (lax.erf(pre * (1.0 / math.sqrt(2.0))) + 1.0) * 0.5
                 active[block, rows, lanes] = (pre * level).astype(BF16)
-                bell = jnp.exp(-0.5 * pre * pre) * (1.0 / math.sqrt(2.0 * math.pi))
-                slope[block, rows, lanes] = (level + pre * bell).astype(BF16)
+                slope[block, rows, lanes] = (
+                    level + pre * bell * (1.0 / math.sqrt(2.0 * math.pi))
+                ).astype(BF16)
 
         for block in range(4):
             activate(block, dot_plain(turned[4 + block], hidden_low[:, lanes]))
@@ -508,6 +521,9 @@
             dot_plain(w_out[...], branch_grad[:, lanes]).astype(BF16).reshape(pairs, LANES, piece)
         )
 
+    def backward_attention(index):
+        lanes = lanes_of(index)
+
         @pl.when(index == 1)
         def _():
             attend_back(index, True)
@@ -532,171 +548,218 @@
                 ends_v[lax.rem(index, 2), :, rows] = (wide_b[rows, :] + through[rows]).T
             ends_copy(index).start()
 
+    def held(job):
+        group = job // 2
+        return (w_down, 0) if group == 0 else (turned, 4 if group == 1 else 0)
+
+    def core_copy(job):
+        buffer, base = held(job)
+        lanes = lanes_in(job)
+        return pltpu.make_async_remote_copy(
+            src_ref=buffer.at[pl.ds(base + 2 * (1 - core), 2), :, lanes],
+            dst_ref=core_in.at[job // 2, :, :, lanes],
+            send_sem=core_send.at[job],
+            recv_sem=core_recv.at[job],
+            device_id={"rep": other_core},
+            device_id_type=MESH,
+        )
+
+    def side_copy(job):
+        buffer, base = held(job)
+        lanes = lanes_in(job)
+        return pltpu.make_async_remote_copy(
+            src_ref=buffer.at[base + 2 * core + (1 - side), :, lanes],
+            dst_ref=side_in.at[job // 2, :, lanes],
+            send_sem=side_send.at[job],
+            recv_sem=side_recv.at[job],
+            device_id={"rep": other_side},
+            device_id_type=MESH,
+        )
+
+    def dp_copy(job, step):
+        buffer, base = held(job)
+        lanes = lanes_in(job)
+        target = lax.rem(dp + step, dp_count)
+        rows = pl.ds(pl.multiple_of(target * share_rows, share_rows), share_rows)
+        return pltpu.make_async_remote_copy(
+            src_ref=buffer.at[base + 2 * core + side, rows, lanes],
+            dst_ref=dp_in.at[job // 2, step - 1, :, lanes],
+            send_sem=dp_send.at[job, step - 1],
+            recv_sem=dp_recv.at[job, step - 1],
+            device_id={"dp": target},
+            device_id_type=MESH,
+        )
+
+    def join_copy(job):
+        lanes = lanes_in(job)
+        return pltpu.make_async_remote_copy(
+            src_ref=fin.at[job // 2, 2 * core + side, :, lanes],
+            dst_ref=fin.at[job // 2, 2 * core + side, :, lanes],
+            send_sem=join_send.at[job],
+            recv_sem=join_recv.at[job],
+            device_id={"rep": other_side},
+            device_id_type=MESH,
+        )
+
+    def last_copy(job):
+        lanes = lanes_in(job)
+        return pltpu.make_async_remote_copy(
+            src_ref=fin.at[job // 2, pl.ds(2 * core, 2), :, lanes],
+            dst_ref=fin.at[job // 2, pl.ds(2 * core, 2), :, lanes],
+            send_sem=last_send.at[job],
+            recv_sem=last_recv.at[job],
+            device_id={"rep": other_core},
+            device_id_type=MESH,
+        )
+
+    def lanes_in(job):
+        half = job % 2
+        return slice(half * (width // 2), (half + 1) * (width // 2))
+
+    def down_sums(job):
+        part = 4 * share_rows
+        count = width // part
+        lanes = lanes_in(job)
+
+        def one(block, carry):
+            result = dot_turned(active[block], down_grad[lanes, :]).astype(BF16)
+            for each in range(count):
+                for position in range(4):
+                    start = each * part + position * share_rows
+                    target = pl.multiple_of((block * count + each) * share_rows, share_rows)
+                    w_down[position, pl.ds(target, share_rows), lanes] = result[
+                        start : start + share_rows
+                    ]
+            return carry
+
+        lax.fori_loop(0, 4, one, 0)
+
+    def up_sums(job):
+        lanes = lanes_in(job)
+
+        def one(block, carry):
+            turned[4 + block, :, lanes] = dot_turned(hidden_low[...], slope[block, lanes, :]).astype(
+                BF16
+            )
+            return carry
+
+        lax.fori_loop(0, 4, one, 0)
+
+    def qkv_sums(job):
+        lanes = lanes_in(job)
+        half_pairs = slice((job % 2) * (pairs // 2), (job % 2 + 1) * (pairs // 2))
+
+        def one(block, carry):
+            turned[block, :, lanes] = dot_turned(
+                x_t[...], qkv[block, half_pairs].reshape(width // 2, PIECES * piece)
+            ).astype(BF16)
+            return carry
+
+        lax.fori_loop(0, 3, one, 0)
+        turned[3, :, lanes] = dot_turned(
+            mixture[...].reshape(width, PIECES * piece), branch_grad[lanes, :]
+        ).astype(BF16)
+
+    def sums_of(job):
+        (down_sums, up_sums, qkv_sums)[job // 2](job)
+        core_copy(job).start()
+
+    def after_core(job):
+        buffer, base = held(job)
+        lanes = lanes_in(job)
+        copy = core_copy(job)
+        copy.wait_send()
+        copy.wait_recv()
+        first = base + 2 * core + (1 - side)
+        buffer[first, :, lanes] = (
+            buffer[first, :, lanes].astype(F32) + core_in[job // 2, 1 - side, :, lanes].astype(F32)
+        ).astype(BF16)
+
+    def after_side(job):
+        buffer, base = held(job)
+        lanes = lanes_in(job)
+        copy = side_copy(job)
+        copy.wait_send()
+        copy.wait_recv()
+        second = base + 2 * core + side
+        buffer[second, :, lanes] = (
+            buffer[second, :, lanes].astype(F32)
+            + core_in[job // 2, side, :, lanes].astype(F32)
+            + side_in[job // 2, :, lanes].astype(F32)
+        ).astype(BF16)
+        for step in range(1, dp_count):
+            dp_copy(job, step).start()
+
+    def after_dp(job):
+        buffer, base = held(job)
+        lanes = lanes_in(job)
+        rows = pl.ds(pl.multiple_of(dp * share_rows, share_rows), share_rows)
+        total = buffer[base + 2 * core + side, rows, lanes].astype(F32)
+        for step in range(1, dp_count):
+            copy = dp_copy(job, step)
+            copy.wait_send()
+            copy.wait_recv()
+            total = total + dp_in[job // 2, step - 1, :, lanes].astype(F32)
+        fin[job // 2, 2 * core + side, :, lanes] = total.astype(BF16)
+        join_copy(job).start()
+
+    def after_join(job):
+        copy = join_copy(job)
+        copy.wait_send()
+        copy.wait_recv()
+        last_copy(job).start()
+
+    def fin_copy(job):
+        lanes = lanes_in(job)
+        return pltpu.make_async_copy(
+            fin.at[job // 2, :, :, lanes], fin_hbm.at[job // 2, :, :, lanes], fin_sem.at[job]
+        )
+
+    def after_last(job):
+        copy = last_copy(job)
+        copy.wait_send()
+        copy.wait_recv()
+        fin_copy(job).start()
+
+    def early_sums():
+        sums_of(0)
+        sums_of(1)
+        after_core(0)
+        side_copy(0).start()
+        sums_of(2)
+        sums_of(3)
+        after_core(1)
+        side_copy(1).start()
+
     def one_step(step, carry):
         first_index = jnp.where(step < 4, step, jnp.where(step < 6, 5 - step, step - 4))
         last_index = jnp.where(step < 2, step, jnp.where(step < 4, 3 - step, lax.div(step, 2)))
         first_is = jnp.where(step < 4, 1, 0)
         last_is = jnp.where(step < 2, 1, jnp.where(step < 4, 0, 1 - lax.rem(step, 2)))
-        index = jnp.where(segment == 0, first_index, last_index)
+        index = jnp.minimum(jnp.where(segment == 0, first_index, last_index), PIECES - 1)
         is_forward = jnp.where(segment == 0, first_is, last_is)
-
-        @pl.when(is_forward == 1)
+        is_last = jnp.where(step == 2 * PIECES, 1, 0)
+        is_split = jnp.where(step >= 2 * PIECES - 1, 1 - segment, 0)
+
+        @pl.when(is_forward * (1 - is_last) == 1)
         def _():
             forward(index)
 
-        @pl.when(is_forward == 0)
+        @pl.when(is_forward + is_last == 0)
         def _():
             backward(index)
 
+        @pl.when(is_last == 1)
+        def _():
+            early_sums()
+
+        @pl.when((1 - is_forward) * (1 - is_split) * (1 - is_last) + is_last * is_split == 1)
+        def _():
+            backward_attention(index)
+
         return carry
 
-    lax.fori_loop(0, 2 * PIECES, one_step, 0)
-
-    def held(group):
-        return (w_down, 0) if group == 0 else (turned, 4 if group == 1 else 0)
-
-    def core_copy(group):
-        buffer, base = held(group)
-        return pltpu.make_async_remote_copy(
-            src_ref=buffer.at[pl.ds(base + 2 * (1 - core), 2)],
-            dst_ref=core_in.at[group],
-            send_sem=core_send.at[group],
-            recv_sem=core_recv.at[group],
-            device_id={"rep": other_core},
-            device_id_type=MESH,
-        )
-
-    def side_copy(group):
-        buffer, base = held(group)
-        return pltpu.make_async_remote_copy(
-            src_ref=buffer.at[base + 2 * core + (1 - side)],
-            dst_ref=side_in.at[group],
-            send_sem=side_send.at[group],
-            recv_sem=side_recv.at[group],
-            device_id={"rep": other_side},
-            device_id_type=MESH,
-        )
-
-    def dp_copy(group, step):
-        buffer, base = held(group)
-        target = lax.rem(dp + step, dp_count)
-        rows = pl.ds(pl.multiple_of(target * share_rows, share_rows), share_rows)
-        return pltpu.make_async_remote_copy(
-            src_ref=buffer.at[base + 2 * core + side, rows],
-            dst_ref=dp_in.at[group, step - 1],
-            send_sem=dp_send.at[group, step - 1],
-            recv_sem=dp_recv.at[group, step - 1],
-            device_id={"dp": target},
-            device_id_type=MESH,
-        )
-
-    def join_copy(group):
-        return pltpu.make_async_remote_copy(
-            src_ref=fin.at[group, 2 * core + side],
-            dst_ref=fin.at[group, 2 * core + side],
-            send_sem=join_send.at[group],
-            recv_sem=join_recv.at[group],
-            device_id={"rep": other_side},
-            device_id_type=MESH,
-        )
-
-    def last_copy(group):
-        return pltpu.make_async_remote_copy(
-            src_ref=fin.at[group, pl.ds(2 * core, 2)],
-            dst_ref=fin.at[group, pl.ds(2 * core, 2)],
-            send_sem=last_send.at[group],
-            recv_sem=last_recv.at[group],
-            device_id={"rep": other_core},
-            device_id_type=MESH,
-        )
-
-    def down_sums():
-        part = 4 * share_rows
-        count = width // part
-
-        def one(block, carry):
-            result = dot_turned(active[block], down_grad[...]).astype(BF16)
-            for each in range(count):
-                for position in range(4):
-                    start = each * part + position * share_rows
-                    target = pl.multiple_of((block * count + each) * share_rows, share_rows)
-                    w_down[position, pl.ds(target, share_rows), :] = result[
-                        start : start + share_rows
-                    ]
-            return carry
-
-        lax.fori_loop(0, 4, one, 0)
-
-    def up_sums():
-        def one(block, carry):
-            turned[4 + block] = dot_turned(hidden_low[...], slope[block]).astype(BF16)
-            return carry
-
-        lax.fori_loop(0, 4, one, 0)
-
-    def qkv_sums():
-        def one(block, carry):
-            turned[block] = dot_turned(
-                x_t[...], qkv[block].reshape(width, PIECES * piece)
-            ).astype(BF16)
-            return carry
-
-        lax.fori_loop(0, 3, one, 0)
-        turned[3] = dot_turned(
-            mixture[...].reshape(width, PIECES * piece), branch_grad[...]
-        ).astype(BF16)
-
-    def after_core(group):
-        buffer, base = held(group)
-        copy = core_copy(group)
-        copy.wait_send()
-        copy.wait_recv()
-        first = base + 2 * core + (1 - side)
-        buffer[first] = (
-            buffer[first].astype(F32) + core_in[group, 1 - side].astype(F32)
-        ).astype(BF16)
-        side_copy(group).start()
-
-    def after_side(group):
-        buffer, base = held(group)
-        copy = side_copy(group)
-        copy.wait_send()
-        copy.wait_recv()
-        second = base + 2 * core + side
-        buffer[second] = (
-            buffer[second].astype(F32)
-            + core_in[group, side].astype(F32)
-            + side_in[group].astype(F32)
-        ).astype(BF16)
-        for step in range(1, dp_count):
-            dp_copy(group, step).start()
-
-    def after_dp(group):
-        buffer, base = held(group)
-        rows = pl.ds(pl.multiple_of(dp * share_rows, share_rows), share_rows)
-        total = buffer[base + 2 * core + side, rows, :].astype(F32)
-        for step in range(1, dp_count):
-            copy = dp_copy(group, step)
-            copy.wait_send()
-            copy.wait_recv()
-            total = total + dp_in[group, step - 1].astype(F32)
-        fin[group, 2 * core + side] = total.astype(BF16)
-        join_copy(group).start()
-
-    def after_join(group):
-        copy = join_copy(group)
-        copy.wait_send()
-        copy.wait_recv()
-        last_copy(group).start()
-
-    def fin_copy(group):
-        return pltpu.make_async_copy(fin.at[group], fin_hbm.at[group], fin_sem.at[group])
-
-    def after_last(group):
-        copy = last_copy(group)
-        copy.wait_send()
-        copy.wait_recv()
-        fin_copy(group).start()
+    lax.fori_loop(0, 2 * PIECES + 1, one_step, 0)
 
     def small_dp_copy(step):
         target = lax.rem(dp + step, dp_count)
@@ -719,14 +782,11 @@
             device_id_type=MESH,
         )
 
-    down_sums()
-    core_copy(0).start()
-    up_sums()
-    core_copy(1).start()
-    after_core(0)
-    qkv_sums()
-    core_copy(2).start()
-    after_core(1)
+    sums_of(4)
+    sums_of(5)
+    after_core(2)
+    after_side(0)
+    side_copy(2).start()
 
     rows_of = [jnp.sum(sums[index].T, axis=0, keepdims=True) for index in range(STATS)]
     small[...] = jnp.zeros(small.shape, F32)
@@ -745,8 +805,10 @@
     for step in range(1, dp_count):
         small_dp_copy(step).start()
 
-    after_core(2)
-    after_side(0)
+
+    after_core(3)
+    after_side(1)
+    side_copy(3).start()
     small_total = small[dp]
     for step in range(1, dp_count):
         copy = small_dp_copy(step)
@@ -756,13 +818,22 @@
     small_rep[rep] = small_total
     for step in range(1, 4):
         small_rep_copy(step).start()
-    after_side(1)
+    after_core(4)
     after_dp(0)
     after_side(2)
+    side_copy(4).start()
+    after_core(5)
+    after_dp(1)
     after_join(0)
-    after_dp(1)
+    after_side(3)
+    side_copy(5).start()
     after_last(0)
+    after_dp(2)
     after_join(1)
+    after_side(4)
+    after_last(1)
+    after_dp(3)
+    after_join(2)
     for step in range(1, 4):
         copy = small_rep_copy(step)
         copy.wait_send()
@@ -770,10 +841,16 @@
     small_out[...] = (small_rep[0] + small_rep[1]) + (small_rep[2] + small_rep[3])
     small_copy = pltpu.make_async_copy(small_out, small_hbm, load_sem.at[0])
     small_copy.start()
-    after_last(1)
-    after_dp(2)
-    after_join(2)
+    after_side(5)
     after_last(2)
+    after_dp(4)
+    after_join(3)
+    after_last(3)
+    after_dp(5)
+    after_join(4)
+    after_last(4)
+    after_join(5)
+    after_last(5)
 
     for index in range(PIECES):
 
@@ -787,8 +864,8 @@
 
     for index in range(2, PIECES):
         ends_copy(index).wait()
-    for group in range(3):
-        fin_copy(group).wait()
+    for job in range(6):
+        fin_copy(job).wait()
     small_copy.wait()
 
 
@@ -805,6 +882,7 @@
     grad_up_bias,
     grad_gains,
     grad_biases,
+    ends_v,
     fin_v,
     wide_qkv,
     wide_out,
@@ -819,11 +897,19 @@
     start = pl.multiple_of(half * (1 - flag_ref[0, 0]), half)
     ends_copies = [
         pltpu.make_async_copy(
-            ends_in.at[pl.ds(0, half)], ends.at[0, pl.ds(start, half)], ends_sem.at[0]
+            ends_v.at[pl.ds(0, half)], ends.at[0, pl.ds(start, half)], ends_sem.at[0]
         ),
         pltpu.make_async_copy(
-            ends_in.at[pl.ds(half, half)], ends.at[0, pl.ds(half - start, half)], ends_sem.at[1]
+            ends_v.at[pl.ds(half, half)], ends.at[0, pl.ds(half - start, half)], ends_sem.at[1]
         ),
+    ]
+    ends_loads = [
+        pltpu.make_async_copy(
+            ends_in.at[pl.ds(part * half, half)],
+            ends_v.at[pl.ds(part * half, half)],
+            ends_sem.at[2 + part],
+        )
+        for part in range(2)
     ]
     loads = [
         pltpu.make_async_copy(fin.at[group], fin_v.at[group], in_sem.at[group])
@@ -835,7 +921,10 @@
             ((wide_down, grad_down), (wide_up, grad_up), (wide_qkv, grad_qkv), (wide_out, grad_out))
         )
     ]
-    for copy in loads + ends_copies:
+    for copy in loads + ends_loads:
+        copy.start()
+    for load, copy in zip(ends_loads, ends_copies):
+        load.wait()
         copy.start()
     loads[0].wait()
     for position in range(4):
@@ -938,21 +1027,21 @@
             dma((PIECES,)),
             dma((PIECES,)),
             dma((PIECES,)),
-            dma((3,)),
-            dma((3,)),
-            dma((3,)),
-            dma((3,)),
-            dma((3, dp_count - 1)),
-            dma((3, dp_count - 1)),
-            dma((3,)),
-            dma((3,)),
-            dma((3,)),
-            dma((3,)),
+            dma((6,)),
+            dma((6,)),
+            dma((6,)),
+            dma((6,)),
+            dma((6, dp_count - 1)),
+            dma((6, dp_count - 1)),
+            dma((6,)),
+            dma((6,)),
+            dma((6,)),
+            dma((6,)),
             dma((dp_count - 1,)),
             dma((dp_count - 1,)),
             dma((3,)),
             dma((3,)),
-            dma((3,)),
+            dma((6,)),
         ],
         compiler_params=pltpu.CompilerParams(
             collective_id=0, has_side_effects=True, vmem_limit_bytes=63 * 1024 * 1024
@@ -984,12 +1073,13 @@
         in_specs=[smem_spec, any_spec, any_spec, vmem_spec],
         out_specs=(any_spec,) * 5 + (vmem_spec,) * 3,
         scratch_shapes=[
+            vmem((rows, width), F32),
             vmem((3, 4, share_rows, width), BF16),
             vmem((share_rows, 3 * width), F32),
             vmem((share_rows, width), F32),
             vmem((share_rows, 4 * width), F32),
             vmem((4 * share_rows, width), F32),
-            dma((2,)),
+            dma((4,)),
             dma((3,)),
             dma((4,)),
         ],

time: 203 us -> 137 us (0.67)
  Pallas kernels: 202 us -> 136 us
    pallas_call x1, Pallas kernels: 66 us -> 5.39 us  [on_device(): pl.pallas_call(finish_kernel, out_shape=(jax.ShapeDtypeStruct((1, rows, w...]
    pallas_call x1, Pallas kernels: 136 us -> 131 us  [on_device(): pl.pallas_call(functools.partial(layer_kernel, dp_count), out_shape=(jax....]
where the time goes in v3:
time: 137 us
  Pallas kernels  136 us (99%)
    pallas_call x1, Pallas kernels, on_device(): pl.pallas_call(functools.partial(layer_kernel, dp_count), out_shape=(jax....  131 us
    pallas_call x1, Pallas kernels, on_device(): pl.pallas_call(finish_kernel, out_shape=(jax.ShapeDtypeStruct((1, rows, w...  5.39 us

profile of v3, /device:TPU:0, one launch (start us, length us, event | category | flops | bytes accessed | tf_op | source)
XLA Modules:
  0.0 137.1 jit_solution(1110032303539068965)
XLA Ops:
  0.6 130.9 %shard_map.161 = (f32[4,256,512]{2,1,0:T(8,128)}, bf16[3,4,128,512]{3,2,1,0:T(8,128)(2,1)}, f32[16,128]{1,0:T(8,128)}) custom-call(s32[1,2]{1,0:T(1,128)} %flag_ref.3, bf16[4,256,512]{2,1,0:T(8,128)(2,1)} %bitcast.4, bf16[4,256,512]{2,1,0:T(8,128)(2,1)} %bitcast.5, bf16[1,512,1536]{2,1,0:T(8,128)(2,1)} %w_qkv_hbm.1, bf16[1,512,512]{2,1,0:T(8,128)(2,1)} %w_out_hbm.1, ...), custom_call_target="tpu_custom_call" | custom-call | tf_op jit(solution)/shard_map/pallas_call | solution.py:976
  131.6 5.4 %shard_map.162 = (f32[1,1024,512]{2,1,0:T(8,128)}, f32[1,128,1536]{2,1,0:T(8,128)}, f32[1,128,512]{2,1,0:T(8,128)}, f32[1,128,2048]{2,1,0:T(8,128)}, f32[1,512,5...) custom-call(s32[1,2]{1,0:T(1,128)} %flag_ref.3, f32[1024,512]{1,0:T(8,128)} %bitcast.3, ...), custom_call_target="tpu_custom_call" | custom-call | tf_op jit(solution)/shard_map/pallas_call | solution.py:1061

commit v4 on v3

--- a/solution.py
+++ b/solution.py
@@ -255,7 +255,7 @@
         query_at = lax.broadcasted_iota(jnp.int32, (LANES, LANES), 1)
         allowed = key_at <= query_at
         blank = jnp.zeros((LANES, LANES), BF16)
-        for pair in range(pairs):
+        def one_pair(pair, carry):
             queries = pair_blocks(qkv[0, pair, :, lanes])
             scores = dot_plain(keys_rm[index, pair], queries)
             if has_off:
@@ -290,6 +290,9 @@
                 if has_off:
                     mixed = mixed + dot_plain(qkv[2, pair, rows, :piece], share_off[pair, head])
                 mixture[pair, rows, lanes] = mixed.astype(BF16)
+            return carry
+
+        lax.fori_loop(0, pairs, one_pair, 0)
 
     def part_sum(values):
         return jnp.sum(values.reshape(values.shape[0] // 8, 8, values.shape[1]), axis=0)
@@ -369,8 +372,11 @@
                     level + pre * bell * (1.0 / math.sqrt(2.0 * math.pi))
                 ).astype(BF16)
 
-        for block in range(4):
+        def up_block(block, carry):
             activate(block, dot_plain(turned[4 + block], hidden_low[:, lanes]))
+            return carry
+
+        lax.fori_loop(0, 4, up_block, 0)
         branch_two = dot_plain(down_turned[...], active[:, :, lanes].reshape(4 * width, piece))
         total = jnp.zeros((8, piece), F32)
         for rows in chunks:
@@ -405,7 +411,7 @@
         half = LANES // 2
         score_scale = 1.0 / math.sqrt(width // HEADS)
         blank = jnp.zeros((LANES, LANES), BF16)
-        for pair in range(pairs):
+        def one_pair(pair, carry):
             grads = grad_mix[pair]
             blocks = pair_blocks(grads)
             back = dot_plain(values_rm[index, pair], blocks)
@@ -457,6 +463,9 @@
                 qkv[0, pair, rows, lanes] = (grad_query * score_scale).astype(BF16)
                 qkv[1, pair, rows, lanes] = grad_key.astype(BF16)
                 qkv[2, pair, rows, lanes] = grad_value.astype(BF16)
+            return carry
+
+        lax.fori_loop(0, pairs, one_pair, 0)
 
     def backward(index):
         lanes = lanes_of(index)
@@ -489,12 +498,15 @@
             wide_a[rows, :] = grad_two
             down_grad[rows, lanes] = grad_two.astype(BF16)
 
-        for block in range(4):
+        def down_block(block, carry):
             back = dot_plain(w_down[block], down_grad[:, lanes])
             for rows in chunks:
                 grad_pre = back[rows] * slope[block, rows, lanes].astype(F32)
                 gather_sum(BIAS_UP + block, rows, grad_pre)
                 slope[block, rows, lanes] = grad_pre.astype(BF16)
+            return carry
+
+        lax.fori_loop(0, 4, down_block, 0)
 
         through = dot_plain(w_up[...], slope[:, :, lanes].reshape(4 * width, piece))
         plain = jnp.zeros((8, piece), F32)

time: 137 us -> 147 us (1.073)
  Pallas kernels: 136 us -> 146 us
    pallas_call x1, Pallas kernels: 131 us -> 140 us  [on_device(): pl.pallas_call(functools.partial(layer_kernel, dp_count), out_shape=(jax....]
where the time goes in v4:
time: 147 us; the launch traced here: 146 us
  Pallas kernels  146 us (99%)
    pallas_call x1, Pallas kernels, on_device(): pl.pallas_call(functools.partial(layer_kernel, dp_count), out_shape=(jax....  140 us
    pallas_call x1, Pallas kernels, on_device(): pl.pallas_call(finish_kernel, out_shape=(jax.ShapeDtypeStruct((1, rows, w...  5.39 us

profile of v4, /device:TPU:0, one launch (start us, length us, event | category | flops | bytes accessed | tf_op | source)
XLA Modules:
  0.0 146.3 jit_solution(5509240319840392577)
XLA Ops:
  0.6 140.3 %shard_map.161 = (f32[4,256,512]{2,1,0:T(8,128)}, bf16[3,4,128,512]{3,2,1,0:T(8,128)(2,1)}, f32[16,128]{1,0:T(8,128)}) custom-call(s32[1,2]{1,0:T(1,128)} %flag_ref.3, bf16[4,256,512]{2,1,0:T(8,128)(2,1)} %bitcast.4, bf16[4,256,512]{2,1,0:T(8,128)(2,1)} %bitcast.5, bf16[1,512,1536]{2,1,0:T(8,128)(2,1)} %w_qkv_hbm.1, bf16[1,512,512]{2,1,0:T(8,128)(2,1)} %w_out_hbm.1, ...), custom_call_target="tpu_custom_call" | custom-call | tf_op jit(solution)/shard_map/pallas_call | solution.py:988
  140.9 5.4 %shard_map.162 = (f32[1,1024,512]{2,1,0:T(8,128)}, f32[1,128,1536]{2,1,0:T(8,128)}, f32[1,128,512]{2,1,0:T(8,128)}, f32[1,128,2048]{2,1,0:T(8,128)}, f32[1,512,5...) custom-call(s32[1,2]{1,0:T(1,128)} %flag_ref.3, f32[1024,512]{1,0:T(8,128)} %bitcast.3, ...), custom_call_target="tpu_custom_call" | custom-call | tf_op jit(solution)/shard_map/pallas_call | solution.py:1073

commit v5 on v3

--- a/solution.py
+++ b/solution.py
@@ -33,25 +33,6 @@
     for start in range(LANES, values.shape[1], LANES):
         total = total + values[:, start : start + LANES]
     return total
-
-
-def normal_level(values, bell):
-    depth = 1.0 + jnp.abs(values) * (0.3275911 / math.sqrt(2.0))
-    near = pl.reciprocal(depth, approx=True)
-    near = near * (2.0 - depth * near)
-    series = near * (0.5 * 1.061405429) + (0.5 * -1.453152027)
-    for factor in (1.421413741, -0.284496736, 0.254829592):
-        series = series * near + 0.5 * factor
-    upper = series * near * bell
-    return jnp.where(values < 0.0, upper, 1.0 - upper)
-
-
-def pair_blocks(values):
-    half = values.shape[0] // 2
-    blank = jnp.zeros((half, values.shape[1]), values.dtype)
-    first = jnp.concatenate([values[:half], blank], axis=0)
-    second = jnp.concatenate([blank, values[half:]], axis=0)
-    return jnp.concatenate([first, second], axis=1)
 
 
 def layer_kernel(
@@ -97,7 +78,6 @@
     columns,
     sums,
     key_sums,
-    score_grad,
     wide_a,
     wide_b,
     ends_v,
@@ -141,13 +121,17 @@
     other_core = side * 2 + (1 - core)
     other_side = (1 - side) * 2 + core
 
-    loads = [
-        (w_qkv_hbm.at[0], w_qkv),
-        (w_out_hbm.at[0], w_out),
-        (w_up_hbm.at[0], w_up),
-    ]
+    loads = []
+    for block in range(3):
+        span = pl.ds(block * width, width)
+        loads.append((w_qkv_hbm.at[0, :, span], w_qkv.at[:, span]))
+    loads.append((w_out_hbm.at[0], w_out))
     for block in range(4):
-        loads.append((w_down_hbm.at[0, pl.ds(block * width, width), :], w_down.at[block]))
+        span = pl.ds(block * width, width)
+        loads.append((w_up_hbm.at[0, :, span], w_up.at[:, span]))
+    for block in range(4):
+        span = pl.ds(block * width, width)
+        loads.append((w_down_hbm.at[0, span, :], w_down.at[block]))
     load_copies = [
         pltpu.make_async_copy(source, target, load_sem.at[index + 1])
         for index, (source, target) in enumerate(loads)
@@ -192,17 +176,18 @@
 
     chunks = [slice(start, start + CHUNK) for start in range(0, width, CHUNK)]
 
-    for copy in load_copies:
+    for block, copy in enumerate(load_copies):
         copy.wait()
+        span = slice(block % 4 * width, (block % 4 + 1) * width)
+        if block < 3:
+            turned[block] = w_qkv[:, span].T
+        elif block == 3:
+            turned[block] = w_out[...].T
+        elif block < 8:
+            turned[block] = w_up[:, span].T
+        else:
+            down_turned[:, span] = w_down[block - 8].T
     first_rows.wait()
-
-    for block in range(3):
-        turned[block] = w_qkv[:, block * width : (block + 1) * width].T
-    turned[3] = w_out[...].T
-    for block in range(4):
-        turned[4 + block] = w_up[:, block * width : (block + 1) * width].T
-    for block in range(4):
-        down_turned[:, block * width : (block + 1) * width] = w_down[block].T
 
     pl.semaphore_wait(barrier, 4 + dp_count - 1)
 
@@ -248,48 +233,84 @@
         picked = rows_in[half].astype(F32) * weight + rows_in[2 + half].astype(F32) * (1.0 - weight)
         return picked.T
 
+    def by_queries(values):
+        half = LANES // 2
+        blank = jnp.zeros((half, LANES), values.dtype)
+        parts = []
+        for part in range(2):
+            span = slice(part * LANES, (part + 1) * LANES)
+            first = jnp.concatenate([values[:half, span], blank], axis=0)
+            second = jnp.concatenate([blank, values[half:, span]], axis=0)
+            parts.append(jnp.concatenate([first, second], axis=1))
+        return parts
+
+    def against(rows_ref, index, pair, parts, has_off):
+        own = rows_ref[index, pair]
+        products = [dot_plain(own[:LANES], parts[0]), dot_plain(own, parts[1])]
+        if has_off:
+            before = rows_ref[0, pair]
+            products += [dot_plain(before, parts[0]), dot_plain(before, parts[1])]
+        return products
+
+    def tiles_of(products, head, part, has_off):
+        lanes = slice(head * LANES, (head + 1) * LANES)
+        own = products[part]
+        tiles = [own[part * LANES : (part + 1) * LANES, lanes]]
+        if part:
+            tiles.append(own[:LANES, lanes])
+        if has_off:
+            off = products[2 + part]
+            tiles += [off[:LANES, lanes], off[LANES:, lanes]]
+        return tiles
+
+    def joined(lows, has_off):
+        blank = jnp.zeros((LANES, LANES), BF16)
+        first = jnp.concatenate([lows[0][0], blank], axis=0)
+        second = jnp.concatenate([lows[1][1], lows[1][0]], axis=0)
+        whole = jnp.concatenate([first, second], axis=1)
+        if not has_off:
+            return whole, None
+        first = jnp.concatenate(lows[0][-2:], axis=0)
+        second = jnp.concatenate(lows[1][-2:], axis=0)
+        return whole, jnp.concatenate([first, second], axis=1)
+
     def attend(index, has_off):
         lanes = lanes_of(index)
         half = LANES // 2
         key_at = lax.broadcasted_iota(jnp.int32, (LANES, LANES), 0)
         query_at = lax.broadcasted_iota(jnp.int32, (LANES, LANES), 1)
         allowed = key_at <= query_at
-        blank = jnp.zeros((LANES, LANES), BF16)
+
+        def scores_of(pair):
+            return against(
+                keys_rm, index, pair, by_queries(qkv[0, pair, :, lanes]), has_off
+            )
+
+        ahead = scores_of(0)
         for pair in range(pairs):
-            queries = pair_blocks(qkv[0, pair, :, lanes])
-            scores = dot_plain(keys_rm[index, pair], queries)
-            if has_off:
-                scores_off = dot_plain(keys_rm[0, pair], queries)
+            scores = ahead
+            if pair + 1 < pairs:
+                ahead = scores_of(pair + 1)
+            mixed = []
             for head in range(2):
                 rows = slice(head * half, (head + 1) * half)
+                lows = []
                 for part in range(2):
-                    start = head * piece + part * LANES
-                    span = slice(start, start + LANES)
-                    place = slice(part * LANES, (part + 1) * LANES)
-                    tiles = [jnp.where(allowed, scores[place, span], -1e30)]
-                    if part:
-                        tiles.append(scores[:LANES, span])
-                    if has_off:
-                        tiles.append(scores_off[:LANES, span])
-                        tiles.append(scores_off[LANES:, span])
-                    top = functools.reduce(jnp.maximum, tiles)
-                    top = jnp.max(top, axis=0, keepdims=True)
+                    tiles = tiles_of(scores, head, part, has_off)
+                    tiles[0] = jnp.where(allowed, tiles[0], -1e30)
+                    top = jnp.max(functools.reduce(jnp.maximum, tiles), axis=0, keepdims=True)
                     raised = [jnp.exp(tile - top) for tile in tiles]
                     total = functools.reduce(jnp.add, raised)
                     scale = 1.0 / jnp.sum(total, axis=0, keepdims=True)
-                    low = [(tile * scale).astype(BF16) for tile in raised]
-                    share[index, pair, head, place, place] = low[0]
-                    if part:
-                        share[index, pair, head, :LANES, place] = low[1]
-                    else:
-                        share[index, pair, head, LANES:, place] = blank
-                    if has_off:
-                        share_off[pair, head, :LANES, place] = low[-2]
-                        share_off[pair, head, LANES:, place] = low[-1]
-                mixed = dot_plain(qkv[2, pair, rows, lanes], share[index, pair, head])
+                    lows.append([(tile * scale).astype(BF16) for tile in raised])
+                low, low_off = joined(lows, has_off)
+                share[index, pair, head] = low
+                mix = dot_plain(qkv[2, pair, rows, lanes], low)
                 if has_off:
-                    mixed = mixed + dot_plain(qkv[2, pair, rows, :piece], share_off[pair, head])
-                mixture[pair, rows, lanes] = mixed.astype(BF16)
+                    share_off[pair, head] = low_off
+                    mix = mix + dot_plain(qkv[2, pair, rows, :piece], low_off)
+                mixed.append(mix.astype(BF16))
+            mixture[pair, :, lanes] = jnp.concatenate(mixed, axis=0)
 
     def part_sum(values):
         return jnp.sum(values.reshape(values.shape[0] // 8, 8, values.shape[1]), axis=0)
@@ -380,90 +401,80 @@
             total = total + part_sum(sum_two)
         mean, inverse = norm_chunks(index, 1, total)
 
-        def outputs(rows):
-            normed = (wide_a[rows, :] - mean) * inverse
-            norm_two[rows, lanes] = normed
-            return normed * column(GAIN_TWO, rows) + column(BIAS_TWO, rows)
+        for rows in chunks:
+            norm_two[rows, lanes] = (wide_a[rows, :] - mean) * inverse
 
         @pl.when(segment == 0)
         def _():
             for rows in chunks:
-                outgoing[index, rows, :] = outputs(rows).astype(BF16)
+                outgoing[index, rows, :] = output_rows(rows, lanes).astype(BF16)
             forward_copy(index).start()
 
-        @pl.when(segment == 1)
-        def _():
-            free_ends(index)
-            for start in range(0, width, LANES):
-                rows = slice(start, start + LANES)
-                ends_v[lax.rem(index, 2), :, rows] = outputs(rows).T
-            ends_copy(index).start()
+    def output_rows(rows, lanes):
+        return norm_two[rows, lanes] * column(GAIN_TWO, rows) + column(BIAS_TWO, rows)
+
+    def last_outputs(index, carry):
+        free_ends(index)
+        for start in range(0, width, LANES):
+            rows = slice(start, start + LANES)
+            ends_v[lax.rem(index, 2), :, rows] = output_rows(rows, lanes_of(index)).T
+        ends_copy(index).start()
+        return carry
 
     def attend_back(index, has_off):
         lanes = lanes_of(index)
         slot = jnp.where(index == 0, 1, 0)
         half = LANES // 2
         score_scale = 1.0 / math.sqrt(width // HEADS)
-        blank = jnp.zeros((LANES, LANES), BF16)
+
+        def backs_of(pair):
+            return against(values_rm, index, pair, by_queries(grad_mix[pair]), has_off)
+
+        ahead = backs_of(0)
         for pair in range(pairs):
-            grads = grad_mix[pair]
-            blocks = pair_blocks(grads)
-            back = dot_plain(values_rm[index, pair], blocks)
-            if has_off:
-                back_off = dot_plain(values_rm[0, pair], blocks)
+            backs = ahead
+            if pair + 1 < pairs:
+                ahead = backs_of(pair + 1)
+            results = ([], [], [])
             for head in range(2):
                 rows = slice(head * half, (head + 1) * half)
+                low = share[index, pair, head]
+                low_off = share_off[pair, head] if has_off else None
+                lows = []
                 for part in range(2):
-                    start = head * piece + part * LANES
-                    span = slice(start, start + LANES)
                     place = slice(part * LANES, (part + 1) * LANES)
-                    shares = [share[index, pair, head, place, place].astype(F32)]
-                    backs = [back[place, span]]
+                    wides = [low[place, place]]
                     if part:
-                        shares.append(share[index, pair, head, :LANES, place].astype(F32))
-                        backs.append(back[:LANES, span])
+                        wides.append(low[:LANES, place])
                     if has_off:
-                        for low_half in range(2):
-                            keys = slice(low_half * LANES, (low_half + 1) * LANES)
-                            shares.append(share_off[pair, head, keys, place].astype(F32))
-                            backs.append(back_off[keys, span])
-                    products = [left * right for left, right in zip(shares, backs)]
+                        wides += [low_off[:LANES, place], low_off[LANES:, place]]
+                    wides = [tile.astype(F32) for tile in wides]
+                    tiles = tiles_of(backs, head, part, has_off)
+                    products = [wide * tile for wide, tile in zip(wides, tiles)]
                     inner = jnp.sum(functools.reduce(jnp.add, products), axis=0, keepdims=True)
-                    low = [
-                        (product - left * inner).astype(BF16)
-                        for product, left in zip(products, shares)
-                    ]
-                    score_grad[head, place, place] = low[0]
-                    if part:
-                        score_grad[head, :LANES, place] = low[1]
-                    else:
-                        score_grad[head, LANES:, place] = blank
-                    if has_off:
-                        score_grad[2 + head, :LANES, place] = low[-2]
-                        score_grad[2 + head, LANES:, place] = low[-1]
+                    lows.append(
+                        [
+                            (product - wide * inner).astype(BF16)
+                            for product, wide in zip(products, wides)
+                        ]
+                    )
+                grad_scores, grad_off = joined(lows, has_off)
                 queries = qkv[0, pair, rows, lanes]
-                grad_scores = score_grad[head]
+                grads = grad_mix[pair, rows]
                 grad_query = dot_plain(qkv[1, pair, rows, lanes], grad_scores)
                 grad_key = dot_turned(queries, grad_scores) + key_sums[slot, 0, pair, rows]
-                grad_value = (
-                    dot_turned(grads[rows], share[index, pair, head])
-                    + key_sums[slot, 1, pair, rows]
-                )
+                grad_value = dot_turned(grads, low) + key_sums[slot, 1, pair, rows]
                 if has_off:
-                    grad_off = score_grad[2 + head]
                     grad_query = grad_query + dot_plain(qkv[1, pair, rows, :piece], grad_off)
                     key_sums[1, 0, pair, rows] = dot_turned(queries, grad_off)
-                    key_sums[1, 1, pair, rows] = dot_turned(grads[rows], share_off[pair, head])
-                qkv[0, pair, rows, lanes] = (grad_query * score_scale).astype(BF16)
-                qkv[1, pair, rows, lanes] = grad_key.astype(BF16)
-                qkv[2, pair, rows, lanes] = grad_value.astype(BF16)
+                    key_sums[1, 1, pair, rows] = dot_turned(grads, low_off)
+                for kept, grad in zip(results, (grad_query * score_scale, grad_key, grad_value)):
+                    kept.append(grad.astype(BF16))
+            for block in range(3):
+                qkv[block, pair, :, lanes] = jnp.concatenate(results[block], axis=0)
 
     def backward(index):
         lanes = lanes_of(index)
-
-        @pl.when(segment == 1)
-        def _():
-            incoming_grad[index] = own_rows(index).astype(BF16)
 
         @pl.when(segment == 0)
         def _():
@@ -759,6 +770,11 @@
 
         return carry
 
+    @pl.when(segment == 1)
+    def _():
+        for index in range(PIECES):
+            incoming_grad[index] = own_rows(index).astype(BF16)
+
     lax.fori_loop(0, 2 * PIECES + 1, one_step, 0)
 
     def small_dp_copy(step):
@@ -787,6 +803,10 @@
     after_core(2)
     after_side(0)
     side_copy(2).start()
+
+    @pl.when(segment == 1)
+    def _():
+        lax.fori_loop(0, PIECES, last_outputs, 0)
 
     rows_of = [jnp.sum(sums[index].T, axis=0, keepdims=True) for index in range(STATS)]
     small[...] = jnp.zeros(small.shape, F32)
@@ -895,22 +915,19 @@
     half = ends_in.shape[0] // 2
     share_rows, width = fin.shape[2:]
     start = pl.multiple_of(half * (1 - flag_ref[0, 0]), half)
-    ends_copies = [
-        pltpu.make_async_copy(
-            ends_v.at[pl.ds(0, half)], ends.at[0, pl.ds(start, half)], ends_sem.at[0]
-        ),
-        pltpu.make_async_copy(
-            ends_v.at[pl.ds(half, half)], ends.at[0, pl.ds(half - start, half)], ends_sem.at[1]
-        ),
-    ]
-    ends_loads = [
-        pltpu.make_async_copy(
-            ends_in.at[pl.ds(part * half, half)],
-            ends_v.at[pl.ds(part * half, half)],
-            ends_sem.at[2 + part],
-        )
-        for part in range(2)
-    ]
+    cut = half // 4
+    ends_copies = []
+    ends_loads = []
+    for part in range(8):
+        source = pl.ds(part * cut, cut)
+        offset = start + part * cut if part < 4 else part * cut - half + (half - start)
+        target = pl.ds(pl.multiple_of(offset, cut), cut)
+        ends_loads.append(
+            pltpu.make_async_copy(ends_in.at[source], ends_v.at[source], ends_sem.at[part])
+        )
+        ends_copies.append(
+            pltpu.make_async_copy(ends_v.at[source], ends.at[0, target], ends_sem.at[8 + part])
+        )
     loads = [
         pltpu.make_async_copy(fin.at[group], fin_v.at[group], in_sem.at[group])
         for group in range(3)
@@ -1011,7 +1028,6 @@
             vmem((STATS, width, LANES), BF16),
             vmem((STATS, width, LANES), F32),
             vmem((2, 2, pairs, LANES, piece), F32),
-            vmem((4, piece, piece), BF16),
             vmem((width, piece), F32),
             vmem((width, piece), F32),
             vmem((2, piece, width), F32),
@@ -1023,7 +1039,7 @@
             vmem((dp_count - 1, 16, small_width), F32),
             vmem((4, 16, small_width), F32),
             vmem((16, small_width), F32),
-            dma((8,)),
+            dma((13,)),
             dma((PIECES,)),
             dma((PIECES,)),
             dma((PIECES,)),
@@ -1079,7 +1095,7 @@
             vmem((share_rows, width), F32),
             vmem((share_rows, 4 * width), F32),
             vmem((4 * share_rows, width), F32),
-            dma((4,)),
+            dma((16,)),
             dma((3,)),
             dma((4,)),
         ],

time: 137 us -> 131 us (0.956)
  Pallas kernels: 136 us -> 130 us
    pallas_call x1, Pallas kernels: 131 us -> 124 us  [on_device(): pl.pallas_call(functools.partial(layer_kernel, dp_count), out_shape=(jax....]
where the time goes in v5:
time: 131 us; the launch traced here: 130 us
  Pallas kernels  130 us (99%)
    pallas_call x1, Pallas kernels, on_device(): pl.pallas_call(functools.partial(layer_kernel, dp_count), out_shape=(jax....  124 us
    pallas_call x1, Pallas kernels, on_device(): pl.pallas_call(finish_kernel, out_shape=(jax.ShapeDtypeStruct((1, rows, w...  5.53 us

profile of v5, /device:TPU:0, one launch (start us, length us, event | category | flops | bytes accessed | tf_op | source)
XLA Modules:
  0.0 130.3 jit_solution(2938840351734395217)
XLA Ops:
  0.6 124.0 %shard_map.161 = (f32[4,256,512]{2,1,0:T(8,128)}, bf16[3,4,128,512]{3,2,1,0:T(8,128)(2,1)}, f32[16,128]{1,0:T(8,128)}) custom-call(s32[1,2]{1,0:T(1,128)} %flag_ref.3, bf16[4,256,512]{2,1,0:T(8,128)(2,1)} %bitcast.4, bf16[4,256,512]{2,1,0:T(8,128)(2,1)} %bitcast.5, bf16[1,512,1536]{2,1,0:T(8,128)(2,1)} %w_qkv_hbm.1, bf16[1,512,512]{2,1,0:T(8,128)(2,1)} %w_out_hbm.1, ...), custom_call_target="tpu_custom_call" | custom-call | tf_op jit(solution)/shard_map/pallas_call | solution.py:993
  124.6 5.5 %shard_map.162 = (f32[1,1024,512]{2,1,0:T(8,128)}, f32[1,128,1536]{2,1,0:T(8,128)}, f32[1,128,512]{2,1,0:T(8,128)}, f32[1,128,2048]{2,1,0:T(8,128)}, f32[1,512,5...) custom-call(s32[1,2]{1,0:T(1,128)} %flag_ref.3, f32[1024,512]{1,0:T(8,128)} %bitcast.3, ...), custom_call_target="tpu_custom_call" | custom-call | tf_op jit(solution)/shard_map/pallas_call | solution.py:1077

commit v6 on v5

--- a/solution.py
+++ b/solution.py
@@ -18,6 +18,7 @@
 GAIN_ONE, GAIN_TWO, BIAS_OUT, BIAS_ONE, BIAS_DOWN, BIAS_TWO, BIAS_UP = range(7)
 STATS = 10
 CHUNK = 64
+DP_FIRST = (0, 5)
 
 
 def dot_plain(left, right):
@@ -113,6 +114,7 @@
     piece = x_t.shape[1] // PIECES
     pairs = qkv.shape[1]
     share_rows = width // dp_count
+    dp_steps = dp_count.bit_length() - 1
     segment = lax.axis_index("segment")
     dp = lax.axis_index("dp")
     rep = lax.axis_index("rep")
@@ -578,26 +580,55 @@
     def side_copy(job):
         buffer, base = held(job)
         lanes = lanes_in(job)
+        source = buffer.at[base + 2 * core + (1 - side), :, lanes]
+        target = side_in.at[job // 2, :, lanes]
+        if job in DP_FIRST:
+            source = buffer.at[base + 2 * core + (1 - side), dp_rows(dp_steps - 1)[1], lanes]
+            target = side_in.at[job // 2, pl.ds(0, share_rows), lanes]
         return pltpu.make_async_remote_copy(
-            src_ref=buffer.at[base + 2 * core + (1 - side), :, lanes],
-            dst_ref=side_in.at[job // 2, :, lanes],
+            src_ref=source,
+            dst_ref=target,
             send_sem=side_send.at[job],
             recv_sem=side_recv.at[job],
             device_id={"rep": other_side},
             device_id_type=MESH,
         )
 
+    def dp_slot(job):
+        return (4, 0, 1, 2, 3, 6)[job]
+
+    def dp_rows(step):
+        count = dp_count // 2
+        start = 0
+        for bit in range(step):
+            start = start + lax.rem(lax.div(dp, 2**bit), 2) * count
+            count = count // 2
+        mine = lax.rem(lax.div(dp, 2**step), 2)
+        sent = pl.multiple_of((start + (1 - mine) * count) * share_rows, share_rows)
+        kept = pl.multiple_of((start + mine * count) * share_rows, share_rows)
+        return pl.ds(sent, count * share_rows), pl.ds(kept, count * share_rows)
+
+    def dp_landing(step):
+        count = dp_count // 2 ** (step + 1)
+        return pl.ds((dp_count - 2 * count) * share_rows, count * share_rows)
+
     def dp_copy(job, step):
         buffer, base = held(job)
         lanes = lanes_in(job)
-        target = lax.rem(dp + step, dp_count)
-        rows = pl.ds(pl.multiple_of(target * share_rows, share_rows), share_rows)
+        slot = dp_slot(job)
+        mine = lax.rem(lax.div(dp, 2**step), 2)
+        if job in DP_FIRST:
+            source = buffer.at[pl.ds(base + 2 * core, 2), dp_rows(step)[0], lanes]
+            target = dp_in.at[pl.ds(slot, 2), dp_landing(step)]
+        else:
+            source = buffer.at[base + 2 * core + side, dp_rows(step)[0], lanes]
+            target = dp_in.at[slot, dp_landing(step)]
         return pltpu.make_async_remote_copy(
-            src_ref=buffer.at[base + 2 * core + side, rows, lanes],
-            dst_ref=dp_in.at[job // 2, step - 1, :, lanes],
-            send_sem=dp_send.at[job, step - 1],
-            recv_sem=dp_recv.at[job, step - 1],
-            device_id={"dp": target},
+            src_ref=source,
+            dst_ref=target,
+            send_sem=dp_send.at[job, step],
+            recv_sem=dp_recv.at[job, step],
+            device_id={"dp": dp + (1 - 2 * mine) * 2**step},
             device_id_type=MESH,
         )
 
@@ -627,6 +658,14 @@
         half = job % 2
         return slice(half * (width // 2), (half + 1) * (width // 2))
 
+    def turned_bits(value, count):
+        place = 0
+        while count > 1:
+            place = place * 2 + value % 2
+            value = value // 2
+            count = count // 2
+        return place
+
     def down_sums(job):
         part = 4 * share_rows
         count = width // part
@@ -634,10 +673,12 @@
 
         def one(block, carry):
             result = dot_turned(active[block], down_grad[lanes, :]).astype(BF16)
+            high = lax.rem(block, 2) * 2 + lax.div(block, 2)
             for each in range(count):
+                place = turned_bits(each, count) * 4 + high
+                target = pl.multiple_of(place * share_rows, share_rows)
                 for position in range(4):
                     start = each * part + position * share_rows
-                    target = pl.multiple_of((block * count + each) * share_rows, share_rows)
                     w_down[position, pl.ds(target, share_rows), lanes] = result[
                         start : start + share_rows
                     ]
@@ -645,13 +686,19 @@
 
         lax.fori_loop(0, 4, one, 0)
 
+    def keep_rows(position, lanes, result):
+        for index in range(dp_count):
+            start = turned_bits(index, dp_count) * share_rows
+            turned[position, start : start + share_rows, lanes] = result[
+                index * share_rows : (index + 1) * share_rows
+            ]
+
     def up_sums(job):
         lanes = lanes_in(job)
 
         def one(block, carry):
-            turned[4 + block, :, lanes] = dot_turned(hidden_low[...], slope[block, lanes, :]).astype(
-                BF16
-            )
+            result = dot_turned(hidden_low[...], slope[block, lanes, :]).astype(BF16)
+            keep_rows(4 + block, lanes, result)
             return carry
 
         lax.fori_loop(0, 4, one, 0)
@@ -661,63 +708,94 @@
         half_pairs = slice((job % 2) * (pairs // 2), (job % 2 + 1) * (pairs // 2))
 
         def one(block, carry):
-            turned[block, :, lanes] = dot_turned(
-                x_t[...], qkv[block, half_pairs].reshape(width // 2, PIECES * piece)
-            ).astype(BF16)
+            grads = qkv[block, half_pairs].reshape(width // 2, PIECES * piece)
+            keep_rows(block, lanes, dot_turned(x_t[...], grads).astype(BF16))
             return carry
 
         lax.fori_loop(0, 3, one, 0)
-        turned[3, :, lanes] = dot_turned(
-            mixture[...].reshape(width, PIECES * piece), branch_grad[lanes, :]
-        ).astype(BF16)
+        mixed = mixture[...].reshape(width, PIECES * piece)
+        keep_rows(3, lanes, dot_turned(mixed, branch_grad[lanes, :]).astype(BF16))
 
     def sums_of(job):
         (down_sums, up_sums, qkv_sums)[job // 2](job)
         core_copy(job).start()
 
+    def arrived(copy):
+        copy.wait_send()
+        copy.wait_recv()
+
     def after_core(job):
         buffer, base = held(job)
         lanes = lanes_in(job)
-        copy = core_copy(job)
-        copy.wait_send()
-        copy.wait_recv()
-        first = base + 2 * core + (1 - side)
-        buffer[first, :, lanes] = (
-            buffer[first, :, lanes].astype(F32) + core_in[job // 2, 1 - side, :, lanes].astype(F32)
-        ).astype(BF16)
+        arrived(core_copy(job))
+        for each in range(2):
+            if each == 0 or job in DP_FIRST:
+                place = 1 - side if each == 0 else side
+                position = base + 2 * core + place
+                buffer[position, :, lanes] = (
+                    buffer[position, :, lanes].astype(F32)
+                    + core_in[job // 2, place, :, lanes].astype(F32)
+                ).astype(BF16)
+        if job in DP_FIRST:
+            dp_copy(job, 0).start()
 
     def after_side(job):
         buffer, base = held(job)
         lanes = lanes_in(job)
-        copy = side_copy(job)
-        copy.wait_send()
-        copy.wait_recv()
+        arrived(side_copy(job))
         second = base + 2 * core + side
+        if job in DP_FIRST:
+            rows = dp_rows(dp_steps - 1)[1]
+            total = buffer[second, rows, lanes].astype(F32) + side_in[
+                job // 2, :share_rows, lanes
+            ].astype(F32)
+            fin[job // 2, 2 * core + side, :, lanes] = total.astype(BF16)
+            join_copy(job).start()
+            return
         buffer[second, :, lanes] = (
             buffer[second, :, lanes].astype(F32)
             + core_in[job // 2, side, :, lanes].astype(F32)
             + side_in[job // 2, :, lanes].astype(F32)
         ).astype(BF16)
-        for step in range(1, dp_count):
-            dp_copy(job, step).start()
-
-    def after_dp(job):
+        dp_copy(job, 0).start()
+
+    def dp_total(job, step, each):
         buffer, base = held(job)
         lanes = lanes_in(job)
-        rows = pl.ds(pl.multiple_of(dp * share_rows, share_rows), share_rows)
-        total = buffer[base + 2 * core + side, rows, lanes].astype(F32)
-        for step in range(1, dp_count):
-            copy = dp_copy(job, step)
-            copy.wait_send()
-            copy.wait_recv()
-            total = total + dp_in[job // 2, step - 1, :, lanes].astype(F32)
-        fin[job // 2, 2 * core + side, :, lanes] = total.astype(BF16)
-        join_copy(job).start()
+        position = base + 2 * core + (each if job in DP_FIRST else side)
+        kept = buffer[position, dp_rows(step)[1], lanes].astype(F32)
+        return position, kept + dp_in[dp_slot(job) + each, dp_landing(step), :].astype(F32)
+
+    def dp_parts(job):
+        return range(2) if job in DP_FIRST else range(1)
+
+    def after_dp(job):
+        buffer, _ = held(job)
+        for step in range(dp_steps - 1):
+            arrived(dp_copy(job, step))
+            for each in dp_parts(job):
+                position, total = dp_total(job, step, each)
+                buffer[position, dp_rows(step)[1], lanes_in(job)] = total.astype(BF16)
+            dp_copy(job, step + 1).start()
+
+    def after_last_dp(job):
+        buffer, _ = held(job)
+        lanes = lanes_in(job)
+        step = dp_steps - 1
+        arrived(dp_copy(job, step))
+        for each in dp_parts(job):
+            position, total = dp_total(job, step, each)
+            if job in DP_FIRST:
+                buffer[position, dp_rows(step)[1], lanes] = total.astype(BF16)
+            else:
+                fin[job // 2, 2 * core + side, :, lanes] = total.astype(BF16)
+        if job in DP_FIRST:
+            side_copy(job).start()
+        else:
+            join_copy(job).start()
 
     def after_join(job):
-        copy = join_copy(job)
-        copy.wait_send()
-        copy.wait_recv()
+        arrived(join_copy(job))
         last_copy(job).start()
 
     def fin_copy(job):
@@ -727,20 +805,19 @@
         )
 
     def after_last(job):
-        copy = last_copy(job)
-        copy.wait_send()
-        copy.wait_recv()
+        arrived(last_copy(job))
         fin_copy(job).start()
 
     def early_sums():
         sums_of(0)
         sums_of(1)
         after_core(0)
-        side_copy(0).start()
         sums_of(2)
-        sums_of(3)
         after_core(1)
         side_copy(1).start()
+        sums_of(3)
+        after_core(2)
+        side_copy(2).start()
 
     def one_step(step, carry):
         first_index = jnp.where(step < 4, step, jnp.where(step < 6, 5 - step, step - 4))
@@ -799,10 +876,13 @@
         )
 
     sums_of(4)
+    after_dp(0)
+    after_core(3)
     sums_of(5)
-    after_core(2)
-    after_side(0)
-    side_copy(2).start()
+    after_side(1)
+    side_copy(3).start()
+    after_core(4)
+    after_core(5)
 
     @pl.when(segment == 1)
     def _():
@@ -825,52 +905,47 @@
     for step in range(1, dp_count):
         small_dp_copy(step).start()
 
-
-    after_core(3)
-    after_side(1)
-    side_copy(3).start()
+    after_last_dp(0)
+    after_side(2)
+    side_copy(4).start()
+    after_dp(1)
+    after_side(0)
     small_total = small[dp]
     for step in range(1, dp_count):
-        copy = small_dp_copy(step)
-        copy.wait_send()
-        copy.wait_recv()
+        arrived(small_dp_copy(step))
         small_total = small_total + small_dp[step - 1]
     small_rep[rep] = small_total
     for step in range(1, 4):
         small_rep_copy(step).start()
-    after_core(4)
-    after_dp(0)
-    after_side(2)
-    side_copy(4).start()
-    after_core(5)
-    after_dp(1)
+    after_last_dp(1)
+    after_dp(2)
+    after_dp(5)
     after_join(0)
     after_side(3)
-    side_copy(5).start()
-    after_last(0)
-    after_dp(2)
+    after_last_dp(2)
+    after_last_dp(5)
     after_join(1)
-    after_side(4)
-    after_last(1)
     after_dp(3)
-    after_join(2)
     for step in range(1, 4):
-        copy = small_rep_copy(step)
-        copy.wait_send()
-        copy.wait_recv()
+        arrived(small_rep_copy(step))
     small_out[...] = (small_rep[0] + small_rep[1]) + (small_rep[2] + small_rep[3])
     small_copy = pltpu.make_async_copy(small_out, small_hbm, load_sem.at[0])
     small_copy.start()
+    after_last(0)
+    after_side(4)
+    after_join(2)
+    after_last_dp(3)
     after_side(5)
+    after_last(1)
+    after_dp(4)
     after_last(2)
-    after_dp(4)
     after_join(3)
+    after_join(5)
+    after_last_dp(4)
     after_last(3)
-    after_dp(5)
+    after_last(5)
     after_join(4)
     after_last(4)
-    after_join(5)
-    after_last(5)
 
     for index in range(PIECES):
 
@@ -908,6 +983,10 @@
     wide_out,
     wide_up,
     wide_down,
+    small_v,
+    up_bias_v,
+    gains_v,
+    biases_v,
     ends_sem,
     in_sem,
     out_sem,
@@ -938,6 +1017,14 @@
             ((wide_down, grad_down), (wide_up, grad_up), (wide_qkv, grad_qkv), (wide_out, grad_out))
         )
     ]
+    small_load = pltpu.make_async_copy(small, small_v, in_sem.at[3])
+    small_stores = [
+        pltpu.make_async_copy(narrow, target, out_sem.at[4 + index])
+        for index, (narrow, target) in enumerate(
+            ((up_bias_v, grad_up_bias), (gains_v, grad_gains), (biases_v, grad_biases))
+        )
+    ]
+    small_load.start()
     for copy in loads + ends_loads:
         copy.start()
     for load, copy in zip(ends_loads, ends_copies):
@@ -958,12 +1045,15 @@
     stores[2].start()
     wide_out[...] = fin_v[2, 3].astype(F32)
     stores[3].start()
+    small_load.wait()
     for position in range(4):
         rows = slice(position * share_rows, (position + 1) * share_rows)
-        grad_up_bias[:, rows] = small[BIAS_UP + position : BIAS_UP + position + 1, :share_rows]
-    grad_gains[0] = small[:2, :share_rows]
-    grad_biases[0] = small[2:BIAS_UP, :share_rows]
-    for copy in stores + ends_copies:
+        up_bias_v[:, rows] = small_v[BIAS_UP + position : BIAS_UP + position + 1, :share_rows]
+    gains_v[0] = small_v[:2, :share_rows]
+    biases_v[0] = small_v[2:BIAS_UP, :share_rows]
+    for copy in small_stores:
+        copy.start()
+    for copy in stores + ends_copies + small_stores:
         copy.wait()
 
 
@@ -985,6 +1075,7 @@
     pairs = width // LANES
     share_rows = width // dp_count
     small_width = max(share_rows, LANES)
+    dp_steps = dp_count.bit_length() - 1
     any_spec = pl.BlockSpec(memory_space=pl.ANY)
     vmem_spec = pl.BlockSpec(memory_space=pltpu.VMEM)
     smem_spec = pl.BlockSpec(memory_space=pltpu.SMEM)
@@ -1033,7 +1124,7 @@
             vmem((2, piece, width), F32),
             vmem((3, 2, width, width), BF16),
             vmem((3, width, width), BF16),
-            vmem((3, dp_count - 1, share_rows, width), BF16),
+            vmem((8, width - share_rows, width // 2), BF16),
             vmem((3, 4, share_rows, width), BF16),
             vmem((dp_count, 16, small_width), F32),
             vmem((dp_count - 1, 16, small_width), F32),
@@ -1047,8 +1138,8 @@
             dma((6,)),
             dma((6,)),
             dma((6,)),
-            dma((6, dp_count - 1)),
-            dma((6, dp_count - 1)),
+            dma((6, dp_steps)),
+            dma((6, dp_steps)),
             dma((6,)),
             dma((6,)),
             dma((6,)),
@@ -1086,8 +1177,8 @@
             jax.ShapeDtypeStruct((1, 2, share_rows), F32),
             jax.ShapeDtypeStruct((1, 4, share_rows), F32),
         ),
-        in_specs=[smem_spec, any_spec, any_spec, vmem_spec],
-        out_specs=(any_spec,) * 5 + (vmem_spec,) * 3,
+        in_specs=[smem_spec] + [any_spec] * 3,
+        out_specs=(any_spec,) * 8,
         scratch_shapes=[
             vmem((rows, width), F32),
             vmem((3, 4, share_rows, width), BF16),
@@ -1095,9 +1186,13 @@
             vmem((share_rows, width), F32),
             vmem((share_rows, 4 * width), F32),
             vmem((4 * share_rows, width), F32),
+            vmem((16, small_width), F32),
+            vmem((1, 4 * share_rows), F32),
+            vmem((1, 2, share_rows), F32),
+            vmem((1, 4, share_rows), F32),
             dma((16,)),
-            dma((3,)),
             dma((4,)),
+            dma((7,)),
         ],
         compiler_params=pltpu.CompilerParams(vmem_limit_bytes=63 * 1024 * 1024),
     )(window_group, ends_in.reshape(rows, width), fin, small)

time: 131 us -> 131 us (level)
  no operation moved by 1% of the time
where the time goes in v6:
time: 131 us
  Pallas kernels  130 us (99%)
    pallas_call x1, Pallas kernels, on_device(): pl.pallas_call(functools.partial(layer_kernel, dp_count), out_shape=(jax....  125 us
    pallas_call x1, Pallas kernels, on_device(): pl.pallas_call(finish_kernel, out_shape=(jax.ShapeDtypeStruct((1, rows, w...  5.01 us

profile of v6, /device:TPU:0, one launch (start us, length us, event | category | flops | bytes accessed | tf_op | source)
XLA Modules:
  0.0 130.9 jit_solution(11669210534221627931)
XLA Ops:
  0.6 125.0 %shard_map.161 = (f32[4,256,512]{2,1,0:T(8,128)}, bf16[3,4,128,512]{3,2,1,0:T(8,128)(2,1)}, f32[16,128]{1,0:T(8,128)}) custom-call(s32[1,2]{1,0:T(1,128)} %flag_ref.3, bf16[4,256,512]{2,1,0:T(8,128)(2,1)} %bitcast.4, bf16[4,256,512]{2,1,0:T(8,128)(2,1)} %bitcast.5, bf16[1,512,1536]{2,1,0:T(8,128)(2,1)} %w_qkv_hbm.1, bf16[1,512,512]{2,1,0:T(8,128)(2,1)} %w_out_hbm.1, ...), custom_call_target="tpu_custom_call" | custom-call | tf_op jit(solution)/shard_map/pallas_call | solution.py:1084
  125.7 5.0 %shard_map.162 = (f32[1,1024,512]{2,1,0:T(8,128)}, f32[1,128,1536]{2,1,0:T(8,128)}, f32[1,128,512]{2,1,0:T(8,128)}, f32[1,128,2048]{2,1,0:T(8,128)}, f32[1,512,5...) custom-call(s32[1,2]{1,0:T(1,128)} %flag_ref.3, f32[1024,512]{1,0:T(8,128)} %bitcast.3, ...), custom_call_target="tpu_custom_call" | custom-call | tf_op jit(solution)/shard_map/pallas_call | solution.py:1168

commit v7 on v6

--- a/solution.py
+++ b/solution.py
@@ -565,33 +565,63 @@
         group = job // 2
         return (w_down, 0) if group == 0 else (turned, 4 if group == 1 else 0)
 
+    class Several:
+        def __init__(self, copies):
+            self.copies = copies
+
+        def start(self):
+            for copy in self.copies:
+                copy.start()
+
+        def wait_send(self):
+            for copy in self.copies:
+                copy.wait_send()
+
+        def wait_recv(self):
+            for copy in self.copies:
+                copy.wait_recv()
+
     def core_copy(job):
         buffer, base = held(job)
         lanes = lanes_in(job)
-        return pltpu.make_async_remote_copy(
-            src_ref=buffer.at[pl.ds(base + 2 * (1 - core), 2), :, lanes],
-            dst_ref=core_in.at[job // 2, :, :, lanes],
-            send_sem=core_send.at[job],
-            recv_sem=core_recv.at[job],
-            device_id={"rep": other_core},
-            device_id_type=MESH,
-        )
+        copies = []
+        for part in range(4):
+            rows = pl.ds(part % 2 * (width // 2), width // 2)
+            copies.append(
+                pltpu.make_async_remote_copy(
+                    src_ref=buffer.at[base + 2 * (1 - core) + part // 2, rows, lanes],
+                    dst_ref=core_in.at[job // 2, part // 2, rows, lanes],
+                    send_sem=core_send.at[job, part],
+                    recv_sem=core_recv.at[job, part],
+                    device_id={"rep": other_core},
+                    device_id_type=MESH,
+                )
+            )
+        return Several(copies)
 
     def side_copy(job):
         buffer, base = held(job)
         lanes = lanes_in(job)
-        source = buffer.at[base + 2 * core + (1 - side), :, lanes]
-        target = side_in.at[job // 2, :, lanes]
+        position = base + 2 * core + (1 - side)
+        pairs_of_rows = []
         if job in DP_FIRST:
-            source = buffer.at[base + 2 * core + (1 - side), dp_rows(dp_steps - 1)[1], lanes]
-            target = side_in.at[job // 2, pl.ds(0, share_rows), lanes]
-        return pltpu.make_async_remote_copy(
-            src_ref=source,
-            dst_ref=target,
-            send_sem=side_send.at[job],
-            recv_sem=side_recv.at[job],
-            device_id={"rep": other_side},
-            device_id_type=MESH,
+            pairs_of_rows.append((dp_rows(dp_steps - 1)[1], pl.ds(0, share_rows)))
+        else:
+            for part in range(4):
+                rows = pl.ds(part * (width // 4), width // 4)
+                pairs_of_rows.append((rows, rows))
+        return Several(
+            [
+                pltpu.make_async_remote_copy(
+                    src_ref=buffer.at[position, rows, lanes],
+                    dst_ref=side_in.at[job // 2, target, lanes],
+                    send_sem=side_send.at[job, part],
+                    recv_sem=side_recv.at[job, part],
+                    device_id={"rep": other_side},
+                    device_id_type=MESH,
+                )
+                for part, (rows, target) in enumerate(pairs_of_rows)
+            ]
         )
 
     def dp_slot(job):
@@ -615,22 +645,27 @@
     def dp_copy(job, step):
         buffer, base = held(job)
         lanes = lanes_in(job)
-        slot = dp_slot(job)
         mine = lax.rem(lax.div(dp, 2**step), 2)
-        if job in DP_FIRST:
-            source = buffer.at[pl.ds(base + 2 * core, 2), dp_rows(step)[0], lanes]
-            target = dp_in.at[pl.ds(slot, 2), dp_landing(step)]
-        else:
-            source = buffer.at[base + 2 * core + side, dp_rows(step)[0], lanes]
-            target = dp_in.at[slot, dp_landing(step)]
-        return pltpu.make_async_remote_copy(
-            src_ref=source,
-            dst_ref=target,
-            send_sem=dp_send.at[job, step],
-            recv_sem=dp_recv.at[job, step],
-            device_id={"dp": dp + (1 - 2 * mine) * 2**step},
-            device_id_type=MESH,
-        )
+        return Several(
+            [
+                pltpu.make_async_remote_copy(
+                    src_ref=buffer.at[
+                        base + 2 * core + (each if job in DP_FIRST else side),
+                        dp_rows(step)[0],
+                        lanes,
+                    ],
+                    dst_ref=dp_in.at[dp_slot(job) + each, dp_landing(step)],
+                    send_sem=dp_send.at[job, step, each],
+                    recv_sem=dp_recv.at[job, step, each],
+                    device_id={"dp": dp + (1 - 2 * mine) * 2**step},
+                    device_id_type=MESH,
+                )
+                for each in dp_parts(job)
+            ]
+        )
+
+    def dp_parts(job):
+        return range(2) if job in DP_FIRST else range(1)
 
     def join_copy(job):
         lanes = lanes_in(job)
@@ -765,9 +800,6 @@
         position = base + 2 * core + (each if job in DP_FIRST else side)
         kept = buffer[position, dp_rows(step)[1], lanes].astype(F32)
         return position, kept + dp_in[dp_slot(job) + each, dp_landing(step), :].astype(F32)
-
-    def dp_parts(job):
-        return range(2) if job in DP_FIRST else range(1)
 
     def after_dp(job):
         buffer, _ = held(job)
@@ -1134,12 +1166,12 @@
             dma((PIECES,)),
             dma((PIECES,)),
             dma((PIECES,)),
-            dma((6,)),
-            dma((6,)),
-            dma((6,)),
-            dma((6,)),
-            dma((6, dp_steps)),
-            dma((6, dp_steps)),
+            dma((6, 4)),
+            dma((6, 4)),
+            dma((6, 4)),
+            dma((6, 4)),
+            dma((6, dp_steps, 2)),
+            dma((6, dp_steps, 2)),
             dma((6,)),
             dma((6,)),
             dma((6,)),

time: 131 us -> 132 us (level)
  no operation moved by 1% of the time
where the time goes in v7:
time: 132 us; the launch traced here: 131 us
  Pallas kernels  131 us (99%)
    pallas_call x1, Pallas kernels, on_device(): pl.pallas_call(functools.partial(layer_kernel, dp_count), out_shape=(jax....  126 us
    pallas_call x1, Pallas kernels, on_device(): pl.pallas_call(finish_kernel, out_shape=(jax.ShapeDtypeStruct((1, rows, w...  5.01 us

profile of v7, /device:TPU:0, one launch (start us, length us, event | category | flops | bytes accessed | tf_op | source)
XLA Modules:
  0.0 131.5 jit_solution(8612017465383319621)
XLA Ops:
  0.6 125.7 %shard_map.161 = (f32[4,256,512]{2,1,0:T(8,128)}, bf16[3,4,128,512]{3,2,1,0:T(8,128)(2,1)}, f32[16,128]{1,0:T(8,128)}) custom-call(s32[1,2]{1,0:T(1,128)} %flag_ref.3, bf16[4,256,512]{2,1,0:T(8,128)(2,1)} %bitcast.4, bf16[4,256,512]{2,1,0:T(8,128)(2,1)} %bitcast.5, bf16[1,512,1536]{2,1,0:T(8,128)(2,1)} %w_qkv_hbm.1, bf16[1,512,512]{2,1,0:T(8,128)(2,1)} %w_out_hbm.1, ...), custom_call_target="tpu_custom_call" | custom-call | tf_op jit(solution)/shard_map/pallas_call | solution.py:1116
  126.3 5.0 %shard_map.162 = (f32[1,1024,512]{2,1,0:T(8,128)}, f32[1,128,1536]{2,1,0:T(8,128)}, f32[1,128,512]{2,1,0:T(8,128)}, f32[1,128,2048]{2,1,0:T(8,128)}, f32[1,512,5...) custom-call(s32[1,2]{1,0:T(1,128)} %flag_ref.3, f32[1024,512]{1,0:T(8,128)} %bitcast.3, ...), custom_call_target="tpu_custom_call" | custom-call | tf_op jit(solution)/shard_map/pallas_call | solution.py:1200

commit v8 on v6

--- a/solution.py
+++ b/solution.py
@@ -18,7 +18,26 @@
 GAIN_ONE, GAIN_TWO, BIAS_OUT, BIAS_ONE, BIAS_DOWN, BIAS_TWO, BIAS_UP = range(7)
 STATS = 10
 CHUNK = 64
-DP_FIRST = (0, 5)
+JOBS = 12
+DP_FIRST = (1, 3, 6, 10)
+SUM, CORE, SIDE, SIDED, DP, DPED, JOIN, LAST, SMALL = range(9)
+ORDER_ONE = (
+    (SUM, 0), (SUM, 2),
+)
+ORDER_TWO = (
+    (SUM, 4), (CORE, 1), (CORE, 0), (SIDE, 0), (SUM, 6), (CORE, 2), (SIDE, 2), (CORE, 3),
+)
+ORDER_THREE = (
+    (CORE, 5), (SUM, 8), (SIDE, 5), (CORE, 6), (DP, 3), (CORE, 4), (SUM, 10), (CORE, 7), (SIDE, 4),
+    (SIDED, 5), (SIDED, 2), (SIDE, 7), (DP, 1), (CORE, 8), (CORE, 11), (DPED, 3), (DP, 6), (SIDED, 0),
+    (DP, 2), (DPED, 1), (SIDED, 4), (SIDE, 11), (JOIN, 3), (SIDED, 7), (CORE, 10), (DP, 0), (DP, 5),
+    (CORE, 9), (SMALL, 0), (SIDE, 8), (DP, 4), (SIDE, 9), (SIDED, 11), (DP, 7), (JOIN, 1), (SIDED, 8),
+    (SMALL, 1), (LAST, 1), (DPED, 0), (DP, 10), (DPED, 5), (DPED, 2), (LAST, 3), (SIDED, 9), (DPED, 6),
+    (DP, 8), (JOIN, 0), (DPED, 4), (DPED, 10), (DP, 11), (JOIN, 4), (JOIN, 5), (DP, 9), (JOIN, 2), (LAST, 0),
+    (DPED, 8), (JOIN, 6), (DPED, 7), (DPED, 11), (DPED, 9), (LAST, 4), (JOIN, 10), (JOIN, 7), (JOIN, 11),
+    (JOIN, 8), (JOIN, 9), (SMALL, 2), (LAST, 5), (LAST, 8), (LAST, 2), (LAST, 9), (LAST, 10), (LAST, 11),
+    (LAST, 7), (LAST, 6),
+)
 
 
 def dot_plain(left, right):
@@ -56,7 +75,6 @@
     w_up,
     w_down,
     turned,
-    down_turned,
     rows_in,
     x_t,
     qkv,
@@ -188,7 +206,7 @@
         elif block < 8:
             turned[block] = w_up[:, span].T
         else:
-            down_turned[:, span] = w_down[block - 8].T
+            turned[block] = w_down[block - 8].T
     first_rows.wait()
 
     pl.semaphore_wait(barrier, 4 + dp_count - 1)
@@ -382,19 +400,21 @@
             hidden = normed * column(GAIN_ONE, rows) + column(BIAS_ONE, rows)
             hidden_low[rows, lanes] = hidden.astype(BF16)
 
-        def activate(block, pre_block):
+        branch_two = None
+        for block in range(4):
+            pre_block = dot_plain(turned[4 + block], hidden_low[:, lanes])
+            lows = []
             for rows in chunks:
                 pre = pre_block[rows] + column(BIAS_UP + block, rows)
+                level = (lax.erf(pre * (1.0 / math.sqrt(2.0))) + 1.0) * 0.5
                 bell = jnp.exp2(pre * pre * (-0.5 * math.log2(math.e)))
-                level = (lax.erf(pre * (1.0 / math.sqrt(2.0))) + 1.0) * 0.5
-                active[block, rows, lanes] = (pre * level).astype(BF16)
+                lows.append((pre * level).astype(BF16))
+                active[block, rows, lanes] = lows[-1]
                 slope[block, rows, lanes] = (
                     level + pre * bell * (1.0 / math.sqrt(2.0 * math.pi))
                 ).astype(BF16)
-
-        for block in range(4):
-            activate(block, dot_plain(turned[4 + block], hidden_low[:, lanes]))
-        branch_two = dot_plain(down_turned[...], active[:, :, lanes].reshape(4 * width, piece))
+            part = dot_plain(turned[8 + block], jnp.concatenate(lows, axis=0))
+            branch_two = part if branch_two is None else branch_two + part
         total = jnp.zeros((8, piece), F32)
         for rows in chunks:
             hidden = norm_one[rows, lanes] * column(GAIN_ONE, rows) + column(BIAS_ONE, rows)
@@ -502,6 +522,8 @@
             wide_a[rows, :] = grad_two
             down_grad[rows, lanes] = grad_two.astype(BF16)
 
+    def backward_feed(index):
+        lanes = lanes_of(index)
         for block in range(4):
             back = dot_plain(w_down[block], down_grad[:, lanes])
             for rows in chunks:
@@ -562,40 +584,52 @@
             ends_copy(index).start()
 
     def held(job):
-        group = job // 2
-        return (w_down, 0) if group == 0 else (turned, 4 if group == 1 else 0)
+        return turned, (8, 4, 0)[job // 4]
+
+    def lanes_in(job):
+        start = job % 4 * (width // 4)
+        return slice(start, start + width // 4)
+
+    def parts_of(job):
+        return range(2) if job in DP_FIRST else range(1)
 
     def core_copy(job):
         buffer, base = held(job)
         lanes = lanes_in(job)
         return pltpu.make_async_remote_copy(
             src_ref=buffer.at[pl.ds(base + 2 * (1 - core), 2), :, lanes],
-            dst_ref=core_in.at[job // 2, :, :, lanes],
+            dst_ref=core_in.at[job // 4, :, :, lanes],
             send_sem=core_send.at[job],
             recv_sem=core_recv.at[job],
             device_id={"rep": other_core},
             device_id_type=MESH,
         )
 
-    def side_copy(job):
+    def side_copies(job):
         buffer, base = held(job)
         lanes = lanes_in(job)
-        source = buffer.at[base + 2 * core + (1 - side), :, lanes]
-        target = side_in.at[job // 2, :, lanes]
-        if job in DP_FIRST:
-            source = buffer.at[base + 2 * core + (1 - side), dp_rows(dp_steps - 1)[1], lanes]
-            target = side_in.at[job // 2, pl.ds(0, share_rows), lanes]
-        return pltpu.make_async_remote_copy(
-            src_ref=source,
-            dst_ref=target,
-            send_sem=side_send.at[job],
-            recv_sem=side_recv.at[job],
-            device_id={"rep": other_side},
-            device_id_type=MESH,
-        )
+        copies = []
+        for each in parts_of(job):
+            if job in DP_FIRST:
+                source = buffer.at[base + 2 * core + each, dp_rows(dp_steps - 1)[1], lanes]
+                target = side_in.at[job // 4, pl.ds(each * share_rows, share_rows), lanes]
+            else:
+                source = buffer.at[base + 2 * core + (1 - side), :, lanes]
+                target = side_in.at[job // 4, :, lanes]
+            copies.append(
+                pltpu.make_async_remote_copy(
+                    src_ref=source,
+                    dst_ref=target,
+                    send_sem=side_send.at[job, each],
+                    recv_sem=side_recv.at[job, each],
+                    device_id={"rep": other_side},
+                    device_id_type=MESH,
+                )
+            )
+        return copies
 
     def dp_slot(job):
-        return (4, 0, 1, 2, 3, 6)[job]
+        return sum(len(parts_of(before)) for before in range(job))
 
     def dp_rows(step):
         count = dp_count // 2
@@ -612,31 +646,30 @@
         count = dp_count // 2 ** (step + 1)
         return pl.ds((dp_count - 2 * count) * share_rows, count * share_rows)
 
-    def dp_copy(job, step):
+    def dp_copies(job, step):
         buffer, base = held(job)
         lanes = lanes_in(job)
-        slot = dp_slot(job)
         mine = lax.rem(lax.div(dp, 2**step), 2)
-        if job in DP_FIRST:
-            source = buffer.at[pl.ds(base + 2 * core, 2), dp_rows(step)[0], lanes]
-            target = dp_in.at[pl.ds(slot, 2), dp_landing(step)]
-        else:
-            source = buffer.at[base + 2 * core + side, dp_rows(step)[0], lanes]
-            target = dp_in.at[slot, dp_landing(step)]
-        return pltpu.make_async_remote_copy(
-            src_ref=source,
-            dst_ref=target,
-            send_sem=dp_send.at[job, step],
-            recv_sem=dp_recv.at[job, step],
-            device_id={"dp": dp + (1 - 2 * mine) * 2**step},
-            device_id_type=MESH,
-        )
+        copies = []
+        for each in parts_of(job):
+            position = base + 2 * core + (each if job in DP_FIRST else side)
+            copies.append(
+                pltpu.make_async_remote_copy(
+                    src_ref=buffer.at[position, dp_rows(step)[0], lanes],
+                    dst_ref=dp_in.at[dp_slot(job) + each, dp_landing(step)],
+                    send_sem=dp_send.at[job, step, each],
+                    recv_sem=dp_recv.at[job, step, each],
+                    device_id={"dp": dp + (1 - 2 * mine) * 2**step},
+                    device_id_type=MESH,
+                )
+            )
+        return copies
 
     def join_copy(job):
         lanes = lanes_in(job)
         return pltpu.make_async_remote_copy(
-            src_ref=fin.at[job // 2, 2 * core + side, :, lanes],
-            dst_ref=fin.at[job // 2, 2 * core + side, :, lanes],
+            src_ref=fin.at[job // 4, 2 * core + side, :, lanes],
+            dst_ref=fin.at[job // 4, 2 * core + side, :, lanes],
             send_sem=join_send.at[job],
             recv_sem=join_recv.at[job],
             device_id={"rep": other_side},
@@ -646,17 +679,29 @@
     def last_copy(job):
         lanes = lanes_in(job)
         return pltpu.make_async_remote_copy(
-            src_ref=fin.at[job // 2, pl.ds(2 * core, 2), :, lanes],
-            dst_ref=fin.at[job // 2, pl.ds(2 * core, 2), :, lanes],
+            src_ref=fin.at[job // 4, pl.ds(2 * core, 2), :, lanes],
+            dst_ref=fin.at[job // 4, pl.ds(2 * core, 2), :, lanes],
             send_sem=last_send.at[job],
             recv_sem=last_recv.at[job],
             device_id={"rep": other_core},
             device_id_type=MESH,
         )
 
-    def lanes_in(job):
-        half = job % 2
-        return slice(half * (width // 2), (half + 1) * (width // 2))
+    def fin_copy(job):
+        lanes = lanes_in(job)
+        return pltpu.make_async_copy(
+            fin.at[job // 4, :, :, lanes], fin_hbm.at[job // 4, :, :, lanes], fin_sem.at[job]
+        )
+
+    def arrived(*copies):
+        for copy in copies:
+            copy.wait_send()
+        for copy in copies:
+            copy.wait_recv()
+
+    def start_all(copies):
+        for copy in copies:
+            copy.start()
 
     def turned_bits(value, count):
         place = 0
@@ -666,10 +711,16 @@
             count = count // 2
         return place
 
-    def down_sums(job):
+    def keep_rows(position, lanes, result):
+        for index in range(dp_count):
+            start = turned_bits(index, dp_count) * share_rows
+            turned[position, start : start + share_rows, lanes] = result[
+                index * share_rows : (index + 1) * share_rows
+            ]
+
+    def down_sums(lanes):
         part = 4 * share_rows
         count = width // part
-        lanes = lanes_in(job)
 
         def one(block, carry):
             result = dot_turned(active[block], down_grad[lanes, :]).astype(BF16)
@@ -679,23 +730,14 @@
                 target = pl.multiple_of(place * share_rows, share_rows)
                 for position in range(4):
                     start = each * part + position * share_rows
-                    w_down[position, pl.ds(target, share_rows), lanes] = result[
+                    turned[8 + position, pl.ds(target, share_rows), lanes] = result[
                         start : start + share_rows
                     ]
             return carry
 
         lax.fori_loop(0, 4, one, 0)
 
-    def keep_rows(position, lanes, result):
-        for index in range(dp_count):
-            start = turned_bits(index, dp_count) * share_rows
-            turned[position, start : start + share_rows, lanes] = result[
-                index * share_rows : (index + 1) * share_rows
-            ]
-
-    def up_sums(job):
-        lanes = lanes_in(job)
-
+    def up_sums(lanes):
         def one(block, carry):
             result = dot_turned(hidden_low[...], slope[block, lanes, :]).astype(BF16)
             keep_rows(4 + block, lanes, result)
@@ -703,12 +745,11 @@
 
         lax.fori_loop(0, 4, one, 0)
 
-    def qkv_sums(job):
-        lanes = lanes_in(job)
-        half_pairs = slice((job % 2) * (pairs // 2), (job % 2 + 1) * (pairs // 2))
+    def qkv_sums(lanes):
+        span = slice(lanes.start // LANES, lanes.stop // LANES)
 
         def one(block, carry):
-            grads = qkv[block, half_pairs].reshape(width // 2, PIECES * piece)
+            grads = qkv[block, span].reshape(lanes.stop - lanes.start, PIECES * piece)
             keep_rows(block, lanes, dot_turned(x_t[...], grads).astype(BF16))
             return carry
 
@@ -717,142 +758,88 @@
         keep_rows(3, lanes, dot_turned(mixed, branch_grad[lanes, :]).astype(BF16))
 
     def sums_of(job):
-        (down_sums, up_sums, qkv_sums)[job // 2](job)
+        lanes = slice(lanes_in(job).start, lanes_in(job + 1).stop)
+        (down_sums, up_sums, qkv_sums)[job // 4](lanes)
         core_copy(job).start()
-
-    def arrived(copy):
-        copy.wait_send()
-        copy.wait_recv()
+        core_copy(job + 1).start()
 
     def after_core(job):
         buffer, base = held(job)
         lanes = lanes_in(job)
         arrived(core_copy(job))
-        for each in range(2):
-            if each == 0 or job in DP_FIRST:
-                place = 1 - side if each == 0 else side
-                position = base + 2 * core + place
-                buffer[position, :, lanes] = (
-                    buffer[position, :, lanes].astype(F32)
-                    + core_in[job // 2, place, :, lanes].astype(F32)
-                ).astype(BF16)
+        for each in parts_of(job):
+            place = 1 - side if each == 0 else side
+            position = base + 2 * core + place
+            buffer[position, :, lanes] = (
+                buffer[position, :, lanes].astype(F32)
+                + core_in[job // 4, place, :, lanes].astype(F32)
+            ).astype(BF16)
         if job in DP_FIRST:
-            dp_copy(job, 0).start()
+            start_all(dp_copies(job, 0))
+
+    def start_side(job):
+        start_all(side_copies(job))
 
     def after_side(job):
         buffer, base = held(job)
         lanes = lanes_in(job)
-        arrived(side_copy(job))
+        arrived(*side_copies(job))
         second = base + 2 * core + side
-        if job in DP_FIRST:
-            rows = dp_rows(dp_steps - 1)[1]
-            total = buffer[second, rows, lanes].astype(F32) + side_in[
-                job // 2, :share_rows, lanes
-            ].astype(F32)
-            fin[job // 2, 2 * core + side, :, lanes] = total.astype(BF16)
-            join_copy(job).start()
-            return
         buffer[second, :, lanes] = (
             buffer[second, :, lanes].astype(F32)
-            + core_in[job // 2, side, :, lanes].astype(F32)
-            + side_in[job // 2, :, lanes].astype(F32)
+            + core_in[job // 4, side, :, lanes].astype(F32)
+            + side_in[job // 4, :, lanes].astype(F32)
         ).astype(BF16)
-        dp_copy(job, 0).start()
+        start_all(dp_copies(job, 0))
 
     def dp_total(job, step, each):
         buffer, base = held(job)
-        lanes = lanes_in(job)
         position = base + 2 * core + (each if job in DP_FIRST else side)
-        kept = buffer[position, dp_rows(step)[1], lanes].astype(F32)
+        kept = buffer[position, dp_rows(step)[1], lanes_in(job)].astype(F32)
         return position, kept + dp_in[dp_slot(job) + each, dp_landing(step), :].astype(F32)
-
-    def dp_parts(job):
-        return range(2) if job in DP_FIRST else range(1)
 
     def after_dp(job):
         buffer, _ = held(job)
         for step in range(dp_steps - 1):
-            arrived(dp_copy(job, step))
-            for each in dp_parts(job):
+            arrived(*dp_copies(job, step))
+            for each in parts_of(job):
                 position, total = dp_total(job, step, each)
                 buffer[position, dp_rows(step)[1], lanes_in(job)] = total.astype(BF16)
-            dp_copy(job, step + 1).start()
+            start_all(dp_copies(job, step + 1))
 
     def after_last_dp(job):
         buffer, _ = held(job)
         lanes = lanes_in(job)
         step = dp_steps - 1
-        arrived(dp_copy(job, step))
-        for each in dp_parts(job):
+        arrived(*dp_copies(job, step))
+        for each in parts_of(job):
             position, total = dp_total(job, step, each)
             if job in DP_FIRST:
                 buffer[position, dp_rows(step)[1], lanes] = total.astype(BF16)
             else:
-                fin[job // 2, 2 * core + side, :, lanes] = total.astype(BF16)
+                fin[job // 4, 2 * core + side, :, lanes] = total.astype(BF16)
         if job in DP_FIRST:
-            side_copy(job).start()
+            start_side(job)
         else:
             join_copy(job).start()
 
     def after_join(job):
-        arrived(join_copy(job))
+        if job in DP_FIRST:
+            buffer, base = held(job)
+            lanes = lanes_in(job)
+            arrived(*side_copies(job))
+            for each in range(2):
+                rows = slice(each * share_rows, (each + 1) * share_rows)
+                own = buffer[base + 2 * core + each, dp_rows(dp_steps - 1)[1], lanes]
+                total = own.astype(F32) + side_in[job // 4, rows, lanes].astype(F32)
+                fin[job // 4, 2 * core + each, :, lanes] = total.astype(BF16)
+        else:
+            arrived(join_copy(job))
         last_copy(job).start()
-
-    def fin_copy(job):
-        lanes = lanes_in(job)
-        return pltpu.make_async_copy(
-            fin.at[job // 2, :, :, lanes], fin_hbm.at[job // 2, :, :, lanes], fin_sem.at[job]
-        )
 
     def after_last(job):
         arrived(last_copy(job))
         fin_copy(job).start()
-
-    def early_sums():
-        sums_of(0)
-        sums_of(1)
-        after_core(0)
-        sums_of(2)
-        after_core(1)
-        side_copy(1).start()
-        sums_of(3)
-        after_core(2)
-        side_copy(2).start()
-
-    def one_step(step, carry):
-        first_index = jnp.where(step < 4, step, jnp.where(step < 6, 5 - step, step - 4))
-        last_index = jnp.where(step < 2, step, jnp.where(step < 4, 3 - step, lax.div(step, 2)))
-        first_is = jnp.where(step < 4, 1, 0)
-        last_is = jnp.where(step < 2, 1, jnp.where(step < 4, 0, 1 - lax.rem(step, 2)))
-        index = jnp.minimum(jnp.where(segment == 0, first_index, last_index), PIECES - 1)
-        is_forward = jnp.where(segment == 0, first_is, last_is)
-        is_last = jnp.where(step == 2 * PIECES, 1, 0)
-        is_split = jnp.where(step >= 2 * PIECES - 1, 1 - segment, 0)
-
-        @pl.when(is_forward * (1 - is_last) == 1)
-        def _():
-            forward(index)
-
-        @pl.when(is_forward + is_last == 0)
-        def _():
-            backward(index)
-
-        @pl.when(is_last == 1)
-        def _():
-            early_sums()
-
-        @pl.when((1 - is_forward) * (1 - is_split) * (1 - is_last) + is_last * is_split == 1)
-        def _():
-            backward_attention(index)
-
-        return carry
-
-    @pl.when(segment == 1)
-    def _():
-        for index in range(PIECES):
-            incoming_grad[index] = own_rows(index).astype(BF16)
-
-    lax.fori_loop(0, 2 * PIECES + 1, one_step, 0)
 
     def small_dp_copy(step):
         target = lax.rem(dp + step, dp_count)
@@ -875,77 +862,108 @@
             device_id_type=MESH,
         )
 
-    sums_of(4)
-    after_dp(0)
-    after_core(3)
-    sums_of(5)
-    after_side(1)
-    side_copy(3).start()
-    after_core(4)
-    after_core(5)
+    small_copy = pltpu.make_async_copy(small_out, small_hbm, load_sem.at[0])
+
+    def small_step(stage):
+        if stage == 0:
+            rows_of = [jnp.sum(sums[index].T, axis=0, keepdims=True) for index in range(STATS)]
+            small[...] = jnp.zeros(small.shape, F32)
+            for share_index in range(dp_count):
+                for index in range(BIAS_UP):
+                    start = share_index * share_rows
+                    small[share_index, index : index + 1, :share_rows] = rows_of[index][
+                        :, start : start + share_rows
+                    ]
+                for part in range(4):
+                    start = (share_index * 4 + part) * share_rows
+                    block, start = start // width, start % width
+                    small[share_index, BIAS_UP + part : BIAS_UP + part + 1, :share_rows] = rows_of[
+                        BIAS_UP + block
+                    ][:, start : start + share_rows]
+            for step in range(1, dp_count):
+                small_dp_copy(step).start()
+        elif stage == 1:
+            total = small[dp]
+            for step in range(1, dp_count):
+                arrived(small_dp_copy(step))
+                total = total + small_dp[step - 1]
+            small_rep[rep] = total
+            for step in range(1, 4):
+                small_rep_copy(step).start()
+        else:
+            for step in range(1, 4):
+                arrived(small_rep_copy(step))
+            small_out[...] = (small_rep[0] + small_rep[1]) + (small_rep[2] + small_rep[3])
+            small_copy.start()
+
+    def run(order):
+        steps = (
+            sums_of,
+            after_core,
+            start_side,
+            after_side,
+            after_dp,
+            after_last_dp,
+            after_join,
+            after_last,
+            small_step,
+        )
+        for stage, job in order:
+            steps[stage](job)
+
+    def one_step(step, carry):
+        first_index = jnp.where(step < 4, step, jnp.where(step < 6, 5 - step, step - 4))
+        last_index = jnp.where(step < 2, step, jnp.where(step < 4, 3 - step, lax.div(step, 2)))
+        first_is = jnp.where(step < 4, 1, 0)
+        last_is = jnp.where(step < 2, 1, jnp.where(step < 4, 0, 1 - lax.rem(step, 2)))
+        index = jnp.minimum(jnp.where(segment == 0, first_index, last_index), PIECES - 1)
+        is_last = jnp.where(step == 2 * PIECES, 1, 0)
+        is_forward = jnp.where(segment == 0, first_is, last_is) * (1 - is_last)
+        is_backward = (1 - is_forward) * (1 - is_last)
+        is_split = jnp.where(step >= 2 * PIECES - 1, 1 - segment, 0)
+        is_rest = is_backward * (1 - is_split) + is_last * is_split
+
+        @pl.when(is_forward == 1)
+        def _():
+            forward(index)
+
+        @pl.when(is_backward == 1)
+        def _():
+            backward(index)
+
+        @pl.when(is_last == 1)
+        def _():
+            run(ORDER_ONE)
+
+        @pl.when(is_rest == 1)
+        def _():
+            backward_feed(index)
+
+        @pl.when(is_last == 1)
+        def _():
+            run(ORDER_TWO)
+
+        @pl.when(is_rest == 1)
+        def _():
+            backward_attention(index)
+
+        return carry
+
+    @pl.when(segment == 1)
+    def _():
+        for index in range(PIECES):
+            incoming_grad[index] = own_rows(index).astype(BF16)
+
+    lax.fori_loop(0, 2 * PIECES + 1, one_step, 0)
+
+    cut = ORDER_THREE.index((SMALL, 0))
+    run(ORDER_THREE[:cut])
 
     @pl.when(segment == 1)
     def _():
         lax.fori_loop(0, PIECES, last_outputs, 0)
 
-    rows_of = [jnp.sum(sums[index].T, axis=0, keepdims=True) for index in range(STATS)]
-    small[...] = jnp.zeros(small.shape, F32)
-    for share_index in range(dp_count):
-        for index in range(BIAS_UP):
-            start = share_index * share_rows
-            small[share_index, index : index + 1, :share_rows] = rows_of[index][
-                :, start : start + share_rows
-            ]
-        for part in range(4):
-            start = (share_index * 4 + part) * share_rows
-            block, start = start // width, start % width
-            small[share_index, BIAS_UP + part : BIAS_UP + part + 1, :share_rows] = rows_of[
-                BIAS_UP + block
-            ][:, start : start + share_rows]
-    for step in range(1, dp_count):
-        small_dp_copy(step).start()
-
-    after_last_dp(0)
-    after_side(2)
-    side_copy(4).start()
-    after_dp(1)
-    after_side(0)
-    small_total = small[dp]
-    for step in range(1, dp_count):
-        arrived(small_dp_copy(step))
-        small_total = small_total + small_dp[step - 1]
-    small_rep[rep] = small_total
-    for step in range(1, 4):
-        small_rep_copy(step).start()
-    after_last_dp(1)
-    after_dp(2)
-    after_dp(5)
-    after_join(0)
-    after_side(3)
-    after_last_dp(2)
-    after_last_dp(5)
-    after_join(1)
-    after_dp(3)
-    for step in range(1, 4):
-        arrived(small_rep_copy(step))
-    small_out[...] = (small_rep[0] + small_rep[1]) + (small_rep[2] + small_rep[3])
-    small_copy = pltpu.make_async_copy(small_out, small_hbm, load_sem.at[0])
-    small_copy.start()
-    after_last(0)
-    after_side(4)
-    after_join(2)
-    after_last_dp(3)
-    after_side(5)
-    after_last(1)
-    after_dp(4)
-    after_last(2)
-    after_join(3)
-    after_join(5)
-    after_last_dp(4)
-    after_last(3)
-    after_last(5)
-    after_join(4)
-    after_last(4)
+    run(ORDER_THREE[cut:])
 
     for index in range(PIECES):
 
@@ -959,7 +977,7 @@
 
     for index in range(2, PIECES):
         ends_copy(index).wait()
-    for job in range(6):
+    for job in range(JOBS):
         fin_copy(job).wait()
     small_copy.wait()
 
@@ -1095,8 +1113,7 @@
             vmem((width, width), BF16),
             vmem((width, 4 * width), BF16),
             vmem((4, width, width), BF16),
-            vmem((8, width, width), BF16),
-            vmem((width, 4 * width), BF16),
+            vmem((12, width, width), BF16),
             vmem((PIECES, piece, width), BF16),
             vmem((width, rows), BF16),
             vmem((3, pairs, LANES, rows), BF16),
@@ -1124,7 +1141,7 @@
             vmem((2, piece, width), F32),
             vmem((3, 2, width, width), BF16),
             vmem((3, width, width), BF16),
-            vmem((8, width - share_rows, width // 2), BF16),
+            vmem((JOBS + len(DP_FIRST), width - share_rows, width // 4), BF16),
             vmem((3, 4, share_rows, width), BF16),
             vmem((dp_count, 16, small_width), F32),
             vmem((dp_count - 1, 16, small_width), F32),
@@ -1134,21 +1151,21 @@
             dma((PIECES,)),
             dma((PIECES,)),
             dma((PIECES,)),
-            dma((6,)),
-            dma((6,)),
-            dma((6,)),
-            dma((6,)),
-            dma((6, dp_steps)),
-            dma((6, dp_steps)),
-            dma((6,)),
-            dma((6,)),
-            dma((6,)),
-            dma((6,)),
+            dma((JOBS,)),
+            dma((JOBS,)),
+            dma((JOBS, 2)),
+            dma((JOBS, 2)),
+            dma((JOBS, dp_steps, 2)),
+            dma((JOBS, dp_steps, 2)),
+            dma((JOBS,)),
+            dma((JOBS,)),
+            dma((JOBS,)),
+            dma((JOBS,)),
             dma((dp_count - 1,)),
             dma((dp_count - 1,)),
             dma((3,)),
             dma((3,)),
-            dma((6,)),
+            dma((JOBS,)),
         ],
         compiler_params=pltpu.CompilerParams(
             collective_id=0, has_side_effects=True, vmem_limit_bytes=63 * 1024 * 1024

time: 131 us -> 127 us (0.969)
  Pallas kernels: 130 us -> 125 us
    pallas_call x1, Pallas kernels: 125 us -> 120 us  [on_device(): pl.pallas_call(functools.partial(layer_kernel, dp_count), out_shape=(jax....]
where the time goes in v8:
time: 127 us; the launch traced here: 126 us
  Pallas kernels  125 us (98%)
    pallas_call x1, Pallas kernels, on_device(): pl.pallas_call(functools.partial(layer_kernel, dp_count), out_shape=(jax....  120 us
    pallas_call x1, Pallas kernels, on_device(): pl.pallas_call(finish_kernel, out_shape=(jax.ShapeDtypeStruct((1, rows, w...  5.01 us

profile of v8, /device:TPU:0, one launch (start us, length us, event | category | flops | bytes accessed | tf_op | source)
XLA Modules:
  0.0 126.3 jit_solution(4335375304363795236)
XLA Ops:
  0.6 120.5 %shard_map.161 = (f32[4,256,512]{2,1,0:T(8,128)}, bf16[3,4,128,512]{3,2,1,0:T(8,128)(2,1)}, f32[16,128]{1,0:T(8,128)}) custom-call(s32[1,2]{1,0:T(1,128)} %flag_ref.3, bf16[4,256,512]{2,1,0:T(8,128)(2,1)} %bitcast.4, bf16[4,256,512]{2,1,0:T(8,128)(2,1)} %bitcast.5, bf16[1,512,1536]{2,1,0:T(8,128)(2,1)} %w_qkv_hbm.1, bf16[1,512,512]{2,1,0:T(8,128)(2,1)} %w_out_hbm.1, ...), custom_call_target="tpu_custom_call" | custom-call | tf_op jit(solution)/shard_map/pallas_call | solution.py:1102
  121.1 5.0 %shard_map.162 = (f32[1,1024,512]{2,1,0:T(8,128)}, f32[1,128,1536]{2,1,0:T(8,128)}, f32[1,128,512]{2,1,0:T(8,128)}, f32[1,128,2048]{2,1,0:T(8,128)}, f32[1,512,5...) custom-call(s32[1,2]{1,0:T(1,128)} %flag_ref.3, f32[1024,512]{1,0:T(8,128)} %bitcast.3, ...), custom_call_target="tpu_custom_call" | custom-call | tf_op jit(solution)/shard_map/pallas_call | solution.py:1185

commit v9 on v8

--- a/solution.py
+++ b/solution.py
@@ -18,7 +18,7 @@
 GAIN_ONE, GAIN_TWO, BIAS_OUT, BIAS_ONE, BIAS_DOWN, BIAS_TWO, BIAS_UP = range(7)
 STATS = 10
 CHUNK = 64
-JOBS = 12
+SPLIT = 4
 DP_FIRST = (1, 3, 6, 10)
 SUM, CORE, SIDE, SIDED, DP, DPED, JOIN, LAST, SMALL = range(9)
 ORDER_ONE = (
@@ -38,6 +38,15 @@
     (JOIN, 8), (JOIN, 9), (SMALL, 2), (LAST, 5), (LAST, 8), (LAST, 2), (LAST, 9), (LAST, 10), (LAST, 11),
     (LAST, 7), (LAST, 6),
 )
+
+
+def plain_orders():
+    one = ((SUM, 0),)
+    two = ((SUM, 1), (CORE, 0), (SIDE, 0))
+    three = ((SUM, 2), (CORE, 1), (SIDE, 1), (CORE, 2), (SIDE, 2), (SMALL, 0), (SMALL, 1), (SMALL, 2))
+    for stage in (SIDED, DP, DPED, JOIN, LAST):
+        three += tuple((stage, job) for job in range(3))
+    return one, two, three
 
 
 def dot_plain(left, right):
@@ -583,39 +592,50 @@
                 ends_v[lax.rem(index, 2), :, rows] = (wide_b[rows, :] + through[rows]).T
             ends_copy(index).start()
 
-    def held(job):
-        return turned, (8, 4, 0)[job // 4]
-
-    def lanes_in(job):
-        start = job % 4 * (width // 4)
-        return slice(start, start + width // 4)
+    split = SPLIT if share_rows % (16 * SPLIT) == 0 else 1
+    dp_first = DP_FIRST if split == SPLIT else ()
+    orders = (ORDER_ONE, ORDER_TWO, ORDER_THREE) if split == SPLIT else plain_orders()
+    jobs = 3 * split
+    cut_rows = share_rows // split
+    job_rows = width // split
+
+    def base_of(job):
+        return (8, 4, 0)[job // split]
+
+    def job_span(job):
+        return pl.ds(job % split * job_rows, job_rows)
+
+    def fin_rows(job):
+        return pl.ds(job % split * cut_rows, cut_rows)
 
     def parts_of(job):
-        return range(2) if job in DP_FIRST else range(1)
-
-    def core_copy(job):
-        buffer, base = held(job)
-        lanes = lanes_in(job)
-        return pltpu.make_async_remote_copy(
-            src_ref=buffer.at[pl.ds(base + 2 * (1 - core), 2), :, lanes],
-            dst_ref=core_in.at[job // 4, :, :, lanes],
-            send_sem=core_send.at[job],
-            recv_sem=core_recv.at[job],
-            device_id={"rep": other_core},
-            device_id_type=MESH,
-        )
+        return range(2) if job in dp_first else range(1)
+
+    def core_copies(job):
+        return [
+            pltpu.make_async_remote_copy(
+                src_ref=turned.at[base_of(job) + 2 * (1 - core) + each, job_span(job)],
+                dst_ref=core_in.at[job // split, each, job_span(job)],
+                send_sem=core_send.at[job, each],
+                recv_sem=core_recv.at[job, each],
+                device_id={"rep": other_core},
+                device_id_type=MESH,
+            )
+            for each in range(2)
+        ]
 
     def side_copies(job):
-        buffer, base = held(job)
-        lanes = lanes_in(job)
+        base = base_of(job)
         copies = []
         for each in parts_of(job):
-            if job in DP_FIRST:
-                source = buffer.at[base + 2 * core + each, dp_rows(dp_steps - 1)[1], lanes]
-                target = side_in.at[job // 4, pl.ds(each * share_rows, share_rows), lanes]
+            if job in dp_first:
+                source = turned.at[base + 2 * core + each, dp_rows(job, dp_steps - 1)[1]]
+                target = side_in.at[
+                    job // split, pl.ds(job % split * job_rows + each * cut_rows, cut_rows)
+                ]
             else:
-                source = buffer.at[base + 2 * core + (1 - side), :, lanes]
-                target = side_in.at[job // 4, :, lanes]
+                source = turned.at[base + 2 * core + (1 - side), job_span(job)]
+                target = side_in.at[job // split, job_span(job)]
             copies.append(
                 pltpu.make_async_remote_copy(
                     src_ref=source,
@@ -631,31 +651,30 @@
     def dp_slot(job):
         return sum(len(parts_of(before)) for before in range(job))
 
-    def dp_rows(step):
+    def dp_rows(job, step):
         count = dp_count // 2
         start = 0
         for bit in range(step):
             start = start + lax.rem(lax.div(dp, 2**bit), 2) * count
             count = count // 2
         mine = lax.rem(lax.div(dp, 2**step), 2)
-        sent = pl.multiple_of((start + (1 - mine) * count) * share_rows, share_rows)
-        kept = pl.multiple_of((start + mine * count) * share_rows, share_rows)
-        return pl.ds(sent, count * share_rows), pl.ds(kept, count * share_rows)
+        first = job % split * job_rows
+        sent = pl.multiple_of(first + (start + (1 - mine) * count) * cut_rows, cut_rows)
+        kept = pl.multiple_of(first + (start + mine * count) * cut_rows, cut_rows)
+        return pl.ds(sent, count * cut_rows), pl.ds(kept, count * cut_rows)
 
     def dp_landing(step):
         count = dp_count // 2 ** (step + 1)
-        return pl.ds((dp_count - 2 * count) * share_rows, count * share_rows)
+        return pl.ds((dp_count - 2 * count) * cut_rows, count * cut_rows)
 
     def dp_copies(job, step):
-        buffer, base = held(job)
-        lanes = lanes_in(job)
         mine = lax.rem(lax.div(dp, 2**step), 2)
         copies = []
         for each in parts_of(job):
-            position = base + 2 * core + (each if job in DP_FIRST else side)
+            position = base_of(job) + 2 * core + (each if job in dp_first else side)
             copies.append(
                 pltpu.make_async_remote_copy(
-                    src_ref=buffer.at[position, dp_rows(step)[0], lanes],
+                    src_ref=turned.at[position, dp_rows(job, step)[0]],
                     dst_ref=dp_in.at[dp_slot(job) + each, dp_landing(step)],
                     send_sem=dp_send.at[job, step, each],
                     recv_sem=dp_recv.at[job, step, each],
@@ -666,31 +685,37 @@
         return copies
 
     def join_copy(job):
-        lanes = lanes_in(job)
+        part = fin.at[job // split, 2 * core + side, fin_rows(job)]
         return pltpu.make_async_remote_copy(
-            src_ref=fin.at[job // 4, 2 * core + side, :, lanes],
-            dst_ref=fin.at[job // 4, 2 * core + side, :, lanes],
+            src_ref=part,
+            dst_ref=part,
             send_sem=join_send.at[job],
             recv_sem=join_recv.at[job],
             device_id={"rep": other_side},
             device_id_type=MESH,
         )
 
-    def last_copy(job):
-        lanes = lanes_in(job)
-        return pltpu.make_async_remote_copy(
-            src_ref=fin.at[job // 4, pl.ds(2 * core, 2), :, lanes],
-            dst_ref=fin.at[job // 4, pl.ds(2 * core, 2), :, lanes],
-            send_sem=last_send.at[job],
-            recv_sem=last_recv.at[job],
-            device_id={"rep": other_core},
-            device_id_type=MESH,
-        )
+    def last_copies(job):
+        copies = []
+        for each in range(2):
+            part = fin.at[job // split, 2 * core + each, fin_rows(job)]
+            copies.append(
+                pltpu.make_async_remote_copy(
+                    src_ref=part,
+                    dst_ref=part,
+                    send_sem=last_send.at[job, each],
+                    recv_sem=last_recv.at[job, each],
+                    device_id={"rep": other_core},
+                    device_id_type=MESH,
+                )
+            )
+        return copies
 
     def fin_copy(job):
-        lanes = lanes_in(job)
         return pltpu.make_async_copy(
-            fin.at[job // 4, :, :, lanes], fin_hbm.at[job // 4, :, :, lanes], fin_sem.at[job]
+            fin.at[job // split, :, fin_rows(job)],
+            fin_hbm.at[job // split, :, fin_rows(job)],
+            fin_sem.at[job],
         )
 
     def arrived(*copies):
@@ -711,134 +736,139 @@
             count = count // 2
         return place
 
-    def keep_rows(position, lanes, result):
+    pack = min(2, split)
+
+    def left_rows(source, part):
+        count = pack * cut_rows
+        start = part * pack * cut_rows
+        return jnp.concatenate(
+            [source(index * share_rows + start, count) for index in range(dp_count)], axis=0
+        )
+
+    def keep_rows(block, part, result):
         for index in range(dp_count):
-            start = turned_bits(index, dp_count) * share_rows
-            turned[position, start : start + share_rows, lanes] = result[
-                index * share_rows : (index + 1) * share_rows
-            ]
-
-    def down_sums(lanes):
-        part = 4 * share_rows
-        count = width // part
+            for each in range(pack):
+                target = (part * pack + each) * job_rows + turned_bits(index, dp_count) * cut_rows
+                start = (index * pack + each) * cut_rows
+                turned[block, target : target + cut_rows, :] = result[start : start + cut_rows]
+
+    def down_sums(part):
+        count = width // (4 * share_rows)
 
         def one(block, carry):
-            result = dot_turned(active[block], down_grad[lanes, :]).astype(BF16)
+            pieces = []
+            for each in range(4 * count):
+                start = each * share_rows + part * pack * cut_rows
+                pieces.append(active[block, start : start + pack * cut_rows, :])
+            result = dot_turned(jnp.concatenate(pieces, axis=0), down_grad[...]).astype(BF16)
             high = lax.rem(block, 2) * 2 + lax.div(block, 2)
             for each in range(count):
                 place = turned_bits(each, count) * 4 + high
-                target = pl.multiple_of(place * share_rows, share_rows)
                 for position in range(4):
-                    start = each * part + position * share_rows
-                    turned[8 + position, pl.ds(target, share_rows), lanes] = result[
-                        start : start + share_rows
-                    ]
+                    for job in range(pack):
+                        target = (part * pack + job) * job_rows + place * cut_rows
+                        start = ((each * 4 + position) * pack + job) * cut_rows
+                        turned[
+                            8 + position, pl.ds(pl.multiple_of(target, cut_rows), cut_rows), :
+                        ] = result[start : start + cut_rows]
             return carry
 
         lax.fori_loop(0, 4, one, 0)
 
-    def up_sums(lanes):
+    def up_sums(part):
         def one(block, carry):
-            result = dot_turned(hidden_low[...], slope[block, lanes, :]).astype(BF16)
-            keep_rows(4 + block, lanes, result)
+            left = left_rows(lambda start, count: hidden_low[start : start + count, :], part)
+            keep_rows(4 + block, part, dot_turned(left, slope[block]).astype(BF16))
             return carry
 
         lax.fori_loop(0, 4, one, 0)
 
-    def qkv_sums(lanes):
-        span = slice(lanes.start // LANES, lanes.stop // LANES)
-
+    def qkv_sums(part):
         def one(block, carry):
-            grads = qkv[block, span].reshape(lanes.stop - lanes.start, PIECES * piece)
-            keep_rows(block, lanes, dot_turned(x_t[...], grads).astype(BF16))
+            left = left_rows(lambda start, count: x_t[start : start + count, :], part)
+            grads = qkv[block].reshape(width, PIECES * piece)
+            keep_rows(block, part, dot_turned(left, grads).astype(BF16))
             return carry
 
         lax.fori_loop(0, 3, one, 0)
-        mixed = mixture[...].reshape(width, PIECES * piece)
-        keep_rows(3, lanes, dot_turned(mixed, branch_grad[lanes, :]).astype(BF16))
+        left = left_rows(
+            lambda start, count: mixture[start // LANES, start % LANES : start % LANES + count, :], part
+        )
+        keep_rows(3, part, dot_turned(left, branch_grad[...]).astype(BF16))
 
     def sums_of(job):
-        lanes = slice(lanes_in(job).start, lanes_in(job + 1).stop)
-        (down_sums, up_sums, qkv_sums)[job // 4](lanes)
-        core_copy(job).start()
-        core_copy(job + 1).start()
+        (down_sums, up_sums, qkv_sums)[job // split](job % split // pack)
+        for each in range(pack):
+            start_all(core_copies(job + each))
 
     def after_core(job):
-        buffer, base = held(job)
-        lanes = lanes_in(job)
-        arrived(core_copy(job))
+        arrived(*core_copies(job))
+        rows = job_span(job)
         for each in parts_of(job):
             place = 1 - side if each == 0 else side
-            position = base + 2 * core + place
-            buffer[position, :, lanes] = (
-                buffer[position, :, lanes].astype(F32)
-                + core_in[job // 4, place, :, lanes].astype(F32)
+            position = base_of(job) + 2 * core + place
+            turned[position, rows, :] = (
+                turned[position, rows, :].astype(F32)
+                + core_in[job // split, place, rows, :].astype(F32)
             ).astype(BF16)
-        if job in DP_FIRST:
+        if job in dp_first:
             start_all(dp_copies(job, 0))
 
     def start_side(job):
         start_all(side_copies(job))
 
     def after_side(job):
-        buffer, base = held(job)
-        lanes = lanes_in(job)
         arrived(*side_copies(job))
-        second = base + 2 * core + side
-        buffer[second, :, lanes] = (
-            buffer[second, :, lanes].astype(F32)
-            + core_in[job // 4, side, :, lanes].astype(F32)
-            + side_in[job // 4, :, lanes].astype(F32)
+        rows = job_span(job)
+        position = base_of(job) + 2 * core + side
+        turned[position, rows, :] = (
+            turned[position, rows, :].astype(F32)
+            + core_in[job // split, side, rows, :].astype(F32)
+            + side_in[job // split, rows, :].astype(F32)
         ).astype(BF16)
         start_all(dp_copies(job, 0))
 
     def dp_total(job, step, each):
-        buffer, base = held(job)
-        position = base + 2 * core + (each if job in DP_FIRST else side)
-        kept = buffer[position, dp_rows(step)[1], lanes_in(job)].astype(F32)
+        position = base_of(job) + 2 * core + (each if job in dp_first else side)
+        kept = turned[position, dp_rows(job, step)[1], :].astype(F32)
         return position, kept + dp_in[dp_slot(job) + each, dp_landing(step), :].astype(F32)
 
     def after_dp(job):
-        buffer, _ = held(job)
         for step in range(dp_steps - 1):
             arrived(*dp_copies(job, step))
             for each in parts_of(job):
                 position, total = dp_total(job, step, each)
-                buffer[position, dp_rows(step)[1], lanes_in(job)] = total.astype(BF16)
+                turned[position, dp_rows(job, step)[1], :] = total.astype(BF16)
             start_all(dp_copies(job, step + 1))
 
     def after_last_dp(job):
-        buffer, _ = held(job)
-        lanes = lanes_in(job)
         step = dp_steps - 1
         arrived(*dp_copies(job, step))
         for each in parts_of(job):
             position, total = dp_total(job, step, each)
-            if job in DP_FIRST:
-                buffer[position, dp_rows(step)[1], lanes] = total.astype(BF16)
+            if job in dp_first:
+                turned[position, dp_rows(job, step)[1], :] = total.astype(BF16)
             else:
-                fin[job // 4, 2 * core + side, :, lanes] = total.astype(BF16)
-        if job in DP_FIRST:
+                fin[job // split, 2 * core + side, fin_rows(job), :] = total.astype(BF16)
+        if job in dp_first:
             start_side(job)
         else:
             join_copy(job).start()
 
     def after_join(job):
-        if job in DP_FIRST:
-            buffer, base = held(job)
-            lanes = lanes_in(job)
+        if job in dp_first:
             arrived(*side_copies(job))
             for each in range(2):
-                rows = slice(each * share_rows, (each + 1) * share_rows)
-                own = buffer[base + 2 * core + each, dp_rows(dp_steps - 1)[1], lanes]
-                total = own.astype(F32) + side_in[job // 4, rows, lanes].astype(F32)
-                fin[job // 4, 2 * core + each, :, lanes] = total.astype(BF16)
+                rows = pl.ds(job % split * job_rows + each * cut_rows, cut_rows)
+                own = turned[base_of(job) + 2 * core + each, dp_rows(job, dp_steps - 1)[1], :]
+                total = own.astype(F32) + side_in[job // split, rows, :].astype(F32)
+                fin[job // split, 2 * core + each, fin_rows(job), :] = total.astype(BF16)
         else:
             arrived(join_copy(job))
-        last_copy(job).start()
+        start_all(last_copies(job))
 
     def after_last(job):
-        arrived(last_copy(job))
+        arrived(*last_copies(job))
         fin_copy(job).start()
 
     def small_dp_copy(step):
@@ -933,7 +963,7 @@
 
         @pl.when(is_last == 1)
         def _():
-            run(ORDER_ONE)
+            run(orders[0])
 
         @pl.when(is_rest == 1)
         def _():
@@ -941,7 +971,7 @@
 
         @pl.when(is_last == 1)
         def _():
-            run(ORDER_TWO)
+            run(orders[1])
 
         @pl.when(is_rest == 1)
         def _():
@@ -956,14 +986,14 @@
 
     lax.fori_loop(0, 2 * PIECES + 1, one_step, 0)
 
-    cut = ORDER_THREE.index((SMALL, 0))
-    run(ORDER_THREE[:cut])
+    cut = orders[2].index((SMALL, 0))
+    run(orders[2][:cut])
 
     @pl.when(segment == 1)
     def _():
         lax.fori_loop(0, PIECES, last_outputs, 0)
 
-    run(ORDER_THREE[cut:])
+    run(orders[2][cut:])
 
     for index in range(PIECES):
 
@@ -977,7 +1007,7 @@
 
     for index in range(2, PIECES):
         ends_copy(index).wait()
-    for job in range(JOBS):
+    for job in range(jobs):
         fin_copy(job).wait()
     small_copy.wait()
 
@@ -1094,6 +1124,9 @@
     share_rows = width // dp_count
     small_width = max(share_rows, LANES)
     dp_steps = dp_count.bit_length() - 1
+    split = SPLIT if share_rows % (16 * SPLIT) == 0 else 1
+    jobs = 3 * split
+    slots = jobs + (len(DP_FIRST) if split == SPLIT else 0)
     any_spec = pl.BlockSpec(memory_space=pl.ANY)
     vmem_spec = pl.BlockSpec(memory_space=pltpu.VMEM)
     smem_spec = pl.BlockSpec(memory_space=pltpu.SMEM)
@@ -1141,7 +1174,7 @@
             vmem((2, piece, width), F32),
             vmem((3, 2, width, width), BF16),
             vmem((3, width, width), BF16),
-            vmem((JOBS + len(DP_FIRST), width - share_rows, width // 4), BF16),
+            vmem((slots, (width - share_rows) // split, width), BF16),
             vmem((3, 4, share_rows, width), BF16),
             vmem((dp_count, 16, small_width), F32),
             vmem((dp_count - 1, 16, small_width), F32),
@@ -1151,21 +1184,21 @@
             dma((PIECES,)),
             dma((PIECES,)),
             dma((PIECES,)),
-            dma((JOBS,)),
-            dma((JOBS,)),
-            dma((JOBS, 2)),
-            dma((JOBS, 2)),
-            dma((JOBS, dp_steps, 2)),
-            dma((JOBS, dp_steps, 2)),
-            dma((JOBS,)),
-            dma((JOBS,)),
-            dma((JOBS,)),
-            dma((JOBS,)),
+            dma((jobs, 2)),
+            dma((jobs, 2)),
+            dma((jobs, 2)),
+            dma((jobs, 2)),
+            dma((jobs, dp_steps, 2)),
+            dma((jobs, dp_steps, 2)),
+            dma((jobs,)),
+            dma((jobs,)),
+            dma((jobs, 2)),
+            dma((jobs, 2)),
             dma((dp_count - 1,)),
             dma((dp_count - 1,)),
             dma((3,)),
             dma((3,)),
-            dma((JOBS,)),
+            dma((jobs,)),
         ],
         compiler_params=pltpu.CompilerParams(
             collective_id=0, has_side_effects=True, vmem_limit_bytes=63 * 1024 * 1024

time: 127 us -> 127 us (level)
  no operation moved by 1% of the time
where the time goes in v9:
time: 127 us; the launch traced here: 126 us
  Pallas kernels  126 us (99%)
    pallas_call x1, Pallas kernels, on_device(): pl.pallas_call(functools.partial(layer_kernel, dp_count), out_shape=(jax....  121 us
    pallas_call x1, Pallas kernels, on_device(): pl.pallas_call(finish_kernel, out_shape=(jax.ShapeDtypeStruct((1, rows, w...  5.01 us

profile of v9, /device:TPU:0, one launch (start us, length us, event | category | flops | bytes accessed | tf_op | source)
XLA Modules:
  0.0 126.3 jit_solution(3309985499522195409)
XLA Ops:
  0.6 120.5 %shard_map.161 = (f32[4,256,512]{2,1,0:T(8,128)}, bf16[3,4,128,512]{3,2,1,0:T(8,128)(2,1)}, f32[16,128]{1,0:T(8,128)}) custom-call(s32[1,2]{1,0:T(1,128)} %flag_ref.3, bf16[4,256,512]{2,1,0:T(8,128)(2,1)} %bitcast.4, bf16[4,256,512]{2,1,0:T(8,128)(2,1)} %bitcast.5, bf16[1,512,1536]{2,1,0:T(8,128)(2,1)} %w_qkv_hbm.1, bf16[1,512,512]{2,1,0:T(8,128)(2,1)} %w_out_hbm.1, ...), custom_call_target="tpu_custom_call" | custom-call | tf_op jit(solution)/shard_map/pallas_call | solution.py:1135
  121.2 5.0 %shard_map.162 = (f32[1,1024,512]{2,1,0:T(8,128)}, f32[1,128,1536]{2,1,0:T(8,128)}, f32[1,128,512]{2,1,0:T(8,128)}, f32[1,128,2048]{2,1,0:T(8,128)}, f32[1,512,5...) custom-call(s32[1,2]{1,0:T(1,128)} %flag_ref.3, f32[1024,512]{1,0:T(8,128)} %bitcast.3, ...), custom_call_target="tpu_custom_call" | custom-call | tf_op jit(solution)/shard_map/pallas_call | solution.py:1218

commit v10 on v9

--- a/solution.py
+++ b/solution.py
@@ -51,6 +51,23 @@
 
 def dot_plain(left, right):
     return lax.dot_general(left, right, (((1,), (0,)), ((), ())), preferred_element_type=F32)
+
+
+def drain(parts):
+    for _ in parts:
+        pass
+
+
+def side_by_side(one, two):
+    spent = [0, 300]
+    live = [one, two]
+    while live[0] or live[1]:
+        which = 0 if live[0] and (not live[1] or spent[0] <= spent[1]) else 1
+        cost = next(live[which], None)
+        if cost is None:
+            live[which] = None
+        else:
+            spent[which] += cost
 
 
 def dot_turned(left, right):
@@ -108,6 +125,7 @@
     key_sums,
     wide_a,
     wide_b,
+    wide_c,
     ends_v,
     core_in,
     side_in,
@@ -223,6 +241,8 @@
     flag = flag_ref[0, 0].astype(F32)
 
     def lanes_of(index):
+        if isinstance(index, int):
+            return pl.ds(index * piece, piece)
         return pl.ds(pl.multiple_of(index * piece, piece), piece)
 
     def forward_copy(index):
@@ -340,6 +360,7 @@
                     mix = mix + dot_plain(qkv[2, pair, rows, :piece], low_off)
                 mixed.append(mix.astype(BF16))
             mixture[pair, :, lanes] = jnp.concatenate(mixed, axis=0)
+            yield 280
 
     def part_sum(values):
         return jnp.sum(values.reshape(values.shape[0] // 8, 8, values.shape[1]), axis=0)
@@ -354,7 +375,7 @@
     def gather_sum(index, rows, values):
         sums[index, rows, :] = sums[index, rows, :] + fold(values)
 
-    def norm_chunks(index, which, total):
+    def norm_chunks(index, which, wide_a, total):
         mean = full_mean(total)
         spread = jnp.zeros((8, piece), F32)
         for rows in chunks:
@@ -364,17 +385,17 @@
         inverses[index, which] = inverse
         return mean, inverse
 
-    def forward(index):
+    def forward_start(index):
+        @pl.when(segment == 0)
+        def _():
+            x_t[:, lanes_of(index)] = own_rows(index).astype(BF16)
+
+        @pl.when(segment == 1)
+        def _():
+            forward_copy(index).wait_recv()
+
+    def forward_first(index):
         lanes = lanes_of(index)
-
-        @pl.when(segment == 0)
-        def _():
-            x_t[:, lanes] = own_rows(index).astype(BF16)
-
-        @pl.when(segment == 1)
-        def _():
-            forward_copy(index).wait_recv()
-
         inputs = x_t[:, lanes]
         score_scale = 1.0 / math.sqrt(width // HEADS)
         for block in range(3):
@@ -387,31 +408,31 @@
                     keys_rm[index, pair] = low.T
                 if block == 2:
                     values_rm[index, pair] = low.T
-
-        @pl.when(index == 1)
-        def _():
-            attend(index, True)
-
-        @pl.when(index != 1)
-        def _():
-            attend(index, False)
-
+            yield 270
+
+    def forward_rest(index, wide_a):
+        lanes = lanes_of(index)
         branch = dot_plain(turned[3], mixture[:, :, lanes].reshape(width, piece))
+        yield 250
         total = jnp.zeros((8, piece), F32)
         for rows in chunks:
             sum_one = x_t[rows, lanes].astype(F32) + (branch[rows] + column(BIAS_OUT, rows))
             wide_a[rows, :] = sum_one
             total = total + part_sum(sum_one)
-        mean, inverse = norm_chunks(index, 0, total)
+            yield 25
+        mean, inverse = norm_chunks(index, 0, wide_a, total)
+        yield 150
         for rows in chunks:
             normed = (wide_a[rows, :] - mean) * inverse
             norm_one[rows, lanes] = normed
             hidden = normed * column(GAIN_ONE, rows) + column(BIAS_ONE, rows)
             hidden_low[rows, lanes] = hidden.astype(BF16)
+            yield 30
 
         branch_two = None
         for block in range(4):
             pre_block = dot_plain(turned[4 + block], hidden_low[:, lanes])
+            yield 50
             lows = []
             for rows in chunks:
                 pre = pre_block[rows] + column(BIAS_UP + block, rows)
@@ -422,24 +443,45 @@
                 slope[block, rows, lanes] = (
                     level + pre * bell * (1.0 / math.sqrt(2.0 * math.pi))
                 ).astype(BF16)
+                yield 65
             part = dot_plain(turned[8 + block], jnp.concatenate(lows, axis=0))
             branch_two = part if branch_two is None else branch_two + part
+            yield 100
         total = jnp.zeros((8, piece), F32)
         for rows in chunks:
             hidden = norm_one[rows, lanes] * column(GAIN_ONE, rows) + column(BIAS_ONE, rows)
             sum_two = hidden + (branch_two[rows] + column(BIAS_DOWN, rows))
             wide_a[rows, :] = sum_two
             total = total + part_sum(sum_two)
-        mean, inverse = norm_chunks(index, 1, total)
-
+            yield 25
+        mean, inverse = norm_chunks(index, 1, wide_a, total)
+        yield 150
         for rows in chunks:
             norm_two[rows, lanes] = (wide_a[rows, :] - mean) * inverse
-
+            yield 20
+
+    def forward_end(index):
         @pl.when(segment == 0)
         def _():
             for rows in chunks:
-                outgoing[index, rows, :] = output_rows(rows, lanes).astype(BF16)
+                outgoing[index, rows, :] = output_rows(rows, lanes_of(index)).astype(BF16)
             forward_copy(index).start()
+
+    def off_or_not(index, run):
+        @pl.when(index == 1)
+        def _():
+            drain(run(index, True))
+
+        @pl.when(index != 1)
+        def _():
+            drain(run(index, False))
+
+    def forward(index):
+        forward_start(index)
+        drain(forward_first(index))
+        off_or_not(index, attend)
+        drain(forward_rest(index, wide_a))
+        forward_end(index)
 
     def output_rows(rows, lanes):
         return norm_two[rows, lanes] * column(GAIN_TWO, rows) + column(BIAS_TWO, rows)
@@ -454,7 +496,7 @@
 
     def attend_back(index, has_off):
         lanes = lanes_of(index)
-        slot = jnp.where(index == 0, 1, 0)
+        slot = (1 if index == 0 else 0) if isinstance(index, int) else jnp.where(index == 0, 1, 0)
         half = LANES // 2
         score_scale = 1.0 / math.sqrt(width // HEADS)
 
@@ -503,14 +545,15 @@
                     kept.append(grad.astype(BF16))
             for block in range(3):
                 qkv[block, pair, :, lanes] = jnp.concatenate(results[block], axis=0)
-
-    def backward(index):
+            yield 440
+
+    def backward_start(index):
+        @pl.when(segment == 0)
+        def _():
+            backward_copy(index).wait_recv()
+
+    def backward_norm(index):
         lanes = lanes_of(index)
-
-        @pl.when(segment == 0)
-        def _():
-            backward_copy(index).wait_recv()
-
         plain = jnp.zeros((8, piece), F32)
         inner = jnp.zeros((8, piece), F32)
         for rows in chunks:
@@ -521,6 +564,7 @@
             gain = column(GAIN_TWO, rows)
             plain = plain + part_sum(grad * gain)
             inner = inner + part_sum(product * gain)
+            yield 40
         plain = full_mean(plain)
         inner = full_mean(inner)
         inverse = inverses[index, 1]
@@ -530,6 +574,7 @@
             gather_sum(BIAS_DOWN, rows, grad_two)
             wide_a[rows, :] = grad_two
             down_grad[rows, lanes] = grad_two.astype(BF16)
+            yield 40
 
     def backward_feed(index):
         lanes = lanes_of(index)
@@ -539,6 +584,7 @@
                 grad_pre = back[rows] * slope[block, rows, lanes].astype(F32)
                 gather_sum(BIAS_UP + block, rows, grad_pre)
                 slope[block, rows, lanes] = grad_pre.astype(BF16)
+            yield 250
 
         through = dot_plain(w_up[...], slope[:, :, lanes].reshape(4 * width, piece))
         plain = jnp.zeros((8, piece), F32)
@@ -552,6 +598,7 @@
             gain = column(GAIN_ONE, rows)
             plain = plain + part_sum(grad_hidden * gain)
             inner = inner + part_sum(product * gain)
+            yield 120 if rows.start == 0 else 45
         plain = full_mean(plain)
         inner = full_mean(inner)
         inverse = inverses[index, 0]
@@ -561,22 +608,15 @@
             gather_sum(BIAS_OUT, rows, grad_one)
             wide_b[rows, :] = grad_one
             branch_grad[rows, lanes] = grad_one.astype(BF16)
+            yield 40
         grad_mix[...] = (
             dot_plain(w_out[...], branch_grad[:, lanes]).astype(BF16).reshape(pairs, LANES, piece)
         )
+        yield 300
 
     def backward_attention(index):
-        lanes = lanes_of(index)
-
-        @pl.when(index == 1)
-        def _():
-            attend_back(index, True)
-
-        @pl.when(index != 1)
-        def _():
-            attend_back(index, False)
-
-        through = dot_plain(w_qkv[...], qkv[:, :, :, lanes].reshape(3 * width, piece))
+        off_or_not(index, attend_back)
+        through = dot_plain(w_qkv[...], qkv[:, :, :, lanes_of(index)].reshape(3 * width, piece))
 
         @pl.when(segment == 1)
         def _():
@@ -591,6 +631,26 @@
                 rows = slice(start, start + LANES)
                 ends_v[lax.rem(index, 2), :, rows] = (wide_b[rows, :] + through[rows]).T
             ends_copy(index).start()
+
+    def backward_both(index, forward_index):
+        forward_copy(forward_index).wait_recv()
+
+        def back():
+            yield from backward_norm(index)
+            yield from backward_feed(index)
+            yield from attend_back(index, False)
+            through = dot_plain(w_qkv[...], qkv[:, :, :, lanes_of(index)].reshape(3 * width, piece))
+            for rows in chunks:
+                outgoing[index, rows, :] = (wide_b[rows, :] + through[rows]).astype(BF16)
+                yield 90
+
+        def ahead():
+            yield from forward_first(forward_index)
+            yield from attend(forward_index, False)
+            yield from forward_rest(forward_index, wide_c)
+
+        side_by_side(back(), ahead())
+        backward_copy(index).start()
 
     split = SPLIT if share_rows % (16 * SPLIT) == 0 else 1
     dp_first = DP_FIRST if split == SPLIT else ()
@@ -943,13 +1003,12 @@
 
     def one_step(step, carry):
         first_index = jnp.where(step < 4, step, jnp.where(step < 6, 5 - step, step - 4))
-        last_index = jnp.where(step < 2, step, jnp.where(step < 4, 3 - step, lax.div(step, 2)))
-        first_is = jnp.where(step < 4, 1, 0)
-        last_is = jnp.where(step < 2, 1, jnp.where(step < 4, 0, 1 - lax.rem(step, 2)))
+        last_index = jnp.where(step < 2, step, jnp.where(step == 2, 1, 3))
         index = jnp.minimum(jnp.where(segment == 0, first_index, last_index), PIECES - 1)
         is_last = jnp.where(step == 2 * PIECES, 1, 0)
-        is_forward = jnp.where(segment == 0, first_is, last_is) * (1 - is_last)
-        is_backward = (1 - is_forward) * (1 - is_last)
+        is_forward = jnp.where(step < jnp.where(segment == 0, 4, 2), 1, 0)
+        last_backward = jnp.where(step == 2, 1, 0) + jnp.where(step == 5, 1, 0)
+        is_backward = jnp.where(segment == 0, (1 - is_forward) * (1 - is_last), last_backward)
         is_split = jnp.where(step >= 2 * PIECES - 1, 1 - segment, 0)
         is_rest = is_backward * (1 - is_split) + is_last * is_split
 
@@ -959,7 +1018,16 @@
 
         @pl.when(is_backward == 1)
         def _():
-            backward(index)
+            backward_start(index)
+            drain(backward_norm(index))
+
+        @pl.when(segment * step == 3)
+        def _():
+            backward_both(0, 2)
+
+        @pl.when(segment * step == 4)
+        def _():
+            backward_both(2, 3)
 
         @pl.when(is_last == 1)
         def _():
@@ -967,7 +1035,7 @@
 
         @pl.when(is_rest == 1)
         def _():
-            backward_feed(index)
+            drain(backward_feed(index))
 
         @pl.when(is_last == 1)
         def _():
@@ -1169,6 +1237,7 @@
             vmem((STATS, width, LANES), BF16),
             vmem((STATS, width, LANES), F32),
             vmem((2, 2, pairs, LANES, piece), F32),
+            vmem((width, piece), F32),
             vmem((width, piece), F32),
             vmem((width, piece), F32),
             vmem((2, piece, width), F32),

time: 127 us -> 123 us (0.969)
  Pallas kernels: 126 us -> 122 us
    pallas_call x1, Pallas kernels: 121 us -> 117 us  [on_device(): pl.pallas_call(functools.partial(layer_kernel, dp_count), out_shape=(jax....]
where the time goes in v10:
time: 123 us
  Pallas kernels  122 us (99%)
    pallas_call x1, Pallas kernels, on_device(): pl.pallas_call(functools.partial(layer_kernel, dp_count), out_shape=(jax....  117 us
    pallas_call x1, Pallas kernels, on_device(): pl.pallas_call(finish_kernel, out_shape=(jax.ShapeDtypeStruct((1, rows, w...  5.01 us

profile of v10, /device:TPU:0, one launch (start us, length us, event | category | flops | bytes accessed | tf_op | source)
XLA Modules:
  0.0 123.3 jit_solution(13231556488629674205)
XLA Ops:
  0.6 117.4 %shard_map.161 = (f32[4,256,512]{2,1,0:T(8,128)}, bf16[3,4,128,512]{3,2,1,0:T(8,128)(2,1)}, f32[16,128]{1,0:T(8,128)}) custom-call(s32[1,2]{1,0:T(1,128)} %flag_ref.3, bf16[4,256,512]{2,1,0:T(8,128)(2,1)} %bitcast.4, bf16[4,256,512]{2,1,0:T(8,128)(2,1)} %bitcast.5, bf16[1,512,1536]{2,1,0:T(8,128)(2,1)} %w_qkv_hbm.1, bf16[1,512,512]{2,1,0:T(8,128)(2,1)} %w_out_hbm.1, ...), custom_call_target="tpu_custom_call" | custom-call | tf_op jit(solution)/shard_map/pallas_call | solution.py:1203
  118.1 5.0 %shard_map.162 = (f32[1,1024,512]{2,1,0:T(8,128)}, f32[1,128,1536]{2,1,0:T(8,128)}, f32[1,128,512]{2,1,0:T(8,128)}, f32[1,128,2048]{2,1,0:T(8,128)}, f32[1,512,5...) custom-call(s32[1,2]{1,0:T(1,128)} %flag_ref.3, f32[1024,512]{1,0:T(8,128)} %bitcast.3, ...), custom_call_target="tpu_custom_call" | custom-call | tf_op jit(solution)/shard_map/pallas_call | solution.py:1287

commit v11 on v10

--- a/solution.py
+++ b/solution.py
@@ -168,21 +168,21 @@
     other_core = side * 2 + (1 - core)
     other_side = (1 - side) * 2 + core
 
-    loads = []
-    for block in range(3):
-        span = pl.ds(block * width, width)
-        loads.append((w_qkv_hbm.at[0, :, span], w_qkv.at[:, span]))
-    loads.append((w_out_hbm.at[0], w_out))
-    for block in range(4):
-        span = pl.ds(block * width, width)
-        loads.append((w_up_hbm.at[0, :, span], w_up.at[:, span]))
-    for block in range(4):
-        span = pl.ds(block * width, width)
-        loads.append((w_down_hbm.at[0, span, :], w_down.at[block]))
-    load_copies = [
-        pltpu.make_async_copy(source, target, load_sem.at[index + 1])
-        for index, (source, target) in enumerate(loads)
-    ]
+    def load_copy(block):
+        def span(first):
+            return pl.ds(pl.multiple_of((block - first) * width, width), width)
+
+        def copy_of(source, target):
+            return pltpu.make_async_copy(source, target, load_sem.at[1 + block])
+
+        return (
+            lambda: copy_of(w_qkv_hbm.at[0, :, span(0)], w_qkv.at[:, span(0)]),
+            lambda: copy_of(w_out_hbm.at[0], w_out),
+            lambda: copy_of(w_up_hbm.at[0, :, span(4)], w_up.at[:, span(4)]),
+            lambda: copy_of(w_down_hbm.at[0, span(8), :], w_down.at[block - 8]),
+        )
+
+    parts_of_load = ((0, 3), (3, 4), (4, 8), (8, 12))
     first_rows = pltpu.make_async_copy(x_hbm, rows_in, load_sem.at[0])
     last_rows = pltpu.make_async_copy(ct_hbm, rows_in, load_sem.at[0])
 
@@ -194,8 +194,9 @@
     def _():
         last_rows.start()
 
-    for copy in load_copies:
-        copy.start()
+    for part, (first, after) in enumerate(parts_of_load):
+        for block in range(first, after):
+            load_copy(block)[part]().start()
 
     barrier = pltpu.get_barrier_semaphore()
     pl.semaphore_signal(
@@ -223,17 +224,23 @@
 
     chunks = [slice(start, start + CHUNK) for start in range(0, width, CHUNK)]
 
-    for block, copy in enumerate(load_copies):
-        copy.wait()
-        span = slice(block % 4 * width, (block % 4 + 1) * width)
-        if block < 3:
-            turned[block] = w_qkv[:, span].T
-        elif block == 3:
-            turned[block] = w_out[...].T
-        elif block < 8:
-            turned[block] = w_up[:, span].T
-        else:
-            turned[block] = w_down[block - 8].T
+    def turn(part):
+        def one(block, carry):
+            load_copy(block)[part]().wait()
+            if part == 3:
+                turned[block] = w_down[block - 8].T
+            elif part == 1:
+                turned[block] = w_out[...].T
+            else:
+                first = parts_of_load[part][0]
+                span = pl.ds(pl.multiple_of((block - first) * width, width), width)
+                turned[block] = (w_qkv if part == 0 else w_up)[:, span].T
+            return carry
+
+        lax.fori_loop(*parts_of_load[part], one, 0)
+
+    for part in range(4):
+        turn(part)
     first_rows.wait()
 
     pl.semaphore_wait(barrier, 4 + dp_count - 1)
@@ -1021,13 +1028,9 @@
             backward_start(index)
             drain(backward_norm(index))
 
-        @pl.when(segment * step == 3)
-        def _():
-            backward_both(0, 2)
-
-        @pl.when(segment * step == 4)
-        def _():
-            backward_both(2, 3)
+        @pl.when(segment * lax.div(step, 3) * (5 - jnp.minimum(step, 5)) >= 1)
+        def _():
+            backward_both(2 * step - 6, step - 1)
 
         @pl.when(is_last == 1)
         def _():

time: 123 us -> 124 us (level)
  no operation moved by 1% of the time
where the time goes in v11:
time: 124 us
  Pallas kernels  123 us (99%)
    pallas_call x1, Pallas kernels, on_device(): pl.pallas_call(functools.partial(layer_kernel, dp_count), out_shape=(jax....  118 us
    pallas_call x1, Pallas kernels, on_device(): pl.pallas_call(finish_kernel, out_shape=(jax.ShapeDtypeStruct((1, rows, w...  5.01 us

profile of v11, /device:TPU:0, one launch (start us, length us, event | category | flops | bytes accessed | tf_op | source)
XLA Modules:
  0.0 123.9 jit_solution(11365278272201113577)
XLA Ops:
  0.6 118.1 %shard_map.161 = (f32[4,256,512]{2,1,0:T(8,128)}, bf16[3,4,128,512]{3,2,1,0:T(8,128)(2,1)}, f32[16,128]{1,0:T(8,128)}) custom-call(s32[1,2]{1,0:T(1,128)} %flag_ref.3, bf16[4,256,512]{2,1,0:T(8,128)(2,1)} %bitcast.4, bf16[4,256,512]{2,1,0:T(8,128)(2,1)} %bitcast.5, bf16[1,512,1536]{2,1,0:T(8,128)(2,1)} %w_qkv_hbm.1, bf16[1,512,512]{2,1,0:T(8,128)(2,1)} %w_out_hbm.1, ...), custom_call_target="tpu_custom_call" | custom-call | tf_op jit(solution)/shard_map/pallas_call | solution.py:1206
  118.7 5.0 %shard_map.162 = (f32[1,1024,512]{2,1,0:T(8,128)}, f32[1,128,1536]{2,1,0:T(8,128)}, f32[1,128,512]{2,1,0:T(8,128)}, f32[1,128,2048]{2,1,0:T(8,128)}, f32[1,512,5...) custom-call(s32[1,2]{1,0:T(1,128)} %flag_ref.3, f32[1024,512]{1,0:T(8,128)} %bitcast.3, ...), custom_call_target="tpu_custom_call" | custom-call | tf_op jit(solution)/shard_map/pallas_call | solution.py:1290

commit v12 on v11

--- a/solution.py
+++ b/solution.py
@@ -19,24 +19,25 @@
 STATS = 10
 CHUNK = 64
 SPLIT = 4
-DP_FIRST = (1, 3, 6, 10)
+DP_FIRST = (1, 5, 9)
 SUM, CORE, SIDE, SIDED, DP, DPED, JOIN, LAST, SMALL = range(9)
 ORDER_ONE = (
     (SUM, 0), (SUM, 2),
 )
 ORDER_TWO = (
-    (SUM, 4), (CORE, 1), (CORE, 0), (SIDE, 0), (SUM, 6), (CORE, 2), (SIDE, 2), (CORE, 3),
+    (CORE, 0), (SIDE, 0), (SUM, 4), (CORE, 3), (CORE, 2), (CORE, 1), (SIDE, 3), (SUM, 6), (SIDED, 0),
+    (SIDE, 2),
 )
 ORDER_THREE = (
-    (CORE, 5), (SUM, 8), (SIDE, 5), (CORE, 6), (DP, 3), (CORE, 4), (SUM, 10), (CORE, 7), (SIDE, 4),
-    (SIDED, 5), (SIDED, 2), (SIDE, 7), (DP, 1), (CORE, 8), (CORE, 11), (DPED, 3), (DP, 6), (SIDED, 0),
-    (DP, 2), (DPED, 1), (SIDED, 4), (SIDE, 11), (JOIN, 3), (SIDED, 7), (CORE, 10), (DP, 0), (DP, 5),
-    (CORE, 9), (SMALL, 0), (SIDE, 8), (DP, 4), (SIDE, 9), (SIDED, 11), (DP, 7), (JOIN, 1), (SIDED, 8),
-    (SMALL, 1), (LAST, 1), (DPED, 0), (DP, 10), (DPED, 5), (DPED, 2), (LAST, 3), (SIDED, 9), (DPED, 6),
-    (DP, 8), (JOIN, 0), (DPED, 4), (DPED, 10), (DP, 11), (JOIN, 4), (JOIN, 5), (DP, 9), (JOIN, 2), (LAST, 0),
-    (DPED, 8), (JOIN, 6), (DPED, 7), (DPED, 11), (DPED, 9), (LAST, 4), (JOIN, 10), (JOIN, 7), (JOIN, 11),
-    (JOIN, 8), (JOIN, 9), (SMALL, 2), (LAST, 5), (LAST, 8), (LAST, 2), (LAST, 9), (LAST, 10), (LAST, 11),
-    (LAST, 7), (LAST, 6),
+    (CORE, 4), (SIDED, 3), (CORE, 6), (SIDE, 6), (CORE, 5), (DP, 0), (SIDE, 4), (SUM, 8), (DPED, 0), (DP, 1),
+    (SIDED, 2), (CORE, 7), (SIDE, 7), (SUM, 10), (DP, 3), (SIDED, 6), (CORE, 8), (SIDE, 8), (SIDED, 4),
+    (DPED, 1), (DP, 2), (CORE, 9), (DP, 6), (DPED, 3), (CORE, 11), (SIDE, 11), (SIDED, 8), (DP, 4),
+    (CORE, 10), (SMALL, 0), (DP, 5), (DPED, 6), (JOIN, 1), (JOIN, 3), (SIDED, 7), (DP, 9), (SIDE, 10),
+    (SIDED, 11), (DP, 8), (DPED, 4), (DPED, 2), (SIDED, 10), (DP, 7), (DPED, 9), (DP, 11), (JOIN, 6),
+    (JOIN, 4), (DPED, 5), (DPED, 8), (DP, 10), (DPED, 7), (SMALL, 1), (LAST, 6), (LAST, 1), (JOIN, 2),
+    (DPED, 11), (LAST, 3), (JOIN, 0), (DPED, 10), (JOIN, 7), (JOIN, 8), (JOIN, 11), (JOIN, 9), (JOIN, 5),
+    (LAST, 4), (SMALL, 2), (LAST, 0), (JOIN, 10), (LAST, 9), (LAST, 11), (LAST, 5), (LAST, 7), (LAST, 8),
+    (LAST, 2), (LAST, 10),
 )
 
 
@@ -239,11 +240,22 @@
 
         lax.fori_loop(*parts_of_load[part], one, 0)
 
-    for part in range(4):
-        turn(part)
+    def turn_apart(first, after):
+        for block in range(first, after):
+            part = (0, 0, 0, 1, 2, 2, 2, 2, 3, 3, 3, 3)[block]
+            load_copy(block)[part]().wait()
+            span = slice(block % 4 * width, (block % 4 + 1) * width)
+            if part == 0:
+                turned[block] = w_qkv[:, span].T
+            elif part == 1:
+                turned[block] = w_out[...].T
+            elif part == 2:
+                turned[block] = w_up[:, span].T
+            else:
+                turned[block] = w_down[block - 8].T
+            yield 230
+
     first_rows.wait()
-
-    pl.semaphore_wait(barrier, 4 + dp_count - 1)
 
     flag = flag_ref[0, 0].astype(F32)
 
@@ -468,11 +480,9 @@
             yield 20
 
     def forward_end(index):
-        @pl.when(segment == 0)
-        def _():
-            for rows in chunks:
-                outgoing[index, rows, :] = output_rows(rows, lanes_of(index)).astype(BF16)
-            forward_copy(index).start()
+        for rows in chunks:
+            outgoing[index, rows, :] = output_rows(rows, lanes_of(index)).astype(BF16)
+        forward_copy(index).start()
 
     def off_or_not(index, run):
         @pl.when(index == 1)
@@ -488,7 +498,10 @@
         drain(forward_first(index))
         off_or_not(index, attend)
         drain(forward_rest(index, wide_a))
-        forward_end(index)
+
+        @pl.when(segment == 0)
+        def _():
+            forward_end(index)
 
     def output_rows(rows, lanes):
         return norm_two[rows, lanes] * column(GAIN_TWO, rows) + column(BIAS_TWO, rows)
@@ -1013,9 +1026,10 @@
         last_index = jnp.where(step < 2, step, jnp.where(step == 2, 1, 3))
         index = jnp.minimum(jnp.where(segment == 0, first_index, last_index), PIECES - 1)
         is_last = jnp.where(step == 2 * PIECES, 1, 0)
-        is_forward = jnp.where(step < jnp.where(segment == 0, 4, 2), 1, 0)
+        begun = jnp.where(step + segment == 0, 0, 1)
+        is_forward = jnp.where(step < jnp.where(segment == 0, 4, 2), begun, 0)
         last_backward = jnp.where(step == 2, 1, 0) + jnp.where(step == 5, 1, 0)
-        is_backward = jnp.where(segment == 0, (1 - is_forward) * (1 - is_last), last_backward)
+        is_backward = jnp.where(segment == 0, begun * (1 - is_forward) * (1 - is_last), last_backward)
         is_split = jnp.where(step >= 2 * PIECES - 1, 1 - segment, 0)
         is_rest = is_backward * (1 - is_split) + is_last * is_split
 
@@ -1052,8 +1066,27 @@
 
     @pl.when(segment == 1)
     def _():
+        for part in range(4):
+            turn(part)
         for index in range(PIECES):
             incoming_grad[index] = own_rows(index).astype(BF16)
+
+    @pl.when(segment == 0)
+    def _():
+        def ahead():
+            x_t[:, lanes_of(0)] = own_rows(0).astype(BF16)
+            yield from forward_first(0)
+            yield from attend(0, False)
+            yield from forward_rest(0, wide_a)
+
+        drain(turn_apart(0, 4))
+        side_by_side(ahead(), turn_apart(4, 12))
+
+    pl.semaphore_wait(barrier, 4 + dp_count - 1)
+
+    @pl.when(segment == 0)
+    def _():
+        forward_end(0)
 
     lax.fori_loop(0, 2 * PIECES + 1, one_step, 0)
 

time: 124 us -> 121 us (0.976)
  Pallas kernels: 123 us -> 120 us
    pallas_call x1, Pallas kernels: 118 us -> 115 us  [on_device(): pl.pallas_call(functools.partial(layer_kernel, dp_count), out_shape=(jax....]
where the time goes in v12:
time: 121 us
  Pallas kernels  120 us (99%)
    pallas_call x1, Pallas kernels, on_device(): pl.pallas_call(functools.partial(layer_kernel, dp_count), out_shape=(jax....  115 us
    pallas_call x1, Pallas kernels, on_device(): pl.pallas_call(finish_kernel, out_shape=(jax.ShapeDtypeStruct((1, rows, w...  5.01 us

profile of v12, /device:TPU:0, one launch (start us, length us, event | category | flops | bytes accessed | tf_op | source)
XLA Modules:
  0.0 121.1 jit_solution(2797430338332230756)
XLA Ops:
  0.6 115.3 %shard_map.161 = (f32[4,256,512]{2,1,0:T(8,128)}, bf16[3,4,128,512]{3,2,1,0:T(8,128)(2,1)}, f32[16,128]{1,0:T(8,128)}) custom-call(s32[1,2]{1,0:T(1,128)} %flag_ref.3, bf16[4,256,512]{2,1,0:T(8,128)(2,1)} %bitcast.4, bf16[4,256,512]{2,1,0:T(8,128)(2,1)} %bitcast.5, bf16[1,512,1536]{2,1,0:T(8,128)(2,1)} %w_qkv_hbm.1, bf16[1,512,512]{2,1,0:T(8,128)(2,1)} %w_out_hbm.1, ...), custom_call_target="tpu_custom_call" | custom-call | tf_op jit(solution)/shard_map/pallas_call | solution.py:1239
  115.9 5.0 %shard_map.162 = (f32[1,1024,512]{2,1,0:T(8,128)}, f32[1,128,1536]{2,1,0:T(8,128)}, f32[1,128,512]{2,1,0:T(8,128)}, f32[1,128,2048]{2,1,0:T(8,128)}, f32[1,512,5...) custom-call(s32[1,2]{1,0:T(1,128)} %flag_ref.3, f32[1024,512]{1,0:T(8,128)} %bitcast.3, ...), custom_call_target="tpu_custom_call" | custom-call | tf_op jit(solution)/shard_map/pallas_call | solution.py:1323

commit v13 on v12

--- a/solution.py
+++ b/solution.py
@@ -1042,9 +1042,13 @@
             backward_start(index)
             drain(backward_norm(index))
 
-        @pl.when(segment * lax.div(step, 3) * (5 - jnp.minimum(step, 5)) >= 1)
-        def _():
-            backward_both(2 * step - 6, step - 1)
+        @pl.when(segment * step == 3)
+        def _():
+            backward_both(0, 2)
+
+        @pl.when(segment * step == 4)
+        def _():
+            backward_both(2, 3)
 
         @pl.when(is_last == 1)
         def _():
@@ -1177,26 +1181,34 @@
         )
     ]
     small_load.start()
-    for copy in loads + ends_loads:
-        copy.start()
-    for load, copy in zip(ends_loads, ends_copies):
-        load.wait()
-        copy.start()
+    for group in range(3):
+        loads[group].start()
+        for copy in ends_loads[group * 3 : group * 3 + 3]:
+            copy.start()
+
+    def ends_on(first, after):
+        for load, copy in zip(ends_loads[first:after], ends_copies[first:after]):
+            load.wait()
+            copy.start()
+
     loads[0].wait()
     for position in range(4):
         rows = slice(position * share_rows, (position + 1) * share_rows)
         wide_down[rows, :] = fin_v[0, position].astype(F32)
     stores[0].start()
+    ends_on(0, 3)
     loads[1].wait()
     for position in range(4):
         wide_up[:, position * width : (position + 1) * width] = fin_v[1, position].astype(F32)
     stores[1].start()
+    ends_on(3, 6)
     loads[2].wait()
     for position in range(3):
         wide_qkv[:, position * width : (position + 1) * width] = fin_v[2, position].astype(F32)
     stores[2].start()
     wide_out[...] = fin_v[2, 3].astype(F32)
     stores[3].start()
+    ends_on(6, 8)
     small_load.wait()
     for position in range(4):
         rows = slice(position * share_rows, (position + 1) * share_rows)

time: 121 us -> 120 us (level)
  no operation moved by 1% of the time
where the time goes in v13:
time: 120 us
  Pallas kernels  119 us (99%)
    pallas_call x1, Pallas kernels, on_device(): pl.pallas_call(functools.partial(layer_kernel, dp_count), out_shape=(jax....  114 us
    pallas_call x1, Pallas kernels, on_device(): pl.pallas_call(finish_kernel, out_shape=(jax.ShapeDtypeStruct((1, rows, w...  4.76 us

profile of v13, /device:TPU:0, one launch (start us, length us, event | category | flops | bytes accessed | tf_op | source)
XLA Modules:
  0.0 119.9 jit_solution(1561399989292566231)
XLA Ops:
  0.6 114.3 %shard_map.161 = (f32[4,256,512]{2,1,0:T(8,128)}, bf16[3,4,128,512]{3,2,1,0:T(8,128)(2,1)}, f32[16,128]{1,0:T(8,128)}) custom-call(s32[1,2]{1,0:T(1,128)} %flag_ref.3, bf16[4,256,512]{2,1,0:T(8,128)(2,1)} %bitcast.4, bf16[4,256,512]{2,1,0:T(8,128)(2,1)} %bitcast.5, bf16[1,512,1536]{2,1,0:T(8,128)(2,1)} %w_qkv_hbm.1, bf16[1,512,512]{2,1,0:T(8,128)(2,1)} %w_out_hbm.1, ...), custom_call_target="tpu_custom_call" | custom-call | tf_op jit(solution)/shard_map/pallas_call | solution.py:1251
  114.9 4.8 %shard_map.162 = (f32[1,1024,512]{2,1,0:T(8,128)}, f32[1,128,1536]{2,1,0:T(8,128)}, f32[1,128,512]{2,1,0:T(8,128)}, f32[1,128,2048]{2,1,0:T(8,128)}, f32[1,512,5...) custom-call(s32[1,2]{1,0:T(1,128)} %flag_ref.3, f32[1024,512]{1,0:T(8,128)} %bitcast.3, ...), custom_call_target="tpu_custom_call" | custom-call | tf_op jit(solution)/shard_map/pallas_call | solution.py:1335

commit v14 on v13

--- a/solution.py
+++ b/solution.py
@@ -59,8 +59,8 @@
         pass
 
 
-def side_by_side(one, two):
-    spent = [0, 300]
+def side_by_side(one, two, behind):
+    spent = [0, behind]
     live = [one, two]
     while live[0] or live[1]:
         which = 0 if live[0] and (not live[1] or spent[0] <= spent[1]) else 1
@@ -669,7 +669,7 @@
             yield from attend(forward_index, False)
             yield from forward_rest(forward_index, wide_c)
 
-        side_by_side(back(), ahead())
+        side_by_side(back(), ahead(), 300)
         backward_copy(index).start()
 
     split = SPLIT if share_rows % (16 * SPLIT) == 0 else 1
@@ -832,25 +832,38 @@
                 start = (index * pack + each) * cut_rows
                 turned[block, target : target + cut_rows, :] = result[start : start + cut_rows]
 
+    def down_block(part, block, tokens, add):
+        count = width // (4 * share_rows)
+        pieces = []
+        for each in range(4 * count):
+            start = pl.multiple_of(each * share_rows + part * (pack * cut_rows), pack * cut_rows)
+            pieces.append(active[block, pl.ds(start, pack * cut_rows), tokens])
+        result = dot_turned(jnp.concatenate(pieces, axis=0), down_grad[:, tokens])
+        high = lax.rem(block, 2) * 2 + lax.div(block, 2)
+        for each in range(count):
+            place = turned_bits(each, count) * 4 + high
+            for position in range(4):
+                for job in range(pack):
+                    target = (part * pack + job) * job_rows + place * cut_rows
+                    rows = pl.ds(pl.multiple_of(target, cut_rows), cut_rows)
+                    start = ((each * 4 + position) * pack + job) * cut_rows
+                    total = result[start : start + cut_rows]
+                    if add:
+                        total = total + turned[8 + position, rows, :].astype(F32)
+                    turned[8 + position, rows, :] = total.astype(BF16)
+
+    half_tokens = PIECES // 2 * piece
+
+    def early_down_sums():
+        def one(step, carry):
+            down_block(lax.div(step, 4), lax.rem(step, 4), slice(0, half_tokens), False)
+            return carry
+
+        lax.fori_loop(0, 4 * (split // pack), one, 0)
+
     def down_sums(part):
-        count = width // (4 * share_rows)
-
         def one(block, carry):
-            pieces = []
-            for each in range(4 * count):
-                start = each * share_rows + part * pack * cut_rows
-                pieces.append(active[block, start : start + pack * cut_rows, :])
-            result = dot_turned(jnp.concatenate(pieces, axis=0), down_grad[...]).astype(BF16)
-            high = lax.rem(block, 2) * 2 + lax.div(block, 2)
-            for each in range(count):
-                place = turned_bits(each, count) * 4 + high
-                for position in range(4):
-                    for job in range(pack):
-                        target = (part * pack + job) * job_rows + place * cut_rows
-                        start = ((each * 4 + position) * pack + job) * cut_rows
-                        turned[
-                            8 + position, pl.ds(pl.multiple_of(target, cut_rows), cut_rows), :
-                        ] = result[start : start + cut_rows]
+            down_block(part, block, slice(half_tokens, 2 * half_tokens), True)
             return carry
 
         lax.fori_loop(0, 4, one, 0)
@@ -1066,14 +1079,22 @@
         def _():
             backward_attention(index)
 
+        @pl.when(step - segment == 5)
+        def _():
+            early_down_sums()
+
         return carry
 
     @pl.when(segment == 1)
     def _():
         for part in range(4):
             turn(part)
-        for index in range(PIECES):
+
+        def one_cotangent(index, carry):
             incoming_grad[index] = own_rows(index).astype(BF16)
+            return carry
+
+        lax.fori_loop(0, PIECES, one_cotangent, 0)
 
     @pl.when(segment == 0)
     def _():
@@ -1083,8 +1104,8 @@
             yield from attend(0, False)
             yield from forward_rest(0, wide_a)
 
-        drain(turn_apart(0, 4))
-        side_by_side(ahead(), turn_apart(4, 12))
+        drain(turn_apart(0, 1))
+        side_by_side(ahead(), turn_apart(1, 12), -400)
 
     pl.semaphore_wait(barrier, 4 + dp_count - 1)
 

time: 120 us -> 119 us (level)
  no operation moved by 1% of the time
where the time goes in v14:
time: 119 us
  Pallas kernels  118 us (99%)
    pallas_call x1, Pallas kernels, on_device(): pl.pallas_call(functools.partial(layer_kernel, dp_count), out_shape=(jax....  113 us
    pallas_call x1, Pallas kernels, on_device(): pl.pallas_call(finish_kernel, out_shape=(jax.ShapeDtypeStruct((1, rows, w...  4.76 us

profile of v14, /device:TPU:0, one launch (start us, length us, event | category | flops | bytes accessed | tf_op | source)
XLA Modules:
  0.0 118.9 jit_solution(2308552254562807135)
XLA Ops:
  0.6 113.3 %shard_map.161 = (f32[4,256,512]{2,1,0:T(8,128)}, bf16[3,4,128,512]{3,2,1,0:T(8,128)(2,1)}, f32[16,128]{1,0:T(8,128)}) custom-call(s32[1,2]{1,0:T(1,128)} %flag_ref.3, bf16[4,256,512]{2,1,0:T(8,128)(2,1)} %bitcast.4, bf16[4,256,512]{2,1,0:T(8,128)(2,1)} %bitcast.5, bf16[1,512,1536]{2,1,0:T(8,128)(2,1)} %w_qkv_hbm.1, bf16[1,512,512]{2,1,0:T(8,128)(2,1)} %w_out_hbm.1, ...), custom_call_target="tpu_custom_call" | custom-call | tf_op jit(solution)/shard_map/pallas_call | solution.py:1272
  114.0 4.8 %shard_map.162 = (f32[1,1024,512]{2,1,0:T(8,128)}, f32[1,128,1536]{2,1,0:T(8,128)}, f32[1,128,512]{2,1,0:T(8,128)}, f32[1,128,2048]{2,1,0:T(8,128)}, f32[1,512,5...) custom-call(s32[1,2]{1,0:T(1,128)} %flag_ref.3, f32[1024,512]{1,0:T(8,128)} %bitcast.3, ...), custom_call_target="tpu_custom_call" | custom-call | tf_op jit(solution)/shard_map/pallas_call | solution.py:1356

commit v15 on v14

--- a/solution.py
+++ b/solution.py
@@ -22,10 +22,10 @@
 DP_FIRST = (1, 5, 9)
 SUM, CORE, SIDE, SIDED, DP, DPED, JOIN, LAST, SMALL = range(9)
 ORDER_ONE = (
-    (SUM, 0), (SUM, 2),
+    (SUM, 0), (SUM, 2), (CORE, 0), (SIDE, 0),
 )
 ORDER_TWO = (
-    (CORE, 0), (SIDE, 0), (SUM, 4), (CORE, 3), (CORE, 2), (CORE, 1), (SIDE, 3), (SUM, 6), (SIDED, 0),
+    (SUM, 4), (CORE, 3), (CORE, 2), (CORE, 1), (SIDE, 3), (SUM, 6), (SIDED, 0),
     (SIDE, 2),
 )
 ORDER_THREE = (

time: 119 us -> 120 us (level)
  no operation moved by 1% of the time
where the time goes in v15:
time: 120 us
  Pallas kernels  119 us (99%)
    pallas_call x1, Pallas kernels, on_device(): pl.pallas_call(functools.partial(layer_kernel, dp_count), out_shape=(jax....  114 us
    pallas_call x1, Pallas kernels, on_device(): pl.pallas_call(finish_kernel, out_shape=(jax.ShapeDtypeStruct((1, rows, w...  4.76 us

profile of v15, /device:TPU:0, one launch (start us, length us, event | category | flops | bytes accessed | tf_op | source)
XLA Modules:
  0.0 119.9 jit_solution(13826374735939794563)
XLA Ops:
  0.6 114.3 %shard_map.161 = (f32[4,256,512]{2,1,0:T(8,128)}, bf16[3,4,128,512]{3,2,1,0:T(8,128)(2,1)}, f32[16,128]{1,0:T(8,128)}) custom-call(s32[1,2]{1,0:T(1,128)} %flag_ref.3, bf16[4,256,512]{2,1,0:T(8,128)(2,1)} %bitcast.4, bf16[4,256,512]{2,1,0:T(8,128)(2,1)} %bitcast.5, bf16[1,512,1536]{2,1,0:T(8,128)(2,1)} %w_qkv_hbm.1, bf16[1,512,512]{2,1,0:T(8,128)(2,1)} %w_out_hbm.1, ...), custom_call_target="tpu_custom_call" | custom-call | tf_op jit(solution)/shard_map/pallas_call | solution.py:1272
  114.9 4.8 %shard_map.162 = (f32[1,1024,512]{2,1,0:T(8,128)}, f32[1,128,1536]{2,1,0:T(8,128)}, f32[1,128,512]{2,1,0:T(8,128)}, f32[1,128,2048]{2,1,0:T(8,128)}, f32[1,512,5...) custom-call(s32[1,2]{1,0:T(1,128)} %flag_ref.3, f32[1024,512]{1,0:T(8,128)} %bitcast.3, ...), custom_call_target="tpu_custom_call" | custom-call | tf_op jit(solution)/shard_map/pallas_call | solution.py:1356
